TPU v7x, 32 devices: a whole 2x2x4 slice. The times are simulated.
32 devices in a mesh: seq: 8 (over z, y), head: 4 (over x, core).
Axes of the slice: x: 2, y: 2, z: 4, core: 2. Of those that a mesh axis runs over, the one named last changes fastest.
Arguments:
- inputs: bfloat16 [8192, 768], P('seq'), may hold values from -4.5 to 4.5
- cotangent: bfloat16 [8192, 768], P('seq'), may hold values from -6 to 6
- item_lengths: int32 [3], replicated, may hold values from 64 to 7168, as said below
- w_query: bfloat16 [768, 768], P('seq', 'head'), may hold values from -0.21875 to 0.21875
- w_key: bfloat16 [768, 768], P('seq', 'head'), may hold values from -0.21875 to 0.21875
- w_value: bfloat16 [768, 768], P('seq', 'head'), may hold values from -0.21875 to 0.21875
- w_out: bfloat16 [768, 768], P('seq', 'head'), may hold values from -0.21875 to 0.21875
- w_up: bfloat16 [768, 3072], P('seq', 'head'), may hold values from -0.21875 to 0.21875
- w_down: bfloat16 [768, 3072], P('seq', 'head'), may hold values from -0.109375 to 0.109375
- bias_query: float32 [768], P('head'), may hold values from -3 to 3
- bias_value: float32 [768], P('head'), may hold values from -3 to 3
- bias_out: float32 [768], replicated, may hold values from -3 to 3
- bias_up: float32 [3072], P('head'), may hold values from -3 to 3
- bias_down: float32 [768], replicated, may hold values from -3 to 3
- gain_one: float32 [768], replicated, may hold values from 0.1 to 1.9
- bias_one: float32 [768], replicated, may hold values from -3 to 3
- gain_two: float32 [768], replicated, may hold values from 0.1 to 1.9
- bias_two: float32 [768], replicated, may hold values from -3 to 3
- conv_taps: float32 [12, 33], P('head'), may hold values from -2 to 2
Outputs:
- output: bfloat16 [8192, 768], P('seq')
- grad_inputs: bfloat16 [8192, 768], P('seq')
- grad_w_query: float32 [768, 768], P('seq', 'head')
- grad_w_key: float32 [768, 768], P('seq', 'head')
- grad_w_value: float32 [768, 768], P('seq', 'head')
- grad_w_out: float32 [768, 768], P('seq', 'head')
- grad_w_up: float32 [768, 3072], P('seq', 'head')
- grad_w_down: float32 [768, 3072], P('seq', 'head')
- grad_bias_query: float32 [768], P('head')
- grad_bias_value: float32 [768], P('head')
- grad_bias_out: float32 [768], replicated
- grad_bias_up: float32 [3072], P('head')
- grad_bias_down: float32 [768], replicated
- grad_gain_one: float32 [768], replicated
- grad_bias_one: float32 [768], replicated
- grad_gain_two: float32 [768], replicated
- grad_bias_two: float32 [768], replicated
- grad_conv_taps: float32 [12, 33], P('head')
Inputs may be any that keep to these rules, and one draw needn't show every extreme that they name: `item_lengths`: every length is a multiple of 64; the first and the last item are 64 and 960 tokens long, in either order, and the middle item holds the rest.
All inputs are finite; a program needn't handle non-finite values.
Results may differ from a plain program's by a relative error of at most 0.038.
Values may be sent and summed in bfloat16 or wider, within the bound.
A program may use at most 128 MiB of HBM per device.

v0:
```python
import jax
import jax.numpy as jnp
from jax import lax
from jax.sharding import PartitionSpec as P

HEAD_DIM = 64
LAND = 64
KERNEL = 33
PINV_STEPS = 6
ITEMS = 3


PRECISE = lax.Precision.HIGHEST
EPSILON = 1e-05
MASKED = -1e30


def extended(cells, sides, width):
    for axis, dim in sides:
        count = lax.axis_size(axis)
        ends = count - 1
        head = lax.slice_in_dim(cells, 0, width, axis=dim)
        tail = lax.slice_in_dim(cells, cells.shape[dim] - width, cells.shape[dim], axis=dim)
        cells = jnp.concatenate(
            [
                lax.ppermute(tail, axis, [(i, (i + 1) % count) for i in range(ends)]),
                cells,
                lax.ppermute(head, axis, [((i + 1) % count, i) for i in range(ends)]),
            ],
            axis=dim,
        )
    return cells


def cut_along(array, dim, length):
    lengths = array.shape
    parts = array.reshape(*lengths[:dim], length, lengths[dim] // length, *lengths[dim + 1 :])
    return jnp.moveaxis(parts, dim, 0)


def sent_and_summed(array, axis, dim):
    parts = cut_along(array, dim, lax.axis_size(axis))
    arrived = lax.all_to_all(parts, axis, split_axis=0, concat_axis=0, tiled=True)
    return arrived.astype(jnp.float32).sum(axis=0)


def side_by_side(arrays, axis, dim, along):
    both = jnp.concatenate(arrays, axis=along)
    out, at, outs = (sent_and_summed(both, axis, dim), 0, [])
    for a in arrays:
        outs.append(lax.slice_in_dim(out, at, at + a.shape[along], axis=along))
        at += a.shape[along]
    return tuple(outs)


def locate(item_lengths, positions):
    item_ends = jnp.cumsum(item_lengths)
    item_starts = item_ends - item_lengths
    located = jnp.sum((positions[:, None] >= item_ends[None, :]).astype(jnp.int32), axis=1)
    inside = (positions >= 0) & (located < ITEMS)
    picked = jnp.minimum(located, ITEMS - 1)
    onehot = (picked[:, None] == jnp.arange(ITEMS, dtype=jnp.int32)[None, :]).astype(jnp.int32)
    item_start = jnp.sum(onehot * item_starts[None, :], axis=1)
    length = jnp.sum(onehot * item_lengths[None, :], axis=1)
    segment = (positions - item_start) * LAND // length
    land_slot = picked * LAND + jnp.clip(segment, 0, LAND - 1)
    return (jnp.where(inside, picked, -1), land_slot)


def normalize(values):
    row_mean = jnp.mean(values, axis=-1, keepdims=True)
    centered = values - row_mean
    variance = jnp.mean(centered * centered, axis=-1, keepdims=True)
    inv_std = lax.rsqrt(variance + EPSILON)
    return (centered * inv_std, inv_std)


def norm_back(grad_norm, normed, inv_std):
    return inv_std * (
        grad_norm
        - jnp.mean(grad_norm, axis=-1, keepdims=True)
        - normed * jnp.mean(grad_norm * normed, axis=-1, keepdims=True)
    )


def pseudo_inverse(land_kernel):
    identity = jnp.eye(LAND, dtype=jnp.float32)
    frobenius = jnp.sum(land_kernel * land_kernel, axis=(-2, -1), keepdims=True)
    result = jnp.swapaxes(land_kernel, -1, -2) / frobenius
    for iteration in range(PINV_STEPS):
        product = jnp.matmul(land_kernel, result, precision=PRECISE)
        nested = 7.0 * identity - product
        nested = 15.0 * identity - jnp.matmul(product, nested, precision=PRECISE)
        nested = 13.0 * identity - jnp.matmul(product, nested, precision=PRECISE)
        result = 0.25 * jnp.matmul(result, nested, precision=PRECISE)
    return result


def gelu_tanh(values):
    return jax.nn.gelu(values, approximate=True)


def matmul_low(left, right):
    return jnp.dot(left, right, preferred_element_type=jnp.float32)


def against(left, right):
    return lax.dot_general(
        left, right, (((1,), (1,)), ((), ())), preferred_element_type=jnp.float32
    )


def across(left, right):
    return lax.dot_general(
        left, right, (((0,), (0,)), ((), ())), preferred_element_type=jnp.float32
    )


def body(
    inputs,
    cotangent,
    item_lengths,
    w_query,
    w_key,
    w_value,
    w_out,
    w_up,
    w_down,
    bias_query,
    bias_value,
    bias_out,
    bias_up,
    bias_down,
    gain_one,
    bias_one,
    gain_two,
    bias_two,
    conv_taps,
):
    low_type = jnp.bfloat16
    tok_rows = inputs.shape[0]
    heads_here = conv_taps.shape[0]
    width_here = heads_here * HEAD_DIM
    slots = ITEMS * LAND
    reach = (KERNEL - 1) // 2
    score_scale = HEAD_DIM ** (-0.5)
    pref = jnp.float32
    first_row = lax.axis_index("seq") * tok_rows
    positions = first_row + jnp.arange(tok_rows, dtype=jnp.int32)
    item_id, land_slot = locate(item_lengths, positions)
    rim_item = locate(
        item_lengths, first_row - reach + jnp.arange(tok_rows + 2 * reach, dtype=jnp.int32)
    )[0]
    slot_item = jnp.arange(slots, dtype=jnp.int32) // LAND
    member = land_slot[:, None] == jnp.arange(slots, dtype=jnp.int32)[None, :]
    member_low = member.astype(low_type)
    counts = jnp.repeat((item_lengths // LAND).astype(jnp.float32), LAND)
    same_f = item_id[:, None] == slot_item[None, :]
    same_b = same_f.T
    tap_cols = jnp.repeat(conv_taps, HEAD_DIM, axis=0)
    full_query, full_key, full_value, full_out, full_up, full_down = (
        lax.all_gather(w_query, "seq", axis=0, tiled=True),
        lax.all_gather(w_key, "seq", axis=0, tiled=True),
        lax.all_gather(w_value, "seq", axis=0, tiled=True),
        lax.all_gather(w_out, "seq", axis=0, tiled=True),
        lax.all_gather(w_up, "seq", axis=0, tiled=True),
        lax.all_gather(w_down, "seq", axis=0, tiled=True),
    )
    queries = (matmul_low(inputs, full_query) + bias_query).astype(low_type)
    key_rows = matmul_low(inputs, full_key).astype(low_type)
    value_rows = (matmul_low(inputs, full_value) + bias_value).astype(low_type)
    query_sums, key_sums = lax.psum(
        (across(member_low, queries), across(member_low, key_rows)), "seq"
    )
    query_land = (
        (query_sums / counts[:, None]).astype(low_type).reshape(slots, heads_here, HEAD_DIM)
    )
    key_land = (key_sums / counts[:, None]).astype(low_type).reshape(slots, heads_here, HEAD_DIM)
    query_heads = queries.reshape(tok_rows, heads_here, HEAD_DIM)
    key_heads = key_rows.reshape(tok_rows, heads_here, HEAD_DIM)
    value_heads = value_rows.reshape(tok_rows, heads_here, HEAD_DIM)
    scores_b = (
        jnp.einsum("lhd,thd->hlt", query_land, key_heads, preferred_element_type=pref) * score_scale
    )
    scores_b = jnp.where(same_b[None], scores_b, MASKED)
    maxima_b = lax.pmax(jnp.max(scores_b, axis=2), "seq")
    weights_b = jnp.exp(scores_b - maxima_b[:, :, None])
    weights_b_low = weights_b.astype(low_type)
    numer_sum, totals_b = lax.psum(
        (
            jnp.einsum("hlt,thd->lhd", weights_b_low, value_heads, preferred_element_type=pref),
            jnp.sum(weights_b, axis=2),
        ),
        "seq",
    )
    totals_cols = totals_b.T[:, :, None]
    kernel_v = numer_sum / totals_cols
    land_q = query_land.reshape(ITEMS, LAND, heads_here, HEAD_DIM)
    land_k = key_land.reshape(ITEMS, LAND, heads_here, HEAD_DIM)
    land_kernel = jax.nn.softmax(
        jnp.einsum("ilhd,imhd->ihlm", land_q, land_k, preferred_element_type=pref) * score_scale,
        axis=-1,
    )
    inverse, inverse_back = jax.vjp(pseudo_inverse, land_kernel)
    kernel_items = kernel_v.reshape(ITEMS, LAND, heads_here, HEAD_DIM)
    mixing = jnp.einsum("ihlm,imhd->ilhd", inverse, kernel_items, precision=PRECISE)
    mixing = mixing.astype(low_type).reshape(slots, heads_here, HEAD_DIM)
    scores_f = (
        jnp.einsum("thd,lhd->htl", query_heads, key_land, preferred_element_type=pref) * score_scale
    )
    weights_f = jax.nn.softmax(jnp.where(same_f[None], scores_f, MASKED), axis=-1)
    weights_f_low = weights_f.astype(low_type)
    attended = jnp.einsum("htl,lhd->thd", weights_f_low, mixing, preferred_element_type=pref)
    attended = attended.reshape(tok_rows, width_here)
    value_rim = extended(value_rows, (("seq", 0),), reach)
    conv_sum = jnp.zeros((tok_rows, width_here), jnp.float32)
    for offset in range(KERNEL):
        in_item = (rim_item[offset : offset + tok_rows] == item_id)[:, None]
        conv_sum = conv_sum + jnp.where(
            in_item,
            value_rim[offset : offset + tok_rows].astype(jnp.float32)
            * tap_cols[:, offset][None, :],
            0.0,
        )
    mixed_rows = (attended + conv_sum).astype(low_type)
    attention_sum = lax.psum(against(mixed_rows, full_out).astype(jnp.bfloat16), "head").astype(
        jnp.float32
    )
    pre_one = inputs.astype(jnp.float32) + attention_sum + bias_out
    norm_one, inv_one = normalize(pre_one)
    hidden = norm_one * gain_one + bias_one
    hidden_low = hidden.astype(low_type)
    lifted = matmul_low(hidden_low, full_up) + bias_up
    active, gelu_back = jax.vjp(gelu_tanh, lifted)
    active_low = active.astype(low_type)
    feed_terms = against(active_low, full_down)
    feed_sum = lax.psum(feed_terms.astype(jnp.bfloat16), "head").astype(jnp.float32)
    grad_output = cotangent.astype(jnp.float32)
    pre_two = hidden + feed_sum + bias_down
    norm_two, inv_two = normalize(pre_two)
    out_rows = (norm_two * gain_two + bias_two).astype(low_type)
    grad_gain_two = jnp.sum(grad_output * norm_two, axis=0)
    grad_bias_two = jnp.sum(grad_output, axis=0)
    grad_two = norm_back(grad_output * gain_two, norm_two, inv_two)
    grad_bias_down = jnp.sum(grad_two, axis=0)
    grad_two_low = grad_two.astype(low_type)
    output, grad_two_full = (out_rows, grad_two_low)
    grad_down = across(grad_two_full, active_low)
    (grad_lift,) = gelu_back(matmul_low(grad_two_full, full_down))
    grad_bias_up = jnp.sum(grad_lift, axis=0)
    grad_lift_low = grad_lift.astype(low_type)
    grad_up = across(hidden_low, grad_lift_low)
    up_terms = against(grad_lift_low, full_up)
    grad_hidden = grad_two + lax.psum(up_terms.astype(jnp.bfloat16), "head").astype(jnp.float32)
    grad_gain_one = jnp.sum(grad_hidden * norm_one, axis=0)
    grad_bias_one = jnp.sum(grad_hidden, axis=0)
    grad_one = norm_back(grad_hidden * gain_one, norm_one, inv_one)
    grad_bias_out = jnp.sum(grad_one, axis=0)
    grad_one_low = grad_one.astype(low_type)
    grad_outw = across(grad_one_low, mixed_rows)
    grad_mixed = matmul_low(grad_one_low, full_out).astype(low_type)
    grad_mixed_wide = grad_mixed.astype(jnp.float32)
    grad_heads = grad_mixed.reshape(tok_rows, heads_here, HEAD_DIM)
    grad_rim = extended(grad_mixed, (("seq", 0),), reach)
    grad_conv_v = jnp.zeros((tok_rows, width_here), jnp.float32)
    tap_terms = []
    for offset in range(KERNEL):
        in_item = (rim_item[offset : offset + tok_rows] == item_id)[:, None]
        neighbour = jnp.where(
            in_item, value_rim[offset : offset + tok_rows].astype(jnp.float32), 0.0
        )
        tap_terms.append(
            jnp.sum(
                (grad_mixed_wide * neighbour).reshape(tok_rows, heads_here, HEAD_DIM), axis=(0, 2)
            )
        )
        mirror = 2 * reach - offset
        mirror_item = (rim_item[mirror : mirror + tok_rows] == item_id)[:, None]
        grad_conv_v = grad_conv_v + jnp.where(
            mirror_item,
            grad_rim[mirror : mirror + tok_rows].astype(jnp.float32) * tap_cols[:, offset][None, :],
            0.0,
        )
    grad_taps = jnp.stack(tap_terms, axis=1)
    grad_weights_f = jnp.einsum("thd,lhd->htl", grad_heads, mixing, preferred_element_type=pref)
    grad_mix_part = jnp.einsum(
        "htl,thd->lhd", weights_f_low, grad_heads, preferred_element_type=pref
    )
    grad_scores_f = weights_f * (
        grad_weights_f - jnp.sum(weights_f * grad_weights_f, axis=2, keepdims=True)
    )
    grad_scores_f = grad_scores_f.astype(low_type)
    grad_query_f = (
        jnp.einsum("htl,lhd->thd", grad_scores_f, key_land, preferred_element_type=pref)
        * score_scale
    )
    grad_kland_part = (
        jnp.einsum("htl,thd->lhd", grad_scores_f, query_heads, preferred_element_type=pref)
        * score_scale
    )
    grad_mixing, grad_kland_f = lax.psum((grad_mix_part, grad_kland_part), "seq")
    grad_mix_items = grad_mixing.reshape(ITEMS, LAND, heads_here, HEAD_DIM)
    grad_inverse = jnp.einsum("ilhd,imhd->ihlm", grad_mix_items, kernel_items, precision=PRECISE)
    grad_kernel_v = jnp.einsum("ihlm,ilhd->imhd", inverse, grad_mix_items, precision=PRECISE)
    grad_kernel_v = grad_kernel_v.reshape(slots, heads_here, HEAD_DIM)
    (grad_land_kernel,) = inverse_back(grad_inverse)
    grad_scores_a = land_kernel * (
        grad_land_kernel - jnp.sum(land_kernel * grad_land_kernel, axis=-1, keepdims=True)
    )
    grad_scores_a = grad_scores_a * score_scale
    grad_qland_a = jnp.einsum(
        "ihlm,imhd->ilhd", grad_scores_a, land_k.astype(jnp.float32), precision=PRECISE
    )
    grad_kland_a = jnp.einsum(
        "ihlm,ilhd->imhd", grad_scores_a, land_q.astype(jnp.float32), precision=PRECISE
    )
    grad_numer = (grad_kernel_v / totals_cols).astype(low_type)
    grad_totals = -jnp.sum(grad_kernel_v * kernel_v, axis=2) / totals_b.T
    grad_weights_b = jnp.einsum(
        "lhd,thd->hlt", grad_numer, value_heads, preferred_element_type=pref
    )
    grad_weights_b = grad_weights_b + grad_totals.T[:, :, None]
    grad_scores_b = (weights_b * grad_weights_b).astype(low_type)
    grad_qland_part = (
        jnp.einsum("hlt,thd->lhd", grad_scores_b, key_heads, preferred_element_type=pref)
        * score_scale
    )
    grad_key_b = (
        jnp.einsum("hlt,lhd->thd", grad_scores_b, query_land, preferred_element_type=pref)
        * score_scale
    )
    grad_value_b = jnp.einsum(
        "hlt,lhd->thd", weights_b_low, grad_numer, preferred_element_type=pref
    )
    grad_query_rows = grad_query_f.reshape(tok_rows, width_here)
    grad_values = grad_value_b.reshape(tok_rows, width_here) + grad_conv_v
    (
        grad_qland_b,
        grad_gain_one,
        grad_bias_one,
        grad_gain_two,
        grad_bias_two,
        grad_bias_out,
        grad_bias_down,
        grad_bias_up,
        grad_taps,
        query_f_total,
        grad_bias_value,
    ) = lax.psum(
        (
            grad_qland_part,
            grad_gain_one,
            grad_bias_one,
            grad_gain_two,
            grad_bias_two,
            grad_bias_out,
            grad_bias_down,
            grad_bias_up,
            grad_taps,
            jnp.sum(grad_query_rows, axis=0),
            jnp.sum(grad_values, axis=0),
        ),
        "seq",
    )
    grad_qland = grad_qland_a.reshape(slots, width_here) + grad_qland_b.reshape(slots, width_here)
    grad_kland = grad_kland_a.reshape(slots, width_here) + grad_kland_f.reshape(slots, width_here)
    member_wide = member.astype(jnp.float32)
    grad_queries = grad_query_rows + jnp.dot(
        member_wide, grad_qland / counts[:, None], precision=PRECISE
    )
    grad_keys = grad_key_b.reshape(tok_rows, width_here) + jnp.dot(
        member_wide, grad_kland / counts[:, None], precision=PRECISE
    )
    grad_bias_query = query_f_total + jnp.sum(grad_qland, axis=0)
    queries_low = grad_queries.astype(low_type)
    keys_low = grad_keys.astype(low_type)
    values_low = grad_values.astype(low_type)
    grad_queryw = across(inputs, queries_low)
    grad_keyw = across(inputs, keys_low)
    grad_valuew = across(inputs, values_low)
    input_terms = (
        against(queries_low, full_query)
        + against(keys_low, full_key)
        + against(values_low, full_value)
    )
    grad_inputs = (
        grad_one + lax.psum(input_terms.astype(jnp.bfloat16), "head").astype(jnp.float32)
    ).astype(low_type)
    query_shard, key_shard, value_shard, out_shard, grad_up_shard, grad_down_shard = side_by_side(
        (
            grad_queryw.astype(jnp.bfloat16),
            grad_keyw.astype(jnp.bfloat16),
            grad_valuew.astype(jnp.bfloat16),
            grad_outw.astype(jnp.bfloat16),
            grad_up.astype(jnp.bfloat16),
            grad_down.astype(jnp.bfloat16),
        ),
        "seq",
        0,
        1,
    )
    return (
        output,
        grad_inputs,
        query_shard,
        key_shard,
        value_shard,
        out_shard,
        grad_up_shard,
        grad_down_shard,
        grad_bias_query,
        grad_bias_value,
        grad_bias_out,
        grad_bias_up,
        grad_bias_down,
        grad_gain_one,
        grad_bias_one,
        grad_gain_two,
        grad_bias_two,
        grad_taps,
    )


def solution(mesh):
    return jax.shard_map(
        body,
        mesh=mesh,
        in_specs=(
            P("seq", None),
            P("seq", None),
            P(),
            P("seq", "head"),
            P("seq", "head"),
            P("seq", "head"),
            P("seq", "head"),
            P("seq", "head"),
            P("seq", "head"),
            P("head"),
            P("head"),
            P(),
            P("head"),
            P(),
            P(),
            P(),
            P(),
            P(),
            P("head", None),
        ),
        out_specs=(
            P("seq", None),
            P("seq", None),
            P("seq", "head"),
            P("seq", "head"),
            P("seq", "head"),
            P("seq", "head"),
            P("seq", "head"),
            P("seq", "head"),
            P("head"),
            P("head"),
            P(),
            P("head"),
            P(),
            P(),
            P(),
            P(),
            P(),
            P("head", None),
        ),
        check_vma=False,
    )
```

profile of v0, /device:TPU:0, one launch (start us, length us, event | category | flops | bytes accessed | tf_op | source)
XLA Modules:
  0.0 902.3 jit_solution(12035967452716710101)
XLA Ops:
  9.0 33.0 %all_gather.19 = bf16[768,192]{1,0:T(8,128)(2,1)S(1)} all-gather(bf16[96,192]{1,0:T(8,128)(2,1)} %param.22), channel_id=1, replica_groups=mesh['seq'=8,'head'=4] {'seq'}, dimensions={0}, use_global_device_ids=true | all-gather | bytes 331776 | tf_op jit(solution)/shard_map/all_gather | solution.py:162
  46.2 31.1 %all_gather.18 = bf16[768,192]{1,0:T(8,128)(2,1)S(1)} all-gather(bf16[96,192]{1,0:T(8,128)(2,1)S(1)} %copy-done.130), channel_id=1, replica_groups=mesh['seq'=8,'head'=4] {'seq'}, dimensions={0}, use_global_device_ids=true | all-gather | bytes 331776 | tf_op jit(solution)/shard_map/all_gather | solution.py:164
  79.5 4.3 collective-permute-start
  89.9 31.3 %all_gather.20 = bf16[768,192]{1,0:T(8,128)(2,1)S(1)} all-gather(bf16[96,192]{1,0:T(8,128)(2,1)S(1)} %copy-done.131), channel_id=1, replica_groups=mesh['seq'=8,'head'=4] {'seq'}, dimensions={0}, use_global_device_ids=true | all-gather | bytes 331776 | tf_op jit(solution)/shard_map/all_gather | solution.py:163
  123.3 31.2 %all_gather.21 = bf16[768,192]{1,0:T(8,128)(2,1)S(1)} all-gather(bf16[96,192]{1,0:T(8,128)(2,1)} %param.25), channel_id=1, replica_groups=mesh['seq'=8,'head'=4] {'seq'}, dimensions={0}, use_global_device_ids=true | all-gather | bytes 331776 | tf_op jit(solution)/shard_map/all_gather | solution.py:165
  159.9 22.4 %pmax.7 = f32[3,192]{1,0:T(4,128)} all-reduce(f32[3,192]{1,0:T(4,128)} %get-tuple-element.215), channel_id=1, replica_groups=mesh['seq'=8,'head'=4] {'seq'}, use_global_device_ids=true, to_apply=%region_6.7 | all-reduce | flops 576 | bytes 4608 | tf_op jit(solution)/shard_map/pmax | solution.py:186
  189.7 17.4 %psum.149 = f32[3,192]{1,0:T(4,128)S(1)} all-reduce(f32[3,192]{1,0:T(4,128)S(1)} %fusion.24), channel_id=1, replica_groups=mesh['seq'=8,'head'=4] {'seq'}, use_global_device_ids=true, to_apply=%region_9.10 | all-reduce | flops 576 | bytes 4608 | tf_op jit(solution)/shard_map/psum | solution.py:189
  207.1 47.1 %all-reduce.26.cloned.1.call-done = (f32[192,192]{1,0:T(8,128)}, f32[192,3,64]{0,2,1:T(8,128)}) async-done(((f32[192,192]{1,0:T(8,128)}, f32[192,3,64]{0,2,1:T(8,128)}), (f32[192,192]{1,0:T(8,128)}, f32[192,3,64]{0,2,1:T(8,128)})) %all-reduce.26.cloned.1.call-update) | async-done | bytes 294928 | tf_op jit(solution)/shard_map/psum | solution.py:172
  284.6 10.3 %fusion.112 = bf16[1024,192]{0,1:T(8,128)(2,1)S(1)} fusion(f32[3,64,1024]{2,1,0:T(8,128)S(1)} %fusion.186, bf16[1024,192]{0,1:T(8,128)(2,1)S(1)} %fusion.22, bf16[16,192]{0,1:T(8,128)(2,1)S(1)} %collective-permute-done.1, bf16[16,192]{0,1:T(8,128)(2,1)} %collective-permute-done, f32[192]{0:T(256)} %bitcast.372, f32[192]{0:T(256)} %bitcast.374, ...), kind=kLoop, calls=%fused_computation.383 | loop fusion | flops 45023232 | bytes 1644288 | tf_op jit(solution)/shard_map/convert_element_type | solution.py:225
  298.7 40.8 %all-reduce.14.cloned.1.call-done = bf16[1024,768]{1,0:T(8,128)(2,1)} async-done(((bf16[1024,768]{1,0:T(8,128)(2,1)}), bf16[1024,768]{1,0:T(8,128)(2,1)}) %all-reduce.14.cloned.1.call-update) | async-done | bytes 1572880 | tf_op jit(solution)/shard_map/psum | solution.py:226
  343.2 39.5 %all-gather.3.cloned.1.call-done = bf16[768,768]{1,0:T(8,128)(2,1)} async-done(((bf16[96,768]{1,0:T(8,128)(2,1)}), bf16[768,768]{1,0:T(8,128)(2,1)}) %all-gather.3.cloned.1.call-update) | async-done | bytes 1179664 | tf_op jit(solution)/shard_map/all_gather | solution.py:166
  382.7 4.9 fusion.205
  387.6 37.0 %all-gather.5.cloned.1.call-done = bf16[768,768]{1,0:T(8,128)(2,1)} async-done(((bf16[96,768]{1,0:T(8,128)(2,1)}), bf16[768,768]{1,0:T(8,128)(2,1)}) %all-gather.5.cloned.1.call-update) | async-done | bytes 1179664 | tf_op jit(solution)/shard_map/all_gather | solution.py:167
  424.6 5.5 convolution_convert_fusion.1
  430.3 41.6 %all-reduce.16.cloned.1.call-done = bf16[1024,768]{1,0:T(8,128)(2,1)} async-done(((bf16[1024,768]{1,0:T(8,128)(2,1)}), bf16[1024,768]{1,0:T(8,128)(2,1)}) %all-reduce.16.cloned.1.call-update) | async-done | bytes 1572880 | tf_op jit(solution)/shard_map/psum | solution.py:237
  490.3 41.8 %all-reduce.18.cloned.1.call-done = bf16[1024,768]{1,0:T(8,128)(2,1)} async-done(((bf16[1024,768]{1,0:T(8,128)(2,1)}), bf16[1024,768]{1,0:T(8,128)(2,1)}) %all-reduce.18.cloned.1.call-update) | async-done | bytes 1572880 | tf_op jit(solution)/shard_map/psum | solution.py:254
  532.1 4.6 multiply_reduce_fusion
  547.9 5.2 collective-permute-start.3
  566.9 60.1 %all-reduce.20.cloned.1.call-done = f32[3,64,3,64]{3,1,2,0:T(8,128)} async-done(((f32[3,64,3,64]{3,1,2,0:T(8,128)}), f32[3,64,3,64]{3,1,2,0:T(8,128)}) %all-reduce.20.cloned.1.call-update) | async-done | bytes 147472 | tf_op jit(solution)/shard_map/psum | solution.py:301
  682.1 12.4 %fusion.138 = f32[1024,192]{0,1:T(8,128)} fusion(bf16[1024,192]{0,1:T(8,128)(2,1)S(1)} %copy-done.8, bf16[16,192]{0,1:T(8,128)(2,1)} %collective-permute-done.3, bf16[16,192]{0,1:T(8,128)(2,1)} %collective-permute-done.2, f32[192]{0:T(256)} %bitcast.373, f32[192]{0:T(256)} %bitcast.375, f32[192]{0:T(256)} %bitcast.377, f32[192]{0:T(256)} %bitcast.379, ...), kind=kLoop, calls=%fused_computation.409 | loop fusion | flops 44826624 | bytes 2037504 | tf_op jit(solution)/shard_map/add | solution.py:336
  702.0 48.4 %all-reduce.24.cloned.1.call-done = (f32[192,3,64]{0,2,1:T(8,128)}, f32[192,192]{1,0:T(8,128)}) async-done(((f32[192,3,64]{0,2,1:T(8,128)}, f32[192,192]{1,0:T(8,128)}), (f32[192,3,64]{0,2,1:T(8,128)}, f32[192,192]{1,0:T(8,128)})) %all-reduce.24.cloned.1.call-update) | async-done | bytes 294928 | tf_op jit(solution)/shard_map/psum | solution.py:349
  774.4 5.8 copy.321
  780.3 4.6 all-to-all-start
  811.3 75.0 %all-reduce = (f32[192]{0:T(256)S(1)}, f32[192]{0:T(256)}, f32[768]{0:T(1024)}, f32[768]{0:T(1024)}, f32[768]{0:T(1024)}, /*index=5*/f32[768]{0:T(1024)}, f32[76...) all-reduce(f32[192]{0:T(256)S(1)} %reduce_sum.699, ...), channel_id=1, replica_groups=mesh['seq'=8,'head'=4] {'seq'}, use_global_device_ids=true, to_apply=%region_38.39 | all-reduce | flops 5859 | bytes 46872 | tf_op jit(solution)/shard_map/psum | solution.py:349
  (835 shorter events, 228.7 us)
Async XLA Ops:
  7.2 70.9 %copy-start = (bf16[1024,768]{1,0:T(8,128)(2,1)S(1)}, bf16[1024,768]{1,0:T(8,128)(2,1)}, u32[]{:S(2)}) copy-start(bf16[1024,768]{1,0:T(8,128)(2,1)} %param.19) | copy-start | bytes 4718596
  7.2 147.3 %all-reduce.12.cloned.1.call-start = ((), (), s32[]{:S(2)}) async-start(), calls=%async_computation.1 | async-start | bytes 393216 | tf_op jit(solution)/shard_map/psum | solution.py:172
  42.8 79.0 %copy-start.134 = (s32[1024]{0:T(1024)}, s32[1024]{0:T(1024)S(1)}, u32[]{:S(2)}) copy-start(s32[1024]{0:T(1024)S(1)} %fusion.302) | copy-start | bytes 12292
  45.0 233.4 %copy-start.93 = (bf16[1024,192]{0,1:T(8,128)(2,1)}, bf16[1024,192]{0,1:T(8,128)(2,1)S(1)}, u32[]{:S(2)}) copy-start(bf16[1024,192]{0,1:T(8,128)(2,1)S(1)} %fusion.23) | copy-start | bytes 1179652
  46.2 208.0 %all-reduce.26.cloned.1.call-start = ((), (), s32[]{:S(2)}) async-start(), calls=%async_computation.10 | async-start | bytes 786432 | tf_op jit(solution)/shard_map/psum | solution.py:172
  79.5 204.7 %collective-permute-start = (bf16[16,192]{0,1:T(8,128)(2,1)}, bf16[16,192]{0,1:T(8,128)(2,1)}, u32[]{:S(2)}, u32[]{:S(2)}) collective-permute-start(bf16[16,192]{0,1:T(8,128)(2,1)} %get-tuple-element.146), channel_id=1, source_target_pairs={{0,4},{4,8},{8,12},{12,16},{16,20},{20,24},{24,28},{1,5},{5,9},{9,... | collective-permute-start | bytes 18440 | tf_op jit(solution)/shard_map/ppermute | solution.py:26
  83.8 200.4 %collective-permute-start.1 = (bf16[16,192]{0,1:T(8,128)(2,1)}, bf16[16,192]{0,1:T(8,128)(2,1)S(1)}, u32[]{:S(2)}, u32[]{:S(2)}) collective-permute-start(bf16[16,192]{0,1:T(8,128)(2,1)} %get-tuple-element.147), channel_id=1, source_target_pairs={{4,0},{8,4},{12,8},{16,12},{20,16},{24,20},{28,24},{5,1},{9,5},{13... | collective-permute-start | bytes 18440 | tf_op jit(solution)/shard_map/ppermute | solution.py:28
  89.0 98.3 %copy-start.89 = (pred[192,1024]{1,0:T(8,128)(4,1)}, pred[192,1024]{1,0:T(8,128)(4,1)S(1)}, u32[]{:S(2)}) copy-start(pred[192,1024]{1,0:T(8,128)(4,1)S(1)} %broadcast_compare_fusion.1) | copy-start | bytes 589828
  123.1 151.2 %copy-start.29 = (f32[64,64]{1,0:T(8,128)}, f32[64,64]{1,0:T(8,128)S(1)}, u32[]{:S(2)}) copy-start(f32[64,64]{1,0:T(8,128)S(1)} %get-tuple-element.234) | copy-start | bytes 49156
  154.5 140.4 %copy-start.91 = (bf16[768,192]{1,0:T(8,128)(2,1)}, bf16[768,192]{1,0:T(8,128)(2,1)S(1)}, u32[]{:S(2)}) copy-start(bf16[768,192]{1,0:T(8,128)(2,1)S(1)} %all_gather.21) | copy-start | bytes 884740
  185.4 154.1 %all-reduce.14.cloned.1.call-start = ((), (), s32[]{:S(2)}) async-start(), calls=%async_computation.2 | async-start | bytes 3145728 | tf_op jit(solution)/shard_map/psum | solution.py:226
  297.5 85.3 %all-gather.3.cloned.1.call-start = ((), (), s32[]{:S(2)}) async-start(), calls=%async_computation.3 | async-start | bytes 1327104 | tf_op jit(solution)/shard_map/all_gather | solution.py:166
  298.1 126.6 %all-gather.5.cloned.1.call-start = ((), (), s32[]{:S(2)}) async-start(), calls=%async_computation.4 | async-start | bytes 1327104 | tf_op jit(solution)/shard_map/all_gather | solution.py:167
  298.6 173.3 %all-reduce.16.cloned.1.call-start = ((), (), s32[]{:S(2)}) async-start(), calls=%async_computation.5 | async-start | bytes 3145728 | tf_op jit(solution)/shard_map/psum | solution.py:237
  387.6 84.3 %copy-start.123 = (f32[768]{0:T(1024)S(1)}, f32[768]{0:T(1024)}, u32[]{:S(2)}) copy-start(f32[768]{0:T(1024)} %param.30) | copy-start | bytes 9220
  387.6 84.3 %copy-start.132 = (f32[768]{0:T(1024)S(1)}, f32[768]{0:T(1024)}, u32[]{:S(2)}) copy-start(f32[768]{0:T(1024)} %param.33) | copy-start | bytes 9220
  430.1 101.9 %all-reduce.18.cloned.1.call-start = ((), (), s32[]{:S(2)}) async-start(), calls=%async_computation.6 | async-start | bytes 3145728 | tf_op jit(solution)/shard_map/psum | solution.py:254
  489.0 138.0 %all-reduce.20.cloned.1.call-start = ((), (), s32[]{:S(2)}) async-start(), calls=%async_computation.7 | async-start | bytes 589824 | tf_op jit(solution)/shard_map/psum | solution.py:301
  546.6 135.4 %collective-permute-start.2 = (bf16[16,192]{0,1:T(8,128)(2,1)}, bf16[16,192]{0,1:T(8,128)(2,1)}, u32[]{:S(2)}, u32[]{:S(2)}) collective-permute-start(bf16[16,192]{0,1:T(8,128)(2,1)} %get-tuple-element.144), channel_id=1, source_target_pairs={{4,0},{8,4},{12,8},{16,12},{20,16},{24,20},{28,24},{5,1},{9,5},{13... | collective-permute-start | bytes 18440 | tf_op jit(solution)/shard_map/ppermute | solution.py:28
  547.9 134.1 %collective-permute-start.3 = (bf16[16,192]{0,1:T(8,128)(2,1)}, bf16[16,192]{0,1:T(8,128)(2,1)}, u32[]{:S(2)}, u32[]{:S(2)}) collective-permute-start(bf16[16,192]{0,1:T(8,128)(2,1)} %get-tuple-element.145), channel_id=1, source_target_pairs={{0,4},{4,8},{8,12},{12,16},{16,20},{20,24},{24,28},{1,5},{5,9},{9,... | collective-permute-start | bytes 18440 | tf_op jit(solution)/shard_map/ppermute | solution.py:26
  556.6 193.9 %all-reduce.24.cloned.1.call-start = ((), (), s32[]{:S(2)}) async-start(), calls=%async_computation.9 | async-start | bytes 786432 | tf_op jit(solution)/shard_map/psum | solution.py:349
  780.3 110.5 %all-to-all-start = ((bf16[8,96,2304]{2,1,0:T(8,128)(2,1)}), bf16[8,96,2304]{2,1,0:T(8,128)(2,1)}, u32[]{:S(2)}, u32[]{:S(2)}) async-start(bf16[8,96,2304]{2,1,0:T(8,128)(2,1)} %bitcast.318), calls=%async_computation | async-start | bytes 7077888 | tf_op jit(solution)/shard_map/all_to_all | solution.py:43
  785.0 101.9 %all-reduce.22.cloned.1.call-start = ((), (), s32[]{:S(2)}) async-start(), calls=%async_computation.8 | async-start | bytes 3145728 | tf_op jit(solution)/shard_map/psum | solution.py:387
  795.0 91.3 %copy-start.241 = (f32[3,64]{1,0:T(4,128)S(1)}, f32[3,64]{1,0:T(4,128)}, u32[]{:S(2)}) copy-start(f32[3,64]{1,0:T(4,128)} %get-tuple-element.232) | copy-start | bytes 2308
  (247 other events, 1741.4 us)
Sparse Core Ops, SparseCore 0:
  46.3 71.3 all-reduce.11
  185.5 68.6 all-reduce.25
  297.6 41.9 all-reduce.13
  341.6 41.1 all-gather.2
  384.8 39.8 all-gather.4
  430.2 41.6 all-reduce.15
  489.1 42.9 all-reduce.17
  556.7 70.2 all-reduce.19
  679.9 70.5 all-reduce.23
  795.1 44.0 all-reduce.21
where the time goes:
time: 909 us; the launch traced here: 902 us
  waiting for transfers between devices  358 us (39%)
  blocking collectives  241 us (27%)
  matrix products  131 us (14%)
  other arithmetic  80.5 us (9%)
  local copies, waits for them, and re-layouts  55.6 us (6%)
  between operations  18.5 us (2%)
  starting transfers between devices  17.7 us (2%)
    psum x1, blocking collectives, body(): lax.psum((grad_qland_part, grad_gain_one, grad_bias_one, grad_gain_two, g...  75 us
    psum x1, waiting for transfers between devices, body(): lax.psum((grad_mix_part, grad_kland_part), 'seq')  60.1 us
    psum x1, waiting for transfers between devices, body(): lax.psum((grad_qland_part, grad_gain_one, grad_bias_one, grad_gain_two, g...  48.4 us
    psum x2, waiting for transfers between devices, body(): lax.psum((across(member_low, queries), across(member_low, key_rows)), 'seq')  47.1 us
    psum x1, waiting for transfers between devices, body(): lax.psum(up_terms.astype(jnp.bfloat16), 'head').astype(jnp.float32)  41.8 us
    psum x1, waiting for transfers between devices, body(): lax.psum(feed_terms.astype(jnp.bfloat16), 'head').astype(jnp.float32)  41.6 us
    psum x1, waiting for transfers between devices, body(): lax.psum(against(mixed_rows, full_out).astype(jnp.bfloat16), 'head')  40.8 us
    all_gather x1, waiting for transfers between devices, body(): lax.all_gather(w_up, 'seq', axis=0, tiled=True)  39.5 us
  transfers between devices with their start and end apart: 15, of which 8 were waited for; matrix products, arithmetic and copies ran while one was open for 19% of the time, Pallas kernels for 0%

commit v1 on v0

--- a/solution.py
+++ b/solution.py
@@ -1,6 +1,10 @@
+import functools
+
 import jax
 import jax.numpy as jnp
 from jax import lax
+from jax.experimental import pallas as pl
+from jax.experimental.pallas import tpu as pltpu
 from jax.sharding import PartitionSpec as P
 
 HEAD_DIM = 64
@@ -116,7 +120,402 @@
     )
 
 
-def body(
+MESH = pl.DeviceIdType.MESH
+WIDE = jnp.float32
+LOW = jnp.bfloat16
+CHUNKS = 4
+
+
+def place():
+    s, h = lax.axis_index("seq"), lax.axis_index("head")
+    return s, h, s // 2, lax.rem(s, 2), h // 2, lax.rem(h, 2)
+
+
+def partners(count):
+    s, h, z, y, x, core = place()
+    lines = count // 2
+    core_peer = (s, 2 * x + 1 - core)
+    x_peer = (s, 2 * (1 - x) + core)
+    y_peer = (2 * z + 1 - y, h)
+    z_peers = [(2 * lax.rem(z + j, lines) + y, h) for j in range(1, lines)]
+    return core_peer, x_peer, y_peer, z_peers
+
+
+def remote(src, dst, send, recv, device):
+    return pltpu.make_async_remote_copy(
+        src_ref=src, dst_ref=dst, send_sem=send, recv_sem=recv, device_id=device, device_id_type=MESH
+    )
+
+
+class Gather:
+    def __init__(self, count, shard, full, own, zs, zr, ys, yr):
+        self.count, self.shard, self.full, self.own = count, shard, full, own
+        self.zs, self.zr, self.ys, self.yr = zs, zr, ys, yr
+        s, h, z, y, _, _ = place()
+        _, _, y_peer, z_peers = partners(count)
+        lines = count // 2
+        self.local = pltpu.make_async_copy(shard, full.at[s], own)
+        self.z_copies = [
+            remote(shard, full.at[s], zs.at[j], zr.at[j], z_peers[j]) for j in range(lines - 1)
+        ]
+        self.y_copies = [remote(shard, full.at[s], ys.at[0], yr.at[0], y_peer)]
+        for j in range(1, lines):
+            slot = 2 * lax.rem(z - j + lines, lines) + y
+            self.y_copies.append(
+                remote(full.at[slot], full.at[slot], ys.at[j], yr.at[j], y_peer)
+            )
+
+    def start(self):
+        for copy in self.z_copies:
+            copy.start()
+        self.y_copies[0].start()
+        self.local.start()
+
+    def forward(self):
+        for z_copy, y_copy in zip(self.z_copies, self.y_copies[1:]):
+            z_copy.wait_recv()
+            y_copy.start()
+
+    def finish(self):
+        self.local.wait()
+        for copy in self.y_copies:
+            copy.wait_recv()
+
+    def close(self):
+        for copy in self.z_copies + self.y_copies:
+            copy.wait_send()
+
+
+class Scatter:
+    def __init__(self, count, terms, y_buf, pair, z_buf, ys, yr, zs, zr):
+        self.count, self.terms, self.y_buf, self.pair, self.z_buf = count, terms, y_buf, pair, z_buf
+        s, h, z, y, _, _ = place()
+        _, _, y_peer, z_peers = partners(count)
+        lines = count // 2
+        self.lines, self.z, self.y = lines, z, y
+        self.y_copies = []
+        for j in range(lines):
+            line = lax.rem(z + j, lines)
+            self.y_copies.append(
+                remote(terms.at[2 * line + 1 - y], y_buf.at[line], ys.at[j], yr.at[j], y_peer)
+            )
+        self.z_copies = [
+            remote(pair.at[j], z_buf.at[j], zs.at[j], zr.at[j], z_peers[j])
+            for j in range(lines - 1)
+        ]
+
+    def start(self):
+        for j in list(range(1, self.lines)) + [0]:
+            self.y_copies[j].start()
+
+    def forward(self):
+        for j in range(1, self.lines):
+            line = lax.rem(self.z + j, self.lines)
+            self.y_copies[j].wait_recv()
+            self.pair[j - 1] = (
+                self.terms[2 * line + self.y].astype(WIDE) + self.y_buf[line].astype(WIDE)
+            ).astype(LOW)
+            self.z_copies[j - 1].start()
+
+    def finish(self, out):
+        self.y_copies[0].wait_recv()
+        total = self.terms[2 * self.z + self.y].astype(WIDE) + self.y_buf[self.z].astype(WIDE)
+        for j, copy in enumerate(self.z_copies):
+            copy.wait_recv()
+            total = total + self.z_buf[j].astype(WIDE)
+        out[...] = total
+
+    def close(self):
+        for copy in self.z_copies + self.y_copies:
+            copy.wait_send()
+
+
+def greet(devices):
+    barrier = pltpu.get_barrier_semaphore()
+    for device in devices:
+        pl.semaphore_signal(barrier, inc=1, device_id=device, device_id_type=MESH)
+    pl.semaphore_wait(barrier, len(devices))
+
+
+def fold(rows):
+    return rows.reshape(rows.shape[0] // 8, 8, rows.shape[1]).sum(axis=0)
+
+
+class HeadSum:
+    def __init__(self, terms, core_in, x_out, x_in, sems):
+        self.terms, self.core_in, self.x_out, self.x_in, self.sems = terms, core_in, x_out, x_in, sems
+        _, _, _, _, _, self.core = place()
+        self.half = terms.shape[1] // 2
+        self.core_peer, self.x_peer, _, _ = partners(2)
+
+    def core_copy(self, c):
+        away = pl.ds(pl.multiple_of((1 - self.core) * self.half, self.half), self.half)
+        return remote(
+            self.terms.at[c, away], self.core_in.at[c], self.sems.at[0, c], self.sems.at[1, c], self.core_peer
+        )
+
+    def x_copy(self, c):
+        return remote(self.x_out.at[c], self.x_in.at[c], self.sems.at[2, c], self.sems.at[3, c], self.x_peer)
+
+    def pair_up(self, c):
+        self.core_copy(c).wait_recv()
+        here = pl.ds(pl.multiple_of(self.core * self.half, self.half), self.half)
+        self.x_out[c] = (
+            self.terms[c, here].astype(WIDE) + self.core_in[c].astype(WIDE)
+        ).astype(LOW)
+        self.x_copy(c).start()
+
+    def total(self, c, rows):
+        return self.x_out[c, rows].astype(WIDE) + self.x_in[c, rows].astype(WIDE)
+
+
+def gelu_and_slope(v):
+    square = v * v
+    t = jnp.tanh(0.7978845608 * (v + 0.044715 * v * square))
+    half = 0.5 * (1.0 + t)
+    slope = half + 0.5 * v * (1.0 - t * t) * (0.7978845608 * (1.0 + 0.134145 * square))
+    return v * half, slope
+
+
+def row_kernel(
+    count,
+    mixed_ref, inputs_ref, cot_ref, wo_ref, wu_ref, wd_ref, vec_ref,
+    out_ref, one_ref, gmix_ref, gwo_ref, gwu_ref, gwd_ref, sums_ref,
+    wo, wu, wd, hidden, active, slope, grad_two, grad_lift, grad_one,
+    norm_one, inv_one, wide_two, tmp,
+    terms1, cin1, xo1, xi1, terms2, cin2, xo2, xi2, terms3, cin3, xo3, xi3,
+    go, gu, gd, yb_o, pr_o, zb_o, yb_u, pr_u, zb_u, yb_d, pr_d, zb_d, acc,
+    own_sem, gz_s, gz_r, gy_s, gy_r, sy_s, sy_r, sz_s, sz_r, h1, h2, h3, share_s, share_r,
+):
+    s, h, z, y, x, core = place()
+    core_peer, x_peer, y_peer, z_peers = partners(count)
+    rows, width = inputs_ref.shape
+    size = rows // CHUNKS
+    half = size // 2
+    step = 32
+    gathers = [
+        Gather(count, shard, full, own_sem.at[k], gz_s.at[k], gz_r.at[k], gy_s.at[k], gy_r.at[k])
+        for k, (shard, full) in enumerate(((wo_ref, wo), (wu_ref, wu), (wd_ref, wd)))
+    ]
+    scatters = [
+        Scatter(count, terms, yb, pr, zb, sy_s.at[k], sy_r.at[k], sz_s.at[k], sz_r.at[k])
+        for k, (terms, yb, pr, zb) in enumerate(
+            ((go, yb_o, pr_o, zb_o), (gu, yb_u, pr_u, zb_u), (gd, yb_d, pr_d, zb_d))
+        )
+    ]
+    sums = [
+        HeadSum(terms1, cin1, xo1, xi1, h1),
+        HeadSum(terms2, cin2, xo2, xi2, h2),
+        HeadSum(terms3, cin3, xo3, xi3, h3),
+    ]
+    greet([core_peer, x_peer, y_peer] + z_peers)
+    for gather in gathers:
+        gather.start()
+    for gather in gathers:
+        gather.forward()
+
+    def chunk_rows(c):
+        return pl.ds(pl.multiple_of(c * size, size), size)
+
+    def my_rows(c):
+        return pl.ds(pl.multiple_of(c * size + core * half, half), half)
+
+    def share(k, ref, c):
+        return remote(ref.at[my_rows(c)], ref.at[my_rows(c)], share_s.at[k, c], share_r.at[k, c], core_peer)
+
+    def each(body):
+        lax.fori_loop(0, CHUNKS, lambda c, carry: (body(c), carry)[1], 0)
+
+    def pieces(body):
+        lax.fori_loop(0, half // step, lambda i, carry: (body(pl.multiple_of(i * step, step)), carry)[1], 0)
+
+    bias_out, bias_up, bias_down, gain_one, bias_one, gain_two, bias_two = (
+        vec_ref[k : k + 1, :] for k in range(7)
+    )
+    acc[...] = jnp.zeros_like(acc)
+    gathers[0].finish()
+
+    def project_out(c):
+        terms1[c] = against(mixed_ref[chunk_rows(c)], wo[...].reshape(width, wo.shape[2])).astype(LOW)
+        sums[0].core_copy(c).start()
+
+    each(project_out)
+    each(sums[0].pair_up)
+    gathers[1].finish()
+    gathers[2].finish()
+
+    def feed_forward(c):
+        sums[0].x_copy(c).wait_recv()
+
+        def norm(i):
+            at = pl.ds(pl.multiple_of(c * size + core * half + i, step), step)
+            kept = pl.ds(pl.multiple_of(c * half + i, step), step)
+            pre = inputs_ref[at].astype(WIDE) + sums[0].total(c, pl.ds(i, step)) + bias_out
+            normed, inv = normalize(pre)
+            norm_one[kept] = normed
+            inv_one[kept] = inv
+            hidden[at] = (normed * gain_one + bias_one).astype(LOW)
+
+        pieces(norm)
+        share(0, hidden, c).start()
+        share(0, hidden, c).wait_recv()
+        at = chunk_rows(c)
+        tmp[...] = matmul_low(hidden[at], wu[...].reshape(width, wu.shape[2]))
+
+        def curve(i, carry):
+            r = pl.ds(pl.multiple_of(i * step, step), step)
+            to = pl.ds(pl.multiple_of(c * size + i * step, step), step)
+            value, grade = gelu_and_slope(tmp[r] + bias_up)
+            active[to] = value.astype(LOW)
+            slope[to] = grade
+            return carry
+
+        lax.fori_loop(0, size // step, curve, 0)
+        terms2[c] = against(active[at], wd[...].reshape(width, wd.shape[2])).astype(LOW)
+        sums[1].core_copy(c).start()
+        sums[1].pair_up(c)
+
+    each(feed_forward)
+
+    def feed_back(c):
+        sums[1].x_copy(c).wait_recv()
+
+        def norm(i):
+            at = pl.ds(pl.multiple_of(c * size + core * half + i, step), step)
+            kept = pl.ds(pl.multiple_of(c * half + i, step), step)
+            pre = norm_one[kept] * gain_one + bias_one + sums[1].total(c, pl.ds(i, step)) + bias_down
+            normed, inv = normalize(pre)
+            out_ref[at] = (normed * gain_two + bias_two).astype(LOW)
+            grad = cot_ref[at].astype(WIDE)
+            back = norm_back(grad * gain_two, normed, inv)
+            wide_two[kept] = back
+            grad_two[at] = back.astype(LOW)
+            acc[0] += fold(grad * normed)
+            acc[1] += fold(grad)
+            acc[2] += fold(back)
+
+        pieces(norm)
+        share(1, grad_two, c).start()
+        share(2, out_ref, c).start()
+        share(1, grad_two, c).wait_recv()
+        at = chunk_rows(c)
+        tmp[...] = matmul_low(grad_two[at], wd[...].reshape(width, wd.shape[2]))
+
+        def curve(i, carry):
+            r = pl.ds(pl.multiple_of(i * step, step), step)
+            to = pl.ds(pl.multiple_of(c * size + i * step, step), step)
+            value = tmp[r] * slope[to]
+            grad_lift[to] = value.astype(LOW)
+            acc[6] += fold(value)
+            return carry
+
+        lax.fori_loop(0, size // step, curve, 0)
+        terms3[c] = against(grad_lift[at], wu[...].reshape(width, wu.shape[2])).astype(LOW)
+        sums[2].core_copy(c).start()
+        sums[2].pair_up(c)
+
+    each(feed_back)
+
+    def grads_of(left, right, ref):
+        ref[...] = across(left, right).astype(LOW).reshape(ref.shape)
+
+    grads_of(grad_two[...], active[...], gd)
+    scatters[2].start()
+    grads_of(hidden[...], grad_lift[...], gu)
+    scatters[1].start()
+
+    def mix_back(c):
+        sums[2].x_copy(c).wait_recv()
+
+        def norm(i):
+            at = pl.ds(pl.multiple_of(c * size + core * half + i, step), step)
+            kept = pl.ds(pl.multiple_of(c * half + i, step), step)
+            normed = norm_one[kept]
+            grad = wide_two[kept] + sums[2].total(c, pl.ds(i, step))
+            back = norm_back(grad * gain_one, normed, inv_one[kept])
+            one_ref[kept] = back
+            grad_one[at] = back.astype(LOW)
+            acc[3] += fold(grad * normed)
+            acc[4] += fold(grad)
+            acc[5] += fold(back)
+
+        pieces(norm)
+        share(3, grad_one, c).start()
+        share(3, grad_one, c).wait_recv()
+        at = chunk_rows(c)
+        gmix_ref[at] = matmul_low(grad_one[at], wo[...].reshape(width, wo.shape[2])).astype(LOW)
+
+    each(mix_back)
+    scatters[2].forward()
+    scatters[1].forward()
+    grads_of(grad_one[...], mixed_ref[...], go)
+    scatters[0].start()
+    for k in range(7):
+        sums_ref[k : k + 1, :] = jnp.sum(acc[k], axis=0, keepdims=True)
+    sums_ref[7:8, :] = jnp.zeros_like(sums_ref[7:8, :])
+    scatters[0].forward()
+    for scatter, ref in zip(scatters, (gwo_ref, gwu_ref, gwd_ref)):
+        scatter.finish(ref)
+
+    def settle(c):
+        for head_sum in sums:
+            head_sum.core_copy(c).wait_send()
+            head_sum.x_copy(c).wait_send()
+        share(2, out_ref, c).wait_recv()
+        for k, ref in enumerate((hidden, grad_two, out_ref, grad_one)):
+            share(k, ref, c).wait_send()
+
+    each(settle)
+    for group in gathers + scatters:
+        group.close()
+
+
+def rows_forward_and_back(count, mixed, inputs, cot, w_out, w_up, w_down, vectors):
+    rows, width = inputs.shape
+    feed = w_up.shape[1]
+    near = mixed.shape[1]
+    size = rows // CHUNKS
+    half = size // 2
+    part = width // count
+    lines = count // 2
+    low, wide = (lambda *shape: pltpu.VMEM(shape, LOW)), (lambda *shape: pltpu.VMEM(shape, WIDE))
+    sem = lambda *shape: pltpu.SemaphoreType.DMA(shape)
+    head_sum = [low(CHUNKS, size, width)] + [low(CHUNKS, half, width)] * 3
+    scatter = lambda n: [low(lines, part, n), low(lines - 1, part, n), low(lines - 1, part, n)]
+    vmem = pl.BlockSpec(memory_space=pltpu.VMEM)
+    shape = jax.ShapeDtypeStruct
+    return pl.pallas_call(
+        functools.partial(row_kernel, count),
+        out_shape=(
+            shape((rows, width), LOW),
+            shape((rows // 2, width), WIDE),
+            shape((rows, near), LOW),
+            shape((part, near), WIDE),
+            shape((part, feed), WIDE),
+            shape((part, feed), WIDE),
+            shape((8, width), WIDE),
+        ),
+        in_specs=[vmem] * 7,
+        out_specs=[vmem] * 7,
+        scratch_shapes=[
+            low(count, part, near), low(count, part, feed), low(count, part, feed),
+            low(rows, width), low(rows, feed), wide(rows, feed), low(rows, width), low(rows, feed), low(rows, width),
+            wide(rows // 2, width), wide(rows // 2, 1), wide(rows // 2, width), wide(size, feed),
+            *head_sum, *head_sum, *head_sum,
+            low(count, part, near), low(count, part, feed), low(count, part, feed),
+            *scatter(near), *scatter(feed), *scatter(feed),
+            wide(7, 8, width),
+            sem(3), sem(3, lines - 1), sem(3, lines - 1), sem(3, lines), sem(3, lines),
+            sem(3, lines), sem(3, lines), sem(3, lines - 1), sem(3, lines - 1),
+            sem(4, CHUNKS), sem(4, CHUNKS), sem(4, CHUNKS), sem(4, CHUNKS), sem(4, CHUNKS),
+        ],
+        compiler_params=pltpu.CompilerParams(
+            collective_id=1, has_side_effects=True, vmem_limit_bytes=60 * 2**20
+        ),
+    )(mixed, inputs, cot, w_out, w_up, w_down, vectors)
+
+
+def plain_body(
     inputs,
     cotangent,
     item_lengths,
@@ -421,7 +820,281 @@
     )
 
 
+def fused_body(
+    inputs,
+    cotangent,
+    item_lengths,
+    w_query,
+    w_key,
+    w_value,
+    w_out,
+    w_up,
+    w_down,
+    bias_query,
+    bias_value,
+    bias_out,
+    bias_up,
+    bias_down,
+    gain_one,
+    bias_one,
+    gain_two,
+    bias_two,
+    conv_taps,
+):
+    low_type = jnp.bfloat16
+    tok_rows = inputs.shape[0]
+    heads_here = conv_taps.shape[0]
+    width_here = heads_here * HEAD_DIM
+    slots = ITEMS * LAND
+    reach = (KERNEL - 1) // 2
+    score_scale = HEAD_DIM ** (-0.5)
+    pref = jnp.float32
+    first_row = lax.axis_index("seq") * tok_rows
+    positions = first_row + jnp.arange(tok_rows, dtype=jnp.int32)
+    item_id, land_slot = locate(item_lengths, positions)
+    rim_item = locate(
+        item_lengths, first_row - reach + jnp.arange(tok_rows + 2 * reach, dtype=jnp.int32)
+    )[0]
+    slot_item = jnp.arange(slots, dtype=jnp.int32) // LAND
+    member = land_slot[:, None] == jnp.arange(slots, dtype=jnp.int32)[None, :]
+    member_low = member.astype(low_type)
+    counts = jnp.repeat((item_lengths // LAND).astype(jnp.float32), LAND)
+    same_f = item_id[:, None] == slot_item[None, :]
+    same_b = same_f.T
+    tap_cols = jnp.repeat(conv_taps, HEAD_DIM, axis=0)
+    full_query, full_key, full_value = (
+        lax.all_gather(w_query, "seq", axis=0, tiled=True),
+        lax.all_gather(w_key, "seq", axis=0, tiled=True),
+        lax.all_gather(w_value, "seq", axis=0, tiled=True),
+    )
+    queries = (matmul_low(inputs, full_query) + bias_query).astype(low_type)
+    key_rows = matmul_low(inputs, full_key).astype(low_type)
+    value_rows = (matmul_low(inputs, full_value) + bias_value).astype(low_type)
+    query_sums, key_sums = lax.psum(
+        (across(member_low, queries), across(member_low, key_rows)), "seq"
+    )
+    query_land = (
+        (query_sums / counts[:, None]).astype(low_type).reshape(slots, heads_here, HEAD_DIM)
+    )
+    key_land = (key_sums / counts[:, None]).astype(low_type).reshape(slots, heads_here, HEAD_DIM)
+    query_heads = queries.reshape(tok_rows, heads_here, HEAD_DIM)
+    key_heads = key_rows.reshape(tok_rows, heads_here, HEAD_DIM)
+    value_heads = value_rows.reshape(tok_rows, heads_here, HEAD_DIM)
+    scores_b = (
+        jnp.einsum("lhd,thd->hlt", query_land, key_heads, preferred_element_type=pref) * score_scale
+    )
+    scores_b = jnp.where(same_b[None], scores_b, MASKED)
+    maxima_b = lax.pmax(jnp.max(scores_b, axis=2), "seq")
+    weights_b = jnp.exp(scores_b - maxima_b[:, :, None])
+    weights_b_low = weights_b.astype(low_type)
+    numer_sum, totals_b = lax.psum(
+        (
+            jnp.einsum("hlt,thd->lhd", weights_b_low, value_heads, preferred_element_type=pref),
+            jnp.sum(weights_b, axis=2),
+        ),
+        "seq",
+    )
+    totals_cols = totals_b.T[:, :, None]
+    kernel_v = numer_sum / totals_cols
+    land_q = query_land.reshape(ITEMS, LAND, heads_here, HEAD_DIM)
+    land_k = key_land.reshape(ITEMS, LAND, heads_here, HEAD_DIM)
+    land_kernel = jax.nn.softmax(
+        jnp.einsum("ilhd,imhd->ihlm", land_q, land_k, preferred_element_type=pref) * score_scale,
+        axis=-1,
+    )
+    inverse, inverse_back = jax.vjp(pseudo_inverse, land_kernel)
+    kernel_items = kernel_v.reshape(ITEMS, LAND, heads_here, HEAD_DIM)
+    mixing = jnp.einsum("ihlm,imhd->ilhd", inverse, kernel_items, precision=PRECISE)
+    mixing = mixing.astype(low_type).reshape(slots, heads_here, HEAD_DIM)
+    scores_f = (
+        jnp.einsum("thd,lhd->htl", query_heads, key_land, preferred_element_type=pref) * score_scale
+    )
+    weights_f = jax.nn.softmax(jnp.where(same_f[None], scores_f, MASKED), axis=-1)
+    weights_f_low = weights_f.astype(low_type)
+    attended = jnp.einsum("htl,lhd->thd", weights_f_low, mixing, preferred_element_type=pref)
+    attended = attended.reshape(tok_rows, width_here)
+    value_rim = extended(value_rows, (("seq", 0),), reach)
+    conv_sum = jnp.zeros((tok_rows, width_here), jnp.float32)
+    for offset in range(KERNEL):
+        in_item = (rim_item[offset : offset + tok_rows] == item_id)[:, None]
+        conv_sum = conv_sum + jnp.where(
+            in_item,
+            value_rim[offset : offset + tok_rows].astype(jnp.float32)
+            * tap_cols[:, offset][None, :],
+            0.0,
+        )
+    mixed_rows = (attended + conv_sum).astype(low_type)
+    vectors = jnp.stack(
+        [bias_out, bias_up, bias_down, gain_one, bias_one, gain_two, bias_two, bias_two]
+    )
+    output, grad_one_half, grad_mixed, out_shard, grad_up_shard, grad_down_shard, row_sums = (
+        rows_forward_and_back(
+            lax.axis_size("seq"), mixed_rows, inputs, cotangent, w_out, w_up, w_down, vectors
+        )
+    )
+    chip_sums = lax.psum(row_sums[:6], ("seq", "head")) * 0.5
+    (
+        grad_gain_two,
+        grad_bias_two,
+        grad_bias_down,
+        grad_gain_one,
+        grad_bias_one,
+        grad_bias_out,
+    ) = (chip_sums[k] for k in range(6))
+    grad_bias_up = row_sums[6]
+    grad_mixed_wide = grad_mixed.astype(jnp.float32)
+    grad_heads = grad_mixed.reshape(tok_rows, heads_here, HEAD_DIM)
+    grad_rim = extended(grad_mixed, (("seq", 0),), reach)
+    grad_conv_v = jnp.zeros((tok_rows, width_here), jnp.float32)
+    tap_terms = []
+    for offset in range(KERNEL):
+        in_item = (rim_item[offset : offset + tok_rows] == item_id)[:, None]
+        neighbour = jnp.where(
+            in_item, value_rim[offset : offset + tok_rows].astype(jnp.float32), 0.0
+        )
+        tap_terms.append(
+            jnp.sum(
+                (grad_mixed_wide * neighbour).reshape(tok_rows, heads_here, HEAD_DIM), axis=(0, 2)
+            )
+        )
+        mirror = 2 * reach - offset
+        mirror_item = (rim_item[mirror : mirror + tok_rows] == item_id)[:, None]
+        grad_conv_v = grad_conv_v + jnp.where(
+            mirror_item,
+            grad_rim[mirror : mirror + tok_rows].astype(jnp.float32) * tap_cols[:, offset][None, :],
+            0.0,
+        )
+    grad_taps = jnp.stack(tap_terms, axis=1)
+    grad_weights_f = jnp.einsum("thd,lhd->htl", grad_heads, mixing, preferred_element_type=pref)
+    grad_mix_part = jnp.einsum(
+        "htl,thd->lhd", weights_f_low, grad_heads, preferred_element_type=pref
+    )
+    grad_scores_f = weights_f * (
+        grad_weights_f - jnp.sum(weights_f * grad_weights_f, axis=2, keepdims=True)
+    )
+    grad_scores_f = grad_scores_f.astype(low_type)
+    grad_query_f = (
+        jnp.einsum("htl,lhd->thd", grad_scores_f, key_land, preferred_element_type=pref)
+        * score_scale
+    )
+    grad_kland_part = (
+        jnp.einsum("htl,thd->lhd", grad_scores_f, query_heads, preferred_element_type=pref)
+        * score_scale
+    )
+    grad_mixing, grad_kland_f = lax.psum((grad_mix_part, grad_kland_part), "seq")
+    grad_mix_items = grad_mixing.reshape(ITEMS, LAND, heads_here, HEAD_DIM)
+    grad_inverse = jnp.einsum("ilhd,imhd->ihlm", grad_mix_items, kernel_items, precision=PRECISE)
+    grad_kernel_v = jnp.einsum("ihlm,ilhd->imhd", inverse, grad_mix_items, precision=PRECISE)
+    grad_kernel_v = grad_kernel_v.reshape(slots, heads_here, HEAD_DIM)
+    (grad_land_kernel,) = inverse_back(grad_inverse)
+    grad_scores_a = land_kernel * (
+        grad_land_kernel - jnp.sum(land_kernel * grad_land_kernel, axis=-1, keepdims=True)
+    )
+    grad_scores_a = grad_scores_a * score_scale
+    grad_qland_a = jnp.einsum(
+        "ihlm,imhd->ilhd", grad_scores_a, land_k.astype(jnp.float32), precision=PRECISE
+    )
+    grad_kland_a = jnp.einsum(
+        "ihlm,ilhd->imhd", grad_scores_a, land_q.astype(jnp.float32), precision=PRECISE
+    )
+    grad_numer = (grad_kernel_v / totals_cols).astype(low_type)
+    grad_totals = -jnp.sum(grad_kernel_v * kernel_v, axis=2) / totals_b.T
+    grad_weights_b = jnp.einsum(
+        "lhd,thd->hlt", grad_numer, value_heads, preferred_element_type=pref
+    )
+    grad_weights_b = grad_weights_b + grad_totals.T[:, :, None]
+    grad_scores_b = (weights_b * grad_weights_b).astype(low_type)
+    grad_qland_part = (
+        jnp.einsum("hlt,thd->lhd", grad_scores_b, key_heads, preferred_element_type=pref)
+        * score_scale
+    )
+    grad_key_b = (
+        jnp.einsum("hlt,lhd->thd", grad_scores_b, query_land, preferred_element_type=pref)
+        * score_scale
+    )
+    grad_value_b = jnp.einsum(
+        "hlt,lhd->thd", weights_b_low, grad_numer, preferred_element_type=pref
+    )
+    grad_query_rows = grad_query_f.reshape(tok_rows, width_here)
+    grad_values = grad_value_b.reshape(tok_rows, width_here) + grad_conv_v
+    (grad_qland_b, grad_bias_up, grad_taps, query_f_total, grad_bias_value) = lax.psum(
+        (
+            grad_qland_part,
+            grad_bias_up,
+            grad_taps,
+            jnp.sum(grad_query_rows, axis=0),
+            jnp.sum(grad_values, axis=0),
+        ),
+        "seq",
+    )
+    grad_qland = grad_qland_a.reshape(slots, width_here) + grad_qland_b.reshape(slots, width_here)
+    grad_kland = grad_kland_a.reshape(slots, width_here) + grad_kland_f.reshape(slots, width_here)
+    member_wide = member.astype(jnp.float32)
+    grad_queries = grad_query_rows + jnp.dot(
+        member_wide, grad_qland / counts[:, None], precision=PRECISE
+    )
+    grad_keys = grad_key_b.reshape(tok_rows, width_here) + jnp.dot(
+        member_wide, grad_kland / counts[:, None], precision=PRECISE
+    )
+    grad_bias_query = query_f_total + jnp.sum(grad_qland, axis=0)
+    queries_low = grad_queries.astype(low_type)
+    keys_low = grad_keys.astype(low_type)
+    values_low = grad_values.astype(low_type)
+    grad_queryw = across(inputs, queries_low)
+    grad_keyw = across(inputs, keys_low)
+    grad_valuew = across(inputs, values_low)
+    input_terms = (
+        against(queries_low, full_query)
+        + against(keys_low, full_key)
+        + against(values_low, full_value)
+    )
+    core = lax.rem(lax.axis_index("head"), 2)
+    halves = lax.psum(input_terms.astype(jnp.bfloat16), "head").astype(jnp.float32)
+    size = tok_rows // CHUNKS
+    halves = halves.reshape(CHUNKS, 2, size // 2, -1)
+    grad_one_half = grad_one_half.reshape(CHUNKS, size // 2, -1)
+    mine = (
+        grad_one_half + lax.dynamic_index_in_dim(halves, core, axis=1, keepdims=False)
+    ).astype(low_type)
+    other = lax.ppermute(mine, "head", [(0, 1), (1, 0), (2, 3), (3, 2)])
+    grad_inputs = jnp.where(
+        core == 0, jnp.stack([mine, other], axis=1), jnp.stack([other, mine], axis=1)
+    ).reshape(tok_rows, -1)
+    query_shard, key_shard, value_shard = side_by_side(
+        (
+            grad_queryw.astype(jnp.bfloat16),
+            grad_keyw.astype(jnp.bfloat16),
+            grad_valuew.astype(jnp.bfloat16),
+        ),
+        "seq",
+        0,
+        1,
+    )
+    return (
+        output,
+        grad_inputs,
+        query_shard,
+        key_shard,
+        value_shard,
+        out_shard,
+        grad_up_shard,
+        grad_down_shard,
+        grad_bias_query,
+        grad_bias_value,
+        grad_bias_out,
+        grad_bias_up,
+        grad_bias_down,
+        grad_gain_one,
+        grad_bias_one,
+        grad_gain_two,
+        grad_bias_two,
+        grad_taps,
+    )
+
+
 def solution(mesh):
+    part = 768 // mesh.shape["seq"]
+    body = fused_body if part % 16 == 0 else plain_body
     return jax.shard_map(
         body,
         mesh=mesh,

time: 909 us -> 729 us (0.80)
  waiting for transfers between devices: 358 us -> 155 us
  Pallas kernels: 0 us -> 127 us
  blocking collectives: 241 us -> 198 us
  matrix products: 131 us -> 101 us
  other arithmetic: 80.5 us -> 64.1 us
    psum x8 -> x5, waiting for transfers between devices: 280 us -> 151 us  [the longest x1 51.6 us: fused_body(): lax.psum((grad_qland_part, grad_bias_up, grad_taps, jnp.sum(grad_query_ro...]
    pallas_call x0 -> x1, Pallas kernels: none -> 127 us  [rows_forward_and_back(): pl.pallas_call(functools.partial(row_kernel, count), out_shape=(shape((ro...]
    all_gather x2 -> x0, waiting for transfers between devices: 76.5 us -> none  [the longest x1 39.5 us: body(): lax.all_gather(w_up, 'seq', axis=0, tiled=True)]
    all_gather x4 -> x3, blocking collectives: 127 us -> 95.8 us  [the longest x1 33 us: fused_body(): lax.all_gather(w_query, 'seq', axis=0, tiled=True)]
    add x4 -> x3, other arithmetic: 13 us -> 0.58 us  [the longest x1 0.57 us: fused_body(): grad_bias_query = query_f_total + jnp.sum(grad_qland, axis=0)]
    psum x2 -> x3, blocking collectives: 92.3 us -> 80 us  [the longest x1 40.9 us: fused_body(): chip_sums = lax.psum(row_sums[:6], ('seq', 'head')) * 0.5]
    dot_general x6 -> x3, matrix products: 15.2 us -> 3.33 us  [matmul_low(): return jnp.dot(left, right, preferred_element_type=jnp.float32)]
    convert_element_type x6 -> x7, other arithmetic: 20.6 us -> 18.7 us  [the longest x1 11.9 us: fused_body(): mixed_rows = (attended + conv_sum).astype(low_type)]
  transfers between devices with their start and end apart: 15 -> 11, of which waited for: 8 -> 4; matrix products, arithmetic and copies ran while one was open for 19% -> 14% of each run, Pallas kernels for 0% -> 0%
where the time goes in v1:
time: 729 us; the launch traced here: 723 us
  blocking collectives  198 us (27%)
  waiting for transfers between devices  155 us (21%)
  Pallas kernels  127 us (17%)
  matrix products  101 us (14%)
  other arithmetic  64.1 us (9%)
  local copies, waits for them, and re-layouts  47.6 us (7%)
  between operations  18.2 us (2%)
  starting transfers between devices  12.8 us (2%)
    pallas_call x1, Pallas kernels, rows_forward_and_back(): pl.pallas_call(functools.partial(row_kernel, count), out_shape=(shape((ro...  127 us
    psum x1, waiting for transfers between devices, fused_body(): lax.psum((grad_qland_part, grad_bias_up, grad_taps, jnp.sum(grad_query_ro...  51.6 us
    psum x1, waiting for transfers between devices, fused_body(): lax.psum((grad_mix_part, grad_kland_part), 'seq')  50.1 us
    psum x2, waiting for transfers between devices, fused_body(): lax.psum((across(member_low, queries), across(member_low, key_rows)), 'seq')  49 us
    psum x1, blocking collectives, fused_body(): chip_sums = lax.psum(row_sums[:6], ('seq', 'head')) * 0.5  40.9 us
    all_gather x1, blocking collectives, fused_body(): lax.all_gather(w_query, 'seq', axis=0, tiled=True)  33 us
    all_gather x1, blocking collectives, fused_body(): lax.all_gather(w_key, 'seq', axis=0, tiled=True)  31.8 us
    all_gather x1, blocking collectives, fused_body(): lax.all_gather(w_value, 'seq', axis=0, tiled=True)  31.1 us
  transfers between devices with their start and end apart: 11, of which 4 were waited for; matrix products, arithmetic and copies ran while one was open for 14% of the time, Pallas kernels for 0%

profile of v1, /device:TPU:0, one launch (start us, length us, event | category | flops | bytes accessed | tf_op | source)
XLA Modules:
  0.0 722.7 jit_solution(15715355833569059143)
XLA Ops:
  9.0 33.0 %all_gather.10 = bf16[768,192]{1,0:T(8,128)(2,1)S(1)} all-gather(bf16[96,192]{1,0:T(8,128)(2,1)} %param.22), channel_id=1, replica_groups=mesh['seq'=8,'head'=4] {'seq'}, dimensions={0}, use_global_device_ids=true | all-gather | bytes 331776 | tf_op jit(solution)/shard_map/all_gather | solution.py:866
  46.9 31.1 %all_gather.9 = bf16[768,192]{1,0:T(8,128)(2,1)S(1)} all-gather(bf16[96,192]{1,0:T(8,128)(2,1)S(1)} %copy-done.104), channel_id=1, replica_groups=mesh['seq'=8,'head'=4] {'seq'}, dimensions={0}, use_global_device_ids=true | all-gather | bytes 331776 | tf_op jit(solution)/shard_map/all_gather | solution.py:868
  80.0 3.6 collective-permute-start
  89.1 31.8 %all_gather.11 = bf16[768,192]{1,0:T(8,128)(2,1)S(1)} all-gather(bf16[96,192]{1,0:T(8,128)(2,1)S(1)} %copy-done.105), channel_id=1, replica_groups=mesh['seq'=8,'head'=4] {'seq'}, dimensions={0}, use_global_device_ids=true | all-gather | bytes 331776 | tf_op jit(solution)/shard_map/all_gather | solution.py:867
  128.6 21.9 %pmax.7 = f32[3,192]{1,0:T(4,128)S(1)} all-reduce(f32[3,192]{1,0:T(4,128)} %get-tuple-element.215), channel_id=1, replica_groups=mesh['seq'=8,'head'=4] {'seq'}, use_global_device_ids=true, to_apply=%region_6.7 | all-reduce | flops 576 | bytes 4608 | tf_op jit(solution)/shard_map/pmax | solution.py:887
  155.4 17.3 %psum.93 = f32[3,192]{1,0:T(4,128)S(1)} all-reduce(f32[3,192]{1,0:T(4,128)S(1)} %fusion.10), channel_id=1, replica_groups=mesh['seq'=8,'head'=4] {'seq'}, use_global_device_ids=true, to_apply=%region_9.10 | all-reduce | flops 576 | bytes 4608 | tf_op jit(solution)/shard_map/psum | solution.py:890
  172.8 49.0 %all-reduce.17.cloned.1.call-done = (f32[192,192]{1,0:T(8,128)}, f32[192,3,64]{0,2,1:T(8,128)}) async-done(((f32[192,192]{1,0:T(8,128)}, f32[192,3,64]{0,2,1:T(8,128)}), (f32[192,192]{1,0:T(8,128)}, f32[192,3,64]{0,2,1:T(8,128)})) %all-reduce.17.cloned.1.call-update) | async-done | bytes 294928 | tf_op jit(solution)/shard_map/psum | solution.py:873
  242.2 3.6 fusion.280
  246.2 2.9 fusion.159
  251.0 11.9 %fusion.93.mixed_ref = bf16[1024,192]{1,0:T(8,128)(2,1)} fusion(f32[1024,192]{1,0:T(8,128)S(1)} %copy.319, bf16[1024,192]{1,0:T(8,128)(2,1)S(1)} %fusion.6, bf16[16,192]{1,0:T(8,128)(2,1)S(1)} %collective-permute-done.1, bf16[16,192]{1,0:T(8,128)(2,1)S(1)} %collective-permute-done, f32[192]{0:T(256)S(1)} %bitcast.346, f32[192]{0:T(256)S(1)} %bitcast.348, ...), kind=kLoop, calls=%fused_computation.309 | loop fusion | flops 45023232 | bytes 1644288 | tf_op jit(solution)/shard_map/convert_element_type | solution.py:926
  263.0 127.2 %shard_map.322 = (bf16[1024,768]{1,0:T(8,128)(2,1)}, f32[512,768]{1,0:T(8,128)}, bf16[1024,192]{1,0:T(8,128)(2,1)}, f32[96,192]{1,0:T(8,128)}, f32[96,768]{1,0:T...) custom-call(bf16[1024,192]{1,0:T(8,128)(2,1)} %fusion.93.mixed_ref, bf16[1024,768]{1,0:T(8,128)(2,1)} %inputs_ref.1, ...), custom_call_target="tpu_custom_call" | custom-call | tf_op jit(solution)/shard_map/pallas_call | solution.py:487
  409.0 3.0 fusion.150
  412.1 2.8 fusion.151
  414.9 2.8 fusion.152
  420.5 3.7 collective-permute-done.2
  424.1 50.1 %all-reduce.11.cloned.1.call-done = f32[3,64,3,64]{3,1,2,0:T(8,128)} async-done(((f32[3,64,3,64]{3,1,2,0:T(8,128)}), f32[3,64,3,64]{3,1,2,0:T(8,128)}) %all-reduce.11.cloned.1.call-update) | async-done | bytes 147472 | tf_op jit(solution)/shard_map/psum | solution.py:984
  508.7 3.3 fusion.249
  515.3 2.7 convolution_multiply_fusion
  529.2 10.3 %fusion.272 = (f32[192]{0:T(256)}, bf16[1024,192]{1,0:T(8,128)(2,1)}) fusion(f32[1024,192]{1,0:T(8,128)S(1)} %copy.355, f32[192]{0:T(256)S(1)} %bitcast.347, bf16[1040,192]{1,0:T(8,128)(2,1)S(1)} %get-tuple-element.142, pred[1024]{0:T(1024)(128)(4,1)S(1)} %copy-done.205, f32[192]{0:T(256)S(1)} %bitcast.349, pred[1024]{0:T(1024)(128)(4,1)S(1)} %copy-done.128, ...), kind=kLoop, calls=%fused_computation.559 | loop fusion | flops 26345280 | bytes 14215680 | tf_op jit(solution)/shard_map/reduce_sum | solution.py:1026
  545.8 51.6 %all-reduce.15.cloned.1.call-done = (f32[192,3,64]{0,2,1:T(8,128)}, f32[192,192]{1,0:T(8,128)}) async-done(((f32[192,3,64]{0,2,1:T(8,128)}, f32[192,192]{1,0:T(8,128)}), (f32[192,3,64]{0,2,1:T(8,128)}, f32[192,192]{1,0:T(8,128)})) %all-reduce.15.cloned.1.call-update) | async-done | bytes 294928 | tf_op jit(solution)/shard_map/psum | solution.py:1020
  616.5 4.2 all-to-all-start
  620.8 3.5 add_convert_fusion
  639.4 40.9 %psum.101 = f32[6,768]{1,0:T(8,128)S(1)} all-reduce(f32[6,768]{1,0:T(8,128)S(1)} %bitcast.343), channel_id=1, replica_groups=mesh['seq'=8,'head'=4] {'seq','head'}, use_global_device_ids=true, to_apply=%region_31.32 | all-reduce | flops 4608 | bytes 36864 | tf_op jit(solution)/shard_map/psum | solution.py:935
  683.1 21.8 %all-reduce = (f32[192]{0:T(256)S(1)}, f32[192]{0:T(256)}, f32[768]{0:T(1024)}, f32[3,33]{1,0:T(4,128)}) all-reduce(f32[192]{0:T(256)S(1)} %reduce_sum.556, f32[192]{0:T(256)S(1)} %copy-done.230, f32[768]{0:T(1024)S(1)} %slice_reduce_fusion.6, f32[3,33]{1,0:T(4,128)S(1)} %stack.183), channel_id=1, replica_groups=mesh['seq'=8,'head'=4] {'seq'}, use_global_device_ids=true, to_apply=%region_27.28 | all-reduce | flops 1251 | bytes 10008 | tf_op jit(solution)/shard_map/psum | solution.py:1020
  (854 shorter events, 170.5 us)
Async XLA Ops:
  7.2 71.6 %copy-start.1 = (bf16[1024,768]{1,0:T(8,128)(2,1)S(1)}, bf16[1024,768]{1,0:T(8,128)(2,1)}, u32[]{:S(2)}) copy-start(bf16[1024,768]{1,0:T(8,128)(2,1)} %inputs_ref.1) | copy-start | bytes 4718596
  7.2 71.6 %copy-start.266 = (f32[192]{0:T(256)S(1)}, f32[192]{0:T(256)}, u32[]{:S(2)}) copy-start(f32[192]{0:T(256)} %param.29) | copy-start | bytes 2308
  7.2 117.3 %all-reduce.9.cloned.1.call-start = ((), (), s32[]{:S(2)}) async-start(), calls=%async_computation.1 | async-start | bytes 393216 | tf_op jit(solution)/shard_map/psum | solution.py:873
  42.8 78.7 %copy-start.106 = (s32[1024]{0:T(1024)}, s32[1024]{0:T(1024)S(1)}, u32[]{:S(2)}) copy-start(s32[1024]{0:T(1024)S(1)} %fusion.242) | copy-start | bytes 12292
  46.9 174.9 %all-reduce.17.cloned.1.call-start = ((), (), s32[]{:S(2)}) async-start(), calls=%async_computation.5 | async-start | bytes 786432 | tf_op jit(solution)/shard_map/psum | solution.py:873
  80.0 170.7 %collective-permute-start = (bf16[16,192]{1,0:T(8,128)(2,1)}, bf16[16,192]{1,0:T(8,128)(2,1)S(1)}, u32[]{:S(2)}, u32[]{:S(2)}) collective-permute-start(bf16[16,192]{1,0:T(8,128)(2,1)} %get-tuple-element.143), channel_id=1, source_target_pairs={{0,4},{4,8},{8,12},{12,16},{16,20},{20,24},{24,28},{1,5},{5,9},{9,... | collective-permute-start | bytes 18440 | tf_op jit(solution)/shard_map/ppermute | solution.py:30
  83.6 167.0 %collective-permute-start.1 = (bf16[16,192]{1,0:T(8,128)(2,1)}, bf16[16,192]{1,0:T(8,128)(2,1)S(1)}, u32[]{:S(2)}, u32[]{:S(2)}) collective-permute-start(bf16[16,192]{1,0:T(8,128)(2,1)} %get-tuple-element.144), channel_id=1, source_target_pairs={{4,0},{8,4},{12,8},{16,12},{20,16},{24,20},{28,24},{5,1},{9,5},{13... | collective-permute-start | bytes 18440 | tf_op jit(solution)/shard_map/ppermute | solution.py:32
  152.9 68.9 %copy-start.110 = (f32[192]{0:T(256)S(1)}, f32[192]{0:T(256)}, u32[]{:S(2)}) copy-start(f32[192]{0:T(256)} %copy-done.109) | copy-start | bytes 2308
  153.0 321.3 %all-reduce.11.cloned.1.call-start = ((), (), s32[]{:S(2)}) async-start(), calls=%async_computation.2 | async-start | bytes 589824 | tf_op jit(solution)/shard_map/psum | solution.py:984
  154.8 70.1 %copy-start.84 = (bf16[3,64,3,64]{1,3,2,0:T(8,128)(2,1)S(1)}, bf16[3,64,3,64]{1,3,2,0:T(8,128)(2,1)}, u32[]{:S(2)}) copy-start(bf16[3,64,3,64]{1,3,2,0:T(8,128)(2,1)} %copy.351) | copy-start | bytes 221188
  250.6 153.7 %copy-start.94 = (bf16[16,192]{1,0:T(8,128)(2,1)}, bf16[16,192]{1,0:T(8,128)(2,1)S(1)}, u32[]{:S(2)}) copy-start(bf16[16,192]{1,0:T(8,128)(2,1)S(1)} %collective-permute-done) | copy-start | bytes 18436
  399.0 21.4 %collective-permute-start.3 = (bf16[16,192]{1,0:T(8,128)(2,1)S(1)}, bf16[16,192]{1,0:T(8,128)(2,1)S(1)}, u32[]{:S(2)}, u32[]{:S(2)}) collective-permute-start(bf16[16,192]{1,0:T(8,128)(2,1)S(1)} %copy-done.229), channel_id=1, source_target_pairs={{0,4},{4,8},{8,12},{12,16},{16,20},{20,24},{24,28},{1,5},{5,9},{9,... | collective-permute-start | bytes 18440 | tf_op jit(solution)/shard_map/ppermute | solution.py:30
  402.0 195.4 %all-reduce.15.cloned.1.call-start = ((), (), s32[]{:S(2)}) async-start(), calls=%async_computation.4 | async-start | bytes 786432 | tf_op jit(solution)/shard_map/psum | solution.py:1020
  418.3 5.9 collective-permute-start.2
  540.7 60.2 %copy-start.59 = (f32[3,3,64,64]{2,3,1,0:T(8,128)S(1)}, f32[3,3,64,64]{2,3,1,0:T(8,128)}, u32[]{:S(2)}) copy-start(f32[3,3,64,64]{2,3,1,0:T(8,128)} %copy-done.55) | copy-start | bytes 442372
  540.7 60.2 %copy-start.114 = (f32[3,3,64]{2,1,0:T(4,128)S(1)}, f32[3,3,64]{2,1,0:T(4,128)}, u32[]{:S(2)}) copy-start(f32[3,3,64]{2,1,0:T(4,128)} %copy-done.112) | copy-start | bytes 6916
  540.7 60.2 %copy-start.269 = (f32[3,3,64]{2,1,0:T(4,128)S(1)}, f32[3,3,64]{2,1,0:T(4,128)}, u32[]{:S(2)}) copy-start(f32[3,3,64]{2,1,0:T(4,128)} %copy-done.268) | copy-start | bytes 6916
  545.8 60.2 %copy-start.107 = (s32[1024]{0:T(1024)S(1)}, s32[1024]{0:T(1024)}, u32[]{:S(2)}) copy-start(s32[1024]{0:T(1024)} %copy-done.106) | copy-start | bytes 12292
  545.8 60.2 %copy-start.111 = (f32[192]{0:T(256)S(1)}, f32[192]{0:T(256)}, u32[]{:S(2)}) copy-start(f32[192]{0:T(256)} %copy-done.109) | copy-start | bytes 2308
  616.5 90.4 %all-to-all-start = ((bf16[8,96,576]{2,1,0:T(8,128)(2,1)}), bf16[8,96,576]{2,1,0:T(8,128)(2,1)}, u32[]{:S(2)}, u32[]{:S(2)}) async-start(bf16[8,96,576]{2,1,0:T(8,128)(2,1)} %bitcast.76), calls=%async_computation | async-start | bytes 1966080 | tf_op jit(solution)/shard_map/all_to_all | solution.py:47
  620.7 60.2 %all-reduce.13.cloned.1.call-start = ((), (), s32[]{:S(2)}) async-start(), calls=%async_computation.3 | async-start | bytes 3145728 | tf_op jit(solution)/shard_map/psum | solution.py:1052
  625.9 55.0 %copy-start.9 = (f32[512,768]{1,0:T(8,128)S(1)}, f32[512,768]{1,0:T(8,128)}, u32[]{:S(2)}) copy-start(f32[512,768]{1,0:T(8,128)} %get-tuple-element.26) | copy-start | bytes 4718596
  631.4 73.5 %copy-start.263 = (f32[3,64]{1,0:T(4,128)S(1)}, f32[3,64]{1,0:T(4,128)}, u32[]{:S(2)}) copy-start(f32[3,64]{1,0:T(4,128)} %get-tuple-element.229) | copy-start | bytes 2308
  683.1 25.9 %collective-permute-start.4 = (bf16[4,128,768]{2,1,0:T(8,128)(2,1)}, bf16[4,128,768]{2,1,0:T(8,128)(2,1)}, u32[]{:S(2)}, u32[]{:S(2)}) collective-permute-start(bf16[4,128,768]{2,1,0:T(8,128)(2,1)} %fusion.4), channel_id=1, source_target_pairs={{0,1},{1,0},{2,3},{3,2},{4,5},{5,4},{6,7},{7,6},{8,9},{9,8},{10,11... | collective-permute-start | bytes 2359304 | tf_op jit(solution)/shard_map/ppermute | solution.py:1059
  (257 other events, 1621.5 us)
Sparse Core Ops, SparseCore 0:
  47.0 71.3 all-reduce.8
  153.1 68.6 all-reduce.16
  402.1 72.0 all-reduce.10
  526.8 70.5 all-reduce.14
  626.0 44.6 all-reduce.12

commit v2 on v0

--- a/solution.py
+++ b/solution.py
@@ -1,6 +1,11 @@
+import functools
+import types
+
 import jax
 import jax.numpy as jnp
 from jax import lax
+from jax.experimental import pallas as pl
+from jax.experimental.pallas import tpu as pltpu
 from jax.sharding import PartitionSpec as P
 
 HEAD_DIM = 64
@@ -116,7 +121,1117 @@
     )
 
 
-def body(
+MESH = pl.DeviceIdType.MESH
+WIDE = jnp.float32
+LOW = jnp.bfloat16
+CHUNKS = 4
+PAD = 256
+REACH = (KERNEL - 1) // 2
+BLOCK = 64
+SPAN = BLOCK + 2 * REACH
+BORDER = 16
+
+
+def place():
+    s, h = lax.axis_index("seq"), lax.axis_index("head")
+    return s, h, s // 2, lax.rem(s, 2), h // 2, lax.rem(h, 2)
+
+
+def core_of_chip():
+    s, _, _, _, x, core = place()
+    return (s, 2 * x + 1 - core)
+
+
+def x_neighbour():
+    s, _, _, _, x, core = place()
+    return (s, 2 * (1 - x) + core)
+
+
+def y_neighbour():
+    _, h, z, y, _, _ = place()
+    return (2 * z + 1 - y, h)
+
+
+def along_z(count):
+    _, h, z, y, _, _ = place()
+    lines = count // 2
+    return [(2 * lax.rem(z + j, lines) + y, h) for j in range(1, lines)]
+
+
+def along_seq(count):
+    s, h = place()[:2]
+    return [(lax.rem(s + j, count), h) for j in range(1, count)]
+
+
+def remote(src, dst, send, recv, device):
+    return pltpu.make_async_remote_copy(
+        src_ref=src, dst_ref=dst, send_sem=send, recv_sem=recv, device_id=device, device_id_type=MESH
+    )
+
+
+def greet(devices):
+    for device in devices:
+        pl.semaphore_signal(
+            pltpu.get_barrier_semaphore(), inc=1, device_id=device, device_id_type=MESH
+        )
+
+
+def greeted(devices):
+    pl.semaphore_wait(pltpu.get_barrier_semaphore(), len(devices))
+
+
+class Gather:
+    def __init__(self, count, shard, full, lanes, own, zs, zr, ys, yr):
+        s, _, z, y, _, _ = place()
+        lines = count // 2
+        shard = shard.at[:, lanes]
+        view = lambda slot: full.at[slot, :, lanes]
+        self.local = pltpu.make_async_copy(shard, view(s), own)
+        self.z_copies = [
+            remote(shard, view(s), zs.at[j], zr.at[j], device)
+            for j, device in enumerate(along_z(count))
+        ]
+        self.y_copies = [remote(shard, view(s), ys.at[0], yr.at[0], y_neighbour())]
+        for j in range(1, lines):
+            slot = 2 * lax.rem(z - j + lines, lines) + y
+            self.y_copies.append(remote(view(slot), view(slot), ys.at[j], yr.at[j], y_neighbour()))
+
+    def start(self):
+        for copy in self.z_copies:
+            copy.start()
+        self.y_copies[0].start()
+        self.local.start()
+
+    def forward(self):
+        for z_copy, y_copy in zip(self.z_copies, self.y_copies[1:]):
+            z_copy.wait_recv()
+            y_copy.start()
+
+    def finish(self):
+        self.local.wait()
+        for copy in self.y_copies:
+            copy.wait_recv()
+
+    def close(self):
+        for copy in self.z_copies + self.y_copies:
+            copy.wait_send()
+
+
+class Scatter:
+    def __init__(self, count, terms, y_buf, pair, z_buf, ys, yr, zs, zr):
+        self.terms, self.y_buf, self.pair, self.z_buf = terms, y_buf, pair, z_buf
+        _, _, self.z, self.y, _, _ = place()
+        self.lines = count // 2
+        self.y_copies = []
+        for j in range(self.lines):
+            line = lax.rem(self.z + j, self.lines)
+            self.y_copies.append(
+                remote(
+                    terms.at[2 * line + 1 - self.y], y_buf.at[line], ys.at[j], yr.at[j], y_neighbour()
+                )
+            )
+        self.z_copies = [
+            remote(pair.at[j], z_buf.at[j], zs.at[j], zr.at[j], device)
+            for j, device in enumerate(along_z(count))
+        ]
+
+    def fill(self, left, right):
+        self.terms[...] = across(left, right).astype(LOW).reshape(self.terms.shape)
+
+    def start(self, first=0, last=None):
+        order = list(range(1, self.lines)) + [0]
+        for j in order[first:last]:
+            self.y_copies[j].start()
+
+    def forward(self, first=1, last=None):
+        for j in range(self.lines)[first:last]:
+            line = lax.rem(self.z + j, self.lines)
+            self.y_copies[j].wait_recv()
+            self.pair[j - 1] = (
+                self.terms[2 * line + self.y].astype(WIDE) + self.y_buf[line].astype(WIDE)
+            ).astype(LOW)
+            self.z_copies[j - 1].start()
+
+    def finish(self):
+        self.y_copies[0].wait_recv()
+        total = self.terms[2 * self.z + self.y].astype(WIDE) + self.y_buf[self.z].astype(WIDE)
+        for j, copy in enumerate(self.z_copies):
+            copy.wait_recv()
+            total = total + self.z_buf[j].astype(WIDE)
+        return total
+
+    def close(self):
+        for copy in self.z_copies + self.y_copies:
+            copy.wait_send()
+
+
+class Spread:
+    def __init__(self, count, blocks, send, recv):
+        s = place()[0]
+        self.copies = [
+            remote(blocks.at[s], blocks.at[s], send.at[j], recv.at[j], device)
+            for j, device in enumerate(along_seq(count))
+        ]
+
+    def start(self):
+        for copy in self.copies:
+            copy.start()
+
+    def finish(self):
+        for copy in self.copies:
+            copy.wait_recv()
+
+    def close(self):
+        for copy in self.copies:
+            copy.wait_send()
+
+
+class Swap(Spread):
+    def __init__(self, count, out, into, send, recv):
+        s = place()[0]
+        self.out, self.into = out, into
+        self.copies = [
+            remote(out.at[device[0]], into.at[s], send.at[j], recv.at[j], device)
+            for j, device in enumerate(along_seq(count))
+        ]
+
+    def start(self):
+        s = place()[0]
+        super().start()
+        self.into[s] = self.out[s]
+
+
+class HeadSum:
+    def __init__(self, turn, terms, core_in, x_out, x_in, sems):
+        self.turn, self.terms, self.core_in, self.x_out, self.x_in = turn, terms, core_in, x_out, x_in
+        self.sems = sems
+        self.core = place()[5]
+        self.half = terms.shape[1] // 2
+
+    def core_copy(self, c, turn=None):
+        sems = self.sems.at[self.turn if turn is None else turn]
+        away = pl.ds(pl.multiple_of((1 - self.core) * self.half, self.half), self.half)
+        return remote(
+            self.terms.at[c, away], self.core_in.at[c], sems.at[0, c], sems.at[1, c], core_of_chip()
+        )
+
+    def x_copy(self, c, turn=None):
+        turn = self.turn if turn is None else turn
+        sems = self.sems.at[turn]
+        return remote(
+            self.x_out.at[c], self.x_in.at[turn % 2, c], sems.at[2, c], sems.at[3, c], x_neighbour()
+        )
+
+    def offer(self, c, rows):
+        if self.turn > 0:
+            self.core_copy(c, self.turn - 1).wait_send()
+        self.terms[c] = rows
+        self.core_copy(c).start()
+
+    def pair_up(self, c):
+        self.core_copy(c).wait_recv()
+        if self.turn > 0:
+            self.x_copy(c, self.turn - 1).wait_send()
+        here = pl.ds(pl.multiple_of(self.core * self.half, self.half), self.half)
+        self.x_out[c] = (
+            self.terms[c, here].astype(WIDE) + self.core_in[c].astype(WIDE)
+        ).astype(LOW)
+        self.x_copy(c).start()
+
+    def arrived(self, c):
+        self.x_copy(c).wait_recv()
+
+    def total(self, c, rows):
+        return self.x_out[c, rows].astype(WIDE) + self.x_in[self.turn % 2, c, rows].astype(WIDE)
+
+
+def iota(shape, dim):
+    return lax.broadcasted_iota(jnp.int32, shape, dim)
+
+
+def fold(rows):
+    return rows.reshape(rows.shape[0] // 8, 8, rows.shape[1]).sum(axis=0)
+
+
+def gelu_and_slope(v):
+    square = v * v
+    t = jnp.tanh(0.7978845608 * (v + 0.044715 * v * square))
+    half = 0.5 * (1.0 + t)
+    slope = half + 0.5 * v * (1.0 - t * t) * (0.7978845608 * (1.0 + 0.134145 * square))
+    return v * half, slope
+
+
+def exact(left, right, dims=(1, 0)):
+    return lax.dot_general(
+        left,
+        right,
+        (((dims[0],), (dims[1],)), ((), ())),
+        preferred_element_type=WIDE,
+        precision=PRECISE,
+    )
+
+
+def dense(block):
+    n = block.shape[0]
+    rest = jnp.concatenate([block[0 : n // 2, 128:], block[n // 2 :, 128:]], axis=1)
+    return jnp.concatenate([block[:, 0:128], rest], axis=0)
+
+
+def undense(block):
+    n = block.shape[0] * 2 // 3
+    rest = jnp.concatenate([block[n:, 0:64], block[n:, 64:128]], axis=0)
+    return jnp.concatenate([block[0:n], rest], axis=1)
+
+
+def loop(count, body):
+    lax.fori_loop(0, count, lambda i, carry: (body(i), carry)[1], 0)
+
+
+def layer_kernel(count, names, *refs):
+    r = types.SimpleNamespace(**dict(zip(names, refs)))
+    s, h, z, y, x, core = place()
+    rows, width = r.inputs_hbm.shape
+    near = r.w_query.shape[1]
+    heads = near // HEAD_DIM
+    feed = r.w_up.shape[1]
+    size = rows // CHUNKS
+    half = size // 2
+    step = 32
+    lines = count // 2
+    two = 2 * LAND
+    scale = HEAD_DIM**-0.5
+    chunk_rows = lambda c: pl.ds(pl.multiple_of(c * size, size), size)
+    my_rows = lambda c: pl.ds(pl.multiple_of(c * size + core * half, half), half)
+    everyone = along_seq(count)
+    before, after = (lax.rem(s + count - 1, count), h), (lax.rem(s + 1, count), h)
+
+    flat = lambda ref: ref[...].reshape(1, ref.shape[0])
+    bias_query, bias_value, bias_out = flat(r.bias_query), flat(r.bias_value), flat(r.bias_out)
+    bias_up, bias_down = flat(r.bias_up), flat(r.bias_down)
+    gain_one, bias_one, gain_two, bias_two = (
+        flat(r.gain_one), flat(r.bias_one), flat(r.gain_two), flat(r.bias_two)
+    )
+
+    def gather(k, shard, full, lo, hi):
+        return Gather(
+            count, shard, full, slice(lo, hi), r.g_own.at[k], r.g_zs.at[k], r.g_zr.at[k], r.g_ys.at[k], r.g_yr.at[k]
+        )
+
+    def scatter(k, terms, y_buf, pair, z_buf):
+        return Scatter(
+            count, terms, y_buf, pair, z_buf, r.s_ys.at[k], r.s_yr.at[k], r.s_zs.at[k], r.s_zr.at[k]
+        )
+
+    gather_qk = gather(0, r.packed, r.w_near, 0, 2 * near)
+    gather_vo = gather(1, r.packed, r.w_near, 2 * near, 4 * near)
+    gather_up1 = gather(2, r.w_up, r.full_up, 0, feed // 2)
+    gather_up2 = gather(3, r.w_up, r.full_up, feed // 2, feed)
+    gather_down1 = gather(4, r.w_down, r.full_down, 0, feed // 2)
+    gather_down2 = gather(5, r.w_down, r.full_down, feed // 2, feed)
+    gathers = [gather_qk, gather_vo, gather_up1, gather_up2, gather_down1, gather_down2]
+    scatter_out = scatter(0, r.t_out, r.yb_out, r.pr_out, r.zb_out)
+    scatter_up = scatter(1, r.t_up, r.yb_up, r.pr_up, r.zb_up)
+    scatter_down = scatter(2, r.t_down, r.yb_down, r.pr_down, r.zb_down)
+    scatter_qkv = scatter(3, r.t_qkv, r.yb_qkv, r.pr_qkv, r.zb_qkv)
+    scatters = [scatter_out, scatter_up, scatter_down, scatter_qkv]
+    sums = [HeadSum(k, r.terms, r.core_in, r.x_out, r.x_in, r.h_sems) for k in range(4)]
+    landmarks = Spread(count, r.land_part, r.e_s.at[0], r.e_r.at[0])
+    numer_swap = Swap(count, r.numer_out, r.numer_in, r.e_s.at[1], r.e_r.at[1])
+    kernel_spread = Spread(count, r.kernel_v, r.e_s.at[2], r.e_r.at[2])
+    mixing_spread = Spread(count, r.mix_part, r.e_s.at[3], r.e_r.at[3])
+    kland_spread = Spread(count, r.kland_part, r.e_s.at[4], r.e_r.at[4])
+    qland_spread = Spread(count, r.qland_part, r.e_s.at[5], r.e_r.at[5])
+    vector_spread = Spread(count, r.vector_part, r.e_s.at[6], r.e_r.at[6])
+    small_spread = Spread(count, r.small_part, r.e_s.at[7], r.e_r.at[7])
+    spreads = [
+        landmarks, numer_swap, kernel_spread, mixing_spread, kland_spread, qland_spread, vector_spread, small_spread,
+    ]
+
+    def rim(k, ext):
+        first = remote(
+            ext.at[pl.ds(REACH, REACH)], ext.at[pl.ds(REACH + rows, REACH)], r.rim_s.at[k, 0], r.rim_r.at[k, 0], before
+        )
+        last = remote(
+            ext.at[pl.ds(rows, REACH)], ext.at[pl.ds(0, REACH)], r.rim_s.at[k, 1], r.rim_r.at[k, 1], after
+        )
+        return [first, last]
+
+    rims = [rim(0, r.value_ext), rim(1, r.grad_ext)]
+
+    def share(k, ref, c):
+        return remote(
+            ref.at[my_rows(c)], ref.at[my_rows(c)], r.share_s.at[k, c], r.share_r.at[k, c], core_of_chip()
+        )
+
+    load_inputs = pltpu.make_async_copy(r.inputs_hbm, r.inputs, r.io.at[0])
+    load_cotangent = pltpu.make_async_copy(r.cotangent_hbm, r.cotangent, r.io.at[1])
+    stores = [
+        pltpu.make_async_copy(ref, out, r.io.at[2 + k])
+        for k, (ref, out) in enumerate(
+            (
+                (r.output, r.output_hbm),
+                (r.grad_inputs, r.grad_inputs_hbm),
+                (r.grad_w_out, r.grad_w_out_hbm),
+                (r.grad_w_up, r.grad_w_up_hbm),
+                (r.grad_w_down, r.grad_w_down_hbm),
+                (r.grad_near, r.grad_near_hbm),
+            )
+        )
+    ]
+    store_output, store_grad_inputs, store_out, store_up, store_down, store_near = stores
+    vector_core = remote(
+        r.vector_sum.at[0], r.vector_sum.at[1], r.core_s.at[0], r.core_r.at[0], core_of_chip()
+    )
+
+    met = [core_of_chip(), x_neighbour()] + everyone
+    greet(met)
+    load_inputs.start()
+    r.packed[:, 0:near] = r.w_query[...]
+    r.packed[:, near : 2 * near] = r.w_key[...]
+    r.packed[:, 2 * near : 3 * near] = r.w_value[...]
+    r.packed[:, 3 * near : 4 * near] = r.w_out[...]
+    ends = jnp.where(s == 0, r.lengths[0], jnp.where(s == count - 1, r.lengths[2], 0))
+    edge_start = jnp.where(s == 0, 0, rows - ends)
+    edge_end = edge_start + ends
+    edge_count = ends // LAND
+    mid_count = r.lengths[1] // LAND
+    mid_first = s * rows - r.lengths[0]
+    first_slot = jnp.maximum(mid_first, 0) // mid_count
+    item_edge = jnp.where(s == 0, ends, jnp.where(s == count - 1, rows - ends, -1))
+
+    def members():
+        token, lane = iota((rows, two), 0), iota((rows, two), 1)
+        mid = lane < LAND
+        at_edge = (token >= edge_start) & (token < edge_end)
+        start = jnp.where(mid, (first_slot + lane) * mid_count - mid_first, (lane - LAND) * edge_count + edge_start)
+        length = jnp.where(mid, mid_count, edge_count)
+        inside = (token >= start) & (token < start + length)
+        belongs = jnp.where(mid, jnp.where(at_edge, 0.0, 1.0), jnp.where(at_edge, 1.0, 0.0))
+        r.member[...] = jnp.where(inside, belongs, 0.0).astype(LOW)
+
+    members()
+    greeted(met)
+    gather_qk.start()
+    gather_vo.start()
+    load_cotangent.start()
+    r.small_part[s] = jnp.zeros((8, PAD), WIDE)
+    head_lane = iota((8, PAD), 1) // HEAD_DIM
+    masks = [(head_lane == k).astype(WIDE)[0:1] for k in range(heads)]
+    masks_low = [m[:, :near].astype(LOW) for m in masks]
+
+    def spread_heads(ref, block):
+        for k in range(heads):
+            ref[k * two : (k + 1) * two, :] = block * masks_low[k]
+
+    def own_heads(wide_rows, group, lanes):
+        return sum(
+            wide_rows[k * group : (k + 1) * group, :] * masks[k][:, :lanes] for k in range(heads)
+        )
+
+    def bands(ref, flipped):
+        token, lane = iota((BLOCK, 2 * SPAN), 0), iota((BLOCK, 2 * SPAN), 1)
+        upper = lane < SPAN
+        offset = jnp.where(upper, lane, lane - SPAN) - token
+        for k in range(heads):
+            band = jnp.zeros((BLOCK, 2 * SPAN), WIDE)
+            for j in range(KERNEL):
+                at = KERNEL - 1 - j if flipped else j
+                band = jnp.where(offset == at, r.conv_taps[k, j], band)
+            high = band.astype(LOW).astype(WIDE)
+            ref[k * BLOCK : (k + 1) * BLOCK, :] = jnp.where(upper, high, band - high).astype(LOW)
+
+    bands(r.band, False)
+    bands(r.band_back, True)
+
+    def window(ext, b):
+        taken = ext[pl.ds(pl.multiple_of(b * BLOCK, BLOCK), SPAN), :]
+        start = b * BLOCK
+        left_out = (start == item_edge) | ((s == 0) & (start == 0))
+        right_out = (start + BLOCK == item_edge) | ((s == count - 1) & (start + BLOCK == rows))
+        row = iota((SPAN, taken.shape[1]), 0)
+        keep = jnp.where(
+            row < REACH,
+            jnp.where(left_out, 0.0, 1.0),
+            jnp.where(row >= REACH + BLOCK, jnp.where(right_out, 0.0, 1.0), 1.0),
+        )
+        return taken * keep.astype(LOW)
+
+    def convolve(band, taken):
+        return own_heads(matmul_low(band[...], jnp.concatenate([taken, taken], axis=0)), BLOCK, taken.shape[1])
+
+    gather_qk.forward()
+    load_inputs.wait()
+    gather_qk.finish()
+
+    def project_qk(c):
+        at = chunk_rows(c)
+        both = matmul_low(r.inputs[at], r.w_near[:, :, 0 : 2 * near].reshape(width, 2 * near))
+        r.queries[at] = (both[:, :near] + bias_query).astype(LOW)
+        r.keys[at] = both[:, near:].astype(LOW)
+
+    loop(CHUNKS, project_qk)
+    query_sums = across(r.member[...], r.queries[...])
+    key_sums = across(r.member[...], r.keys[...])
+    mid_scale = 1.0 / mid_count.astype(WIDE)
+    edge_scale = 1.0 / jnp.maximum(edge_count, 1).astype(WIDE)
+    border = jnp.concatenate([query_sums[0:BORDER], key_sums[0:BORDER]], axis=0) * mid_scale
+    r.land_part[s] = dense(border).astype(LOW)
+    landmarks.start()
+    gather_vo.forward()
+    gather_up1.start()
+    r.query_land[LAND:two] = (query_sums[LAND:two] * edge_scale).astype(LOW)
+    r.key_land[LAND:two] = (key_sums[LAND:two] * edge_scale).astype(LOW)
+
+    gather_vo.finish()
+
+    def project_v(c):
+        at = pl.ds(pl.multiple_of(REACH + c * size, REACH), size)
+        values = matmul_low(r.inputs[chunk_rows(c)], r.w_near[:, :, 2 * near : 2 * near + PAD].reshape(width, PAD))
+        values = values[:, :near] + bias_value
+        r.value_ext[at, 0:near] = values.astype(LOW)
+        r.value_ext[at, near:PAD] = jnp.zeros((size, PAD - near), LOW)
+
+    loop(CHUNKS, project_v)
+    for copy in rims[0]:
+        copy.start()
+    r.out_rows[...] = r.w_near[:, :, 3 * near :].reshape(width, near)
+
+    landmarks.finish()
+    lane = iota((LAND, count * BORDER), 1)
+    owner = lane // BORDER
+    starts = jnp.zeros((LAND, count * BORDER), jnp.int32)
+    for d in range(count):
+        starts = jnp.where(owner == d, jnp.maximum(d * rows - r.lengths[0], 0) // mid_count, starts)
+    put = (iota((LAND, count * BORDER), 0) == starts + lane - owner * BORDER).astype(LOW)
+    borders = [undense(r.land_part[d]) for d in range(count)]
+    r.query_land[0:LAND] = matmul_low(put, jnp.concatenate([b[0:BORDER] for b in borders], axis=0)).astype(LOW)
+    r.key_land[0:LAND] = matmul_low(put, jnp.concatenate([b[BORDER:] for b in borders], axis=0)).astype(LOW)
+    spread_heads(r.query_heads, r.query_land[...])
+    spread_heads(r.key_heads, r.key_land[...])
+
+    own_values = lambda: r.value_ext[pl.ds(REACH, rows), :]
+
+    def attend_b(g):
+        at = pl.ds(pl.multiple_of(g * LAND, LAND), LAND)
+        scores = against(r.query_heads[at], r.keys[...]) * scale
+        token = iota((LAND, rows), 1)
+        at_edge = jnp.where((token >= edge_start) & (token < edge_end), 1.0, 0.0)
+        member = jnp.where(lax.rem(g, 2) == 1, at_edge, 1.0 - at_edge)
+        scores = jnp.where(member > 0.5, scores, MASKED)
+        largest = jnp.max(scores, axis=1, keepdims=True)
+        weights = jnp.exp(scores - largest) * member
+        r.weights_b[at] = weights
+        r.weights_b_low[at] = weights.astype(LOW)
+        r.max_b[at] = largest
+        r.total_b[at] = jnp.sum(weights, axis=1, keepdims=True)
+
+    loop(2 * heads, attend_b)
+    numer = own_heads(matmul_low(r.weights_b_low[...], own_values()), two, PAD)
+    lane = iota((two, PAD), 1)
+    for k in range(heads):
+        numer = jnp.where(lane == near + k, r.total_b[k * two : (k + 1) * two], numer)
+        numer = jnp.where(lane == near + heads + k, r.max_b[k * two : (k + 1) * two], numer)
+    r.numer_out[...] = numer[0:LAND].reshape(count, LAND // count, PAD)
+    numer_swap.start()
+
+    def wide_heads(stats, base):
+        lane = iota(stats.shape, 1)
+        out = stats
+        for k in range(heads):
+            out = jnp.where(lane // HEAD_DIM == k, stats[:, base + k : base + k + 1], out)
+        return out
+
+    edge = numer[LAND:two]
+    edge_totals = wide_heads(edge, near)
+    edge_totals = jnp.where(edge_totals > 0.0, edge_totals, 1.0)
+    r.kernel_edge[...] = jnp.where(iota(edge.shape, 1) < near, edge / edge_totals, 0.0)
+
+    pairs = [(k, g) for k in range(heads) for g in range(2)]
+    identity = (iota((LAND, LAND), 0) == iota((LAND, LAND), 1)).astype(WIDE)
+    group = lambda g: slice(g * LAND, (g + 1) * LAND)
+
+    def first_inverse(k, g, i):
+        lands = r.query_heads[k * two + g * LAND : k * two + (g + 1) * LAND, :]
+        scores = against(lands, r.key_land[group(g), :]) * scale
+        weights = jnp.exp(scores - jnp.max(scores, axis=1, keepdims=True))
+        weights = weights / jnp.sum(weights, axis=1, keepdims=True)
+        r.land_kernel[i] = weights
+        return weights.T / jnp.sum(weights * weights)
+
+    def invert(it, inverses):
+        kernels = [r.land_kernel[i] for i in range(len(pairs))]
+        products = [exact(a, b) for a, b in zip(kernels, inverses)]
+        nested = [15.0 * identity - exact(p, 7.0 * identity - p) for p in products]
+        for i, p in enumerate(products):
+            r.history[it, 0, i] = inverses[i]
+            r.history[it, 1, i] = p
+            r.history[it, 2, i] = nested[i]
+        nested = [13.0 * identity - exact(p, n) for p, n in zip(products, nested)]
+        for i, n in enumerate(nested):
+            r.history[it, 3, i] = n
+        return tuple(0.25 * exact(a, n) for a, n in zip(inverses, nested))
+
+    inverses = tuple(first_inverse(k, g, i) for i, (k, g) in enumerate(pairs))
+    inverses = lax.fori_loop(0, PINV_STEPS // 2, invert, inverses)
+
+    gather_up1.forward()
+
+    numer_swap.finish()
+    parts = [r.numer_in[d] for d in range(count)]
+    largest = functools.reduce(jnp.maximum, [wide_heads(p, near + heads) for p in parts])
+    lane = iota(largest.shape, 1)
+    joined = jnp.zeros_like(largest)
+    totals = jnp.zeros_like(largest)
+    for p in parts:
+        weight = jnp.exp(wide_heads(p, near + heads) - largest)
+        joined = joined + jnp.where(lane < near, p * weight, 0.0)
+        totals = totals + jnp.where(lane < near, wide_heads(p, near) * weight, 0.0)
+    joined = jnp.where(lane < near, joined / jnp.where(lane < near, totals, 1.0), 0.0)
+    for k in range(heads):
+        joined = jnp.where(lane == near + k, totals[:, k * HEAD_DIM : k * HEAD_DIM + 1], joined)
+        joined = jnp.where(
+            lane == near + heads + k, largest[:, k * HEAD_DIM : k * HEAD_DIM + 1], joined
+        )
+    r.kernel_v[s] = joined
+    kernel_spread.start()
+    gather_up2.start()
+    inverses = lax.fori_loop(PINV_STEPS // 2, PINV_STEPS, invert, inverses)
+    for i, inverse in enumerate(inverses):
+        r.inverse[i] = inverse
+    gather_down1.start()
+
+    def attend_f(c):
+        at = pl.ds(pl.multiple_of(c * half, half), half)
+        scores = against(r.queries[at], r.key_heads[...]) * scale
+        token, lane = iota((half, two), 0) + c * half, iota((half, two), 1)
+        at_edge = (token >= edge_start) & (token < edge_end)
+        member = jnp.where(lane < LAND, jnp.where(at_edge, 0.0, 1.0), jnp.where(at_edge, 1.0, 0.0))
+        for k in range(heads):
+            own = jnp.where(member > 0.5, scores[:, k * two : (k + 1) * two], MASKED)
+            weights = jnp.exp(own - jnp.max(own, axis=1, keepdims=True))
+            r.weights_f[at, k * two : (k + 1) * two] = weights / jnp.sum(weights, axis=1, keepdims=True)
+
+    loop(rows // half, attend_f)
+    for copy in rims[0]:
+        copy.wait_recv()
+
+    def convolve_values(b):
+        r.conv[pl.ds(pl.multiple_of(b * BLOCK, BLOCK), BLOCK), :] = convolve(
+            r.band, window(r.value_ext, b)
+        )[:, :near]
+
+    loop(rows // BLOCK, convolve_values)
+    gather_up2.forward()
+    gather_down2.start()
+    kernel_spread.finish()
+    kernel_mid = r.kernel_v[...].reshape(LAND, PAD)
+    kernel_of = lambda g: kernel_mid if g == 0 else r.kernel_edge[...]
+    for g in range(2):
+        mixed = jnp.zeros((LAND, PAD), WIDE)
+        for i, (k, own) in enumerate(pairs):
+            if own == g:
+                mixed = mixed + exact(r.inverse[i], kernel_of(g)) * masks[k]
+        r.mixing[group(g), :] = mixed[:, :near].astype(LOW)
+    spread_heads(r.mixing_heads, r.mixing[...])
+
+    def project_out(c):
+        at = chunk_rows(c)
+        attended = matmul_low(r.weights_f[at].astype(LOW), r.mixing_heads[...])
+        r.mixed[at] = (attended + r.conv[at]).astype(LOW)
+        sums[0].offer(c, against(r.mixed[at], r.out_rows[...]).astype(LOW))
+
+    loop(CHUNKS, project_out)
+    loop(CHUNKS, sums[0].pair_up)
+    gather_down1.forward()
+    r.acc[...] = jnp.zeros_like(r.acc)
+    gather_up1.finish()
+    gather_up2.finish()
+    load_cotangent.wait()
+    pieces = lambda body: loop(half // step, lambda i: body(pl.multiple_of(i * step, step)))
+
+    def norm_first(c):
+        def piece(i):
+            at = pl.ds(pl.multiple_of(c * size + core * half + i, step), step)
+            kept = pl.ds(pl.multiple_of(c * half + i, step), step)
+            pre = r.inputs[at].astype(WIDE) + sums[0].total(c, pl.ds(i, step)) + bias_out
+            normed, inv = normalize(pre)
+            r.norm_one[kept] = normed
+            r.inv_one[kept] = inv
+            r.hidden[at] = (normed * gain_one + bias_one).astype(LOW)
+
+        sums[0].arrived(c)
+        pieces(piece)
+        share(0, r.hidden, c).start()
+
+    def lift(c):
+        share(0, r.hidden, c).wait_recv()
+        at = chunk_rows(c)
+        r.tmp[...] = matmul_low(r.hidden[at], r.full_up[...].reshape(width, feed))
+
+        def curve(i):
+            to = pl.ds(pl.multiple_of(c * size + i * step, step), step)
+            value, grade = gelu_and_slope(r.tmp[pl.ds(pl.multiple_of(i * step, step), step)] + bias_up)
+            r.active[to] = value.astype(LOW)
+            r.slope[to] = grade.astype(LOW)
+
+        loop(size // step, curve)
+
+    def lower(c):
+        at = chunk_rows(c)
+        sums[1].offer(c, against(r.active[at], r.full_down[...].reshape(width, feed)).astype(LOW))
+
+    def behind(c, total):
+        @pl.when(c > 0)
+        def _():
+            total.pair_up(c - 1)
+
+    def feed_forward(c):
+        norm_first(c)
+        behind(c, sums[1])
+        lift(c)
+
+        @pl.when(c == 0)
+        def _():
+            gather_down2.forward()
+            gather_down1.finish()
+            gather_down2.finish()
+
+        lower(c)
+
+    loop(CHUNKS, feed_forward)
+    sums[1].pair_up(CHUNKS - 1)
+
+    def feed_back(c):
+        def piece(i):
+            at = pl.ds(pl.multiple_of(c * size + core * half + i, step), step)
+            kept = pl.ds(pl.multiple_of(c * half + i, step), step)
+            pre = r.norm_one[kept] * gain_one + bias_one + sums[1].total(c, pl.ds(i, step)) + bias_down
+            normed, inv = normalize(pre)
+            r.output[at] = (normed * gain_two + bias_two).astype(LOW)
+            grad = r.cotangent[at].astype(WIDE)
+            back = norm_back(grad * gain_two, normed, inv)
+            r.wide_grad[kept] = back
+            r.grad_two[at] = back.astype(LOW)
+            r.acc[0] += fold(grad * normed)
+            r.acc[1] += fold(grad)
+            r.acc[2] += fold(back)
+
+        sums[1].arrived(c)
+        pieces(piece)
+        share(1, r.grad_two, c).start()
+        share(2, r.output, c).start()
+        behind(c, sums[2])
+        share(1, r.grad_two, c).wait_recv()
+        at = chunk_rows(c)
+        r.tmp[...] = matmul_low(r.grad_two[at], r.full_down[...].reshape(width, feed))
+
+        def curve(i):
+            to = pl.ds(pl.multiple_of(c * size + i * step, step), step)
+            value = r.tmp[pl.ds(pl.multiple_of(i * step, step), step)] * r.slope[to].astype(WIDE)
+            r.grad_lift[to] = value.astype(LOW)
+            r.acc[6] += fold(value)
+
+        loop(size // step, curve)
+        sums[2].offer(c, against(r.grad_lift[at], r.full_up[...].reshape(width, feed)).astype(LOW))
+
+    loop(CHUNKS, feed_back)
+    sums[2].pair_up(CHUNKS - 1)
+
+    scatter_down.fill(r.grad_two[...], r.active[...])
+    scatter_down.start()
+    scatter_up.fill(r.hidden[...], r.grad_lift[...])
+    r.mix_grad[...] = jnp.zeros_like(r.mix_grad)
+    r.kland_grad[...] = jnp.zeros_like(r.kland_grad)
+
+    def mix_back(c):
+        def piece(i):
+            at = pl.ds(pl.multiple_of(c * size + core * half + i, step), step)
+            kept = pl.ds(pl.multiple_of(c * half + i, step), step)
+            normed = r.norm_one[kept]
+            grad = r.wide_grad[kept] + sums[2].total(c, pl.ds(i, step))
+            back = norm_back(grad * gain_one, normed, r.inv_one[kept])
+            r.wide_grad[kept] = back
+            r.grad_one[at] = back.astype(LOW)
+            r.acc[3] += fold(grad * normed)
+            r.acc[4] += fold(grad)
+            r.acc[5] += fold(back)
+
+        sums[2].arrived(c)
+        pieces(piece)
+        share(3, r.grad_one, c).start()
+        share(3, r.grad_one, c).wait_recv()
+        at = chunk_rows(c)
+        grad = matmul_low(r.grad_one[at], r.out_rows[...]).astype(LOW)
+        r.grad_ext[pl.ds(pl.multiple_of(REACH + c * size, REACH), size)] = grad
+        weights = r.weights_f[at]
+        weighted = weights * against(grad, r.mixing_heads[...])
+        scores = []
+        for k in range(heads):
+            own = slice(k * two, (k + 1) * two)
+            scores.append(weighted[:, own] - weights[:, own] * jnp.sum(weighted[:, own], axis=1, keepdims=True))
+        scores = jnp.concatenate(scores, axis=1).astype(LOW)
+        r.grad_query[at] = matmul_low(scores, r.key_heads[...]) * scale
+        r.mix_grad[...] += across(weights.astype(LOW), grad)
+        r.kland_grad[...] += across(scores, r.queries[at])
+
+        @pl.when(c == 2)
+        def _():
+            scatter_down.forward(1, 2)
+
+    loop(CHUNKS, mix_back)
+    mix_grad = own_heads(r.mix_grad[...], two, near)
+    kland_grad = own_heads(r.kland_grad[...], two, near) * scale
+    r.mix_part[s] = dense(mix_grad[0:LAND]).astype(LOW)
+    r.kland_part[s] = dense(kland_grad[0:LAND]).astype(LOW)
+    mixing_spread.start()
+    for copy in rims[1]:
+        copy.start()
+    scatter_up.start(0, 2)
+    scatter_down.forward(2)
+
+    def settle_output(c):
+        share(2, r.output, c).wait_recv()
+
+    loop(CHUNKS, settle_output)
+    store_output.start()
+    for k in range(7):
+        r.vector_part[s, k : k + 1] = jnp.sum(r.acc[k], axis=0, keepdims=True)
+    r.vector_part[s, 7:8] = jnp.zeros((1, width), WIDE)
+    for copy in rims[1]:
+        copy.wait_recv()
+
+    r.tap_grad[...] = jnp.zeros_like(r.tap_grad)
+
+    def convolve_back(b):
+        at = pl.ds(pl.multiple_of(b * BLOCK, BLOCK), BLOCK)
+        r.conv[at] = convolve(r.band_back, window(r.grad_ext, b))
+        own = r.grad_ext[pl.ds(pl.multiple_of(b * BLOCK + REACH, REACH), BLOCK), :]
+        own = jnp.concatenate([own * m for m in masks_low], axis=0)
+        r.tap_grad[:, 0:SPAN] += against(own, window(r.value_ext, b)[:, :near])
+
+    loop(rows // BLOCK, convolve_back)
+    token = lax.rem(iota((heads * BLOCK, 128), 0), BLOCK)
+    slanted = r.tap_grad[...]
+    for bit in range(6):
+        moved = pltpu.roll(slanted, 128 - (1 << bit), 1)
+        slanted = jnp.where(lax.rem(token // (1 << bit), 2) == 1, moved, slanted)
+    for k in range(heads):
+        r.small_part[s, 2 + k : 3 + k, 0:128] = jnp.sum(
+            slanted[k * BLOCK : (k + 1) * BLOCK], axis=0, keepdims=True
+        )
+
+    mixing_spread.finish()
+    over_seq = lambda ref: undense(functools.reduce(jnp.add, [ref[d].astype(WIDE) for d in range(count)]))
+    mix_grads = [over_seq(r.mix_part), mix_grad[LAND:two]]
+    stats = r.kernel_v[...].reshape(LAND, PAD)
+    mid_totals = wide_heads(stats, near)[:, :near]
+    divisors = [mid_totals, edge_totals[:, :near]]
+    inverse_grads = []
+    for i, (k, g) in enumerate(pairs):
+        inverse_grads.append(
+            exact(mix_grads[g] * masks[k][:, :near], kernel_of(g)[:, :near], (1, 1))
+        )
+    shrink = [
+        jnp.exp(r.max_b[k * two : k * two + LAND] - stats[:, near + heads + k : near + heads + k + 1])
+        for k in range(heads)
+    ]
+    for g in range(2):
+        grad = jnp.zeros((LAND, near), WIDE)
+        for i, (k, own) in enumerate(pairs):
+            if own == g:
+                grad = grad + exact(r.inverse[i], mix_grads[g], (0, 0)) * masks[k][:, :near]
+        grad = grad / divisors[g]
+        lost = grad * kernel_of(g)[:, :near]
+        for k in range(heads):
+            at = slice(k * two + g * LAND, k * two + (g + 1) * LAND)
+            factor = shrink[k] if g == 0 else 1.0
+            r.numer_heads[at] = (grad * factor * masks[k][:, :near]).astype(LOW)
+            r.total_grad[at] = -jnp.sum(lost * masks[k][:, :near], axis=1, keepdims=True) * factor
+
+    def back_b(g):
+        at = pl.ds(pl.multiple_of(g * LAND, LAND), LAND)
+        grad = against(r.numer_heads[at], own_values()[:, :near]) + r.total_grad[at]
+        r.scores_b[at] = (r.weights_b[at] * grad).astype(LOW)
+
+    loop(2 * heads, back_b)
+    qland_grad = own_heads(matmul_low(r.scores_b[...], r.keys[...]), two, near) * scale
+    r.qland_part[s] = dense(qland_grad[0:LAND]).astype(LOW)
+    qland_spread.start()
+    kland_spread.start()
+    scatter_up.start(2)
+    vector_spread.start()
+    scatter_out.fill(r.grad_one[...], r.mixed[...])
+    scatter_out.start()
+
+    def keys_values(c):
+        at = chunk_rows(c)
+        r.grad_key[at] = across(r.scores_b[:, at], r.query_heads[...]) * scale
+        values = across(r.weights_b_low[:, at], r.numer_heads[...]) + r.conv[at]
+        r.near_grads[at, 2 * near : 3 * near] = values.astype(LOW)
+        return jnp.sum(values, axis=0, keepdims=True)
+
+    value_bias = lax.fori_loop(
+        0, CHUNKS, lambda c, total: total + keys_values(c), jnp.zeros((1, near), WIDE)
+    )
+
+    def invert_back(i, carry):
+        it = PINV_STEPS - 1 - i
+        grads, kernel_grads = carry
+        many = range(len(pairs))
+        held = [[r.history[it, part, p] for p in many] for part in range(4)]
+        befores, products, nested_two, nested_three = held
+        kernels = [r.land_kernel[p] for p in many]
+        grad_three = [0.25 * exact(a, b, (0, 0)) for a, b in zip(befores, grads)]
+        grad_two = [-exact(a, b, (0, 0)) for a, b in zip(products, grad_three)]
+        grad_one = [-exact(a, b, (0, 0)) for a, b in zip(products, grad_two)]
+        grad_product = [
+            -exact(a, b, (1, 1)) - exact(c, 7.0 * identity - d, (1, 1)) - e
+            for a, b, c, d, e in zip(grad_three, nested_two, grad_two, products, grad_one)
+        ]
+        kernel_grads = [k + exact(a, b, (1, 1)) for k, a, b in zip(kernel_grads, grad_product, befores)]
+        grads = [
+            0.25 * exact(a, b, (1, 1)) + exact(k, p, (0, 0))
+            for a, b, k, p in zip(grads, nested_three, kernels, grad_product)
+        ]
+        return tuple(grads), tuple(kernel_grads)
+
+    scatter_up.forward(1, 3)
+    zeros = tuple(jnp.zeros((LAND, LAND), WIDE) for _ in pairs)
+    grads, kernel_grads = lax.fori_loop(0, PINV_STEPS, invert_back, (tuple(inverse_grads), zeros))
+    qland_a = [jnp.zeros((LAND, near), WIDE)] * 2
+    kland_a = [jnp.zeros((LAND, near), WIDE)] * 2
+    for i, (k, g) in enumerate(pairs):
+        kernel = r.land_kernel[i]
+        turned = grads[i].T
+        squares = jnp.sum(kernel * kernel)
+        grad = kernel_grads[i] + turned / squares - kernel * (2.0 * jnp.sum(turned * kernel) / (squares * squares))
+        grad = kernel * (grad - jnp.sum(kernel * grad, axis=1, keepdims=True)) * scale
+        mask = masks[k][:, :near]
+        qland_a[g] = qland_a[g] + exact(grad, r.key_land[group(g)].astype(WIDE)) * mask
+        kland_a[g] = kland_a[g] + exact(grad, r.query_land[group(g)].astype(WIDE), (0, 0)) * mask
+
+    scatter_up.forward(3)
+
+    kland_spread.finish()
+    qland_spread.finish()
+    pick = (iota((LAND, LAND), 1) == iota((LAND, LAND), 0) + first_slot).astype(WIDE)
+
+    def slot_grads(mid, edge):
+        mid = exact(pick, mid * mid_scale)
+        both = jnp.concatenate([mid, edge * edge_scale], axis=0)
+        high = both.astype(LOW)
+        return jnp.concatenate([high, (both - high.astype(WIDE)).astype(LOW)], axis=0)
+
+    r.slot_q[...] = slot_grads(qland_a[0] + over_seq(r.qland_part), qland_a[1] + qland_grad[LAND:two])
+    r.slot_k[...] = slot_grads(kland_a[0] + over_seq(r.kland_part), kland_a[1] + kland_grad[LAND:two])
+
+    def input_back(c):
+        at = chunk_rows(c)
+        member = jnp.concatenate([r.member[at]] * 2, axis=1)
+        queries = r.grad_query[at] + matmul_low(member, r.slot_q[...])
+        keys = r.grad_key[at] + matmul_low(member, r.slot_k[...])
+        r.near_grads[at, 0:near] = queries.astype(LOW)
+        r.near_grads[at, near : 2 * near] = keys.astype(LOW)
+        terms = against(r.near_grads[at], r.w_near[:, :, 0 : 3 * near].reshape(width, 3 * near))
+        sums[3].offer(c, terms.astype(LOW))
+        sums[3].pair_up(c)
+        return jnp.sum(queries, axis=0, keepdims=True)
+
+    query_bias = lax.fori_loop(
+        0, CHUNKS, lambda c, total: total + input_back(c), jnp.zeros((1, near), WIDE)
+    )
+    r.small_part[s, 0:1, 0:near] = query_bias
+    r.small_part[s, 1:2, 0:near] = value_bias
+    small_spread.start()
+    scatter_qkv.fill(r.inputs[...], r.near_grads[...])
+    scatter_qkv.start()
+    scatter_out.forward()
+    vector_spread.finish()
+    r.vector_sum[0] = functools.reduce(jnp.add, [r.vector_part[d] for d in range(count)])
+    vector_core.start()
+    r.grad_w_down[...] = scatter_down.finish()
+    store_down.start()
+    r.grad_w_up[...] = scatter_up.finish()
+    store_up.start()
+    r.grad_w_out[...] = scatter_out.finish()
+    store_out.start()
+    scatter_qkv.forward()
+
+    def inputs_done(c):
+        def piece(i):
+            at = pl.ds(pl.multiple_of(c * size + core * half + i, step), step)
+            kept = pl.ds(pl.multiple_of(c * half + i, step), step)
+            r.grad_inputs[at] = (r.wide_grad[kept] + sums[3].total(c, pl.ds(i, step))).astype(LOW)
+
+        sums[3].arrived(c)
+        pieces(piece)
+        share(4, r.grad_inputs, c).start()
+
+    loop(CHUNKS, inputs_done)
+    near_total = scatter_qkv.finish()
+    for k in range(3):
+        r.grad_near[k] = near_total[:, k * near : (k + 1) * near]
+    store_near.start()
+    vector_core.wait_recv()
+    r.vectors[0:6] = r.vector_sum[0, 0:6] + r.vector_sum[1, 0:6]
+    r.vectors[6:8] = r.vector_sum[0, 6:8]
+    small_spread.finish()
+    r.smalls[...] = functools.reduce(jnp.add, [r.small_part[d] for d in range(count)])
+
+    def settle_inputs(c):
+        share(4, r.grad_inputs, c).wait_recv()
+
+    loop(CHUNKS, settle_inputs)
+    store_grad_inputs.start()
+
+    def settle(c):
+        sums[3].core_copy(c).wait_send()
+        sums[3].x_copy(c).wait_send()
+        for k, ref in enumerate((r.hidden, r.grad_two, r.output, r.grad_one, r.grad_inputs)):
+            share(k, ref, c).wait_send()
+
+    loop(CHUNKS, settle)
+    vector_core.wait_send()
+    for copy in stores:
+        copy.wait()
+    for copy in rims[0] + rims[1]:
+        copy.wait_send()
+    for group_of in gathers + scatters + spreads:
+        group_of.close()
+
+
+def hand_out(
+    output, grad_inputs, grad_out, grad_up, grad_down, grad_near, vectors, smalls,
+    to_output, to_inputs, to_query, to_key, to_value, to_out, to_up, to_down,
+    bias_query, bias_value, bias_out, bias_up, bias_down, gain_one, bias_one, gain_two, bias_two, taps, sems,
+):
+    rows = output.shape[0] // 4
+    copies = []
+    for k, (ref, to) in enumerate(((output, to_output), (grad_inputs, to_inputs))):
+        for j in range(4):
+            at = pl.ds(j * rows, rows)
+            copies.append(pltpu.make_async_copy(ref.at[at], to.at[at], sems.at[k, j]))
+    for k, (ref, to) in enumerate(
+        (
+            (grad_near.at[0], to_query), (grad_near.at[1], to_key), (grad_near.at[2], to_value),
+            (grad_out, to_out), (grad_up, to_up), (grad_down, to_down),
+        )
+    ):
+        copies.append(pltpu.make_async_copy(ref, to, sems.at[2 + k, 0]))
+    for copy in copies:
+        copy.start()
+    for k, ref in enumerate((gain_two, bias_two, bias_down, gain_one, bias_one, bias_out, bias_up)):
+        ref[...] = vectors[k : k + 1].reshape(ref.shape)
+    for k, ref in enumerate((bias_query, bias_value)):
+        ref[...] = smalls[k : k + 1, 0 : ref.shape[0]].reshape(ref.shape)
+    taps[...] = smalls[2 : 2 + taps.shape[0], 0:KERNEL]
+    for copy in copies:
+        copy.wait()
+
+
+def fused_body(
+    inputs, cotangent, item_lengths, w_query, w_key, w_value, w_out, w_up, w_down, bias_query, bias_value,
+    bias_out, bias_up, bias_down, gain_one, bias_one, gain_two, bias_two, conv_taps,
+):
+    count = lax.axis_size("seq")
+    rows, width = inputs.shape
+    near, feed, heads = w_query.shape[1], w_up.shape[1], conv_taps.shape[0]
+    size, part, lines = rows // CHUNKS, width // count, count // 2
+    half, two = size // 2, 2 * LAND
+    low = lambda *shape: pltpu.VMEM(shape, LOW)
+    wide = lambda *shape: pltpu.VMEM(shape, WIDE)
+    sem = lambda *shape: pltpu.SemaphoreType.DMA(shape)
+    vmem, smem = pl.BlockSpec(memory_space=pltpu.VMEM), pl.BlockSpec(memory_space=pltpu.SMEM)
+    operands = dict(
+        lengths=item_lengths, conv_taps=conv_taps,
+        inputs_hbm=inputs, cotangent_hbm=cotangent,
+        w_query=w_query, w_key=w_key, w_value=w_value, w_out=w_out, w_up=w_up, w_down=w_down,
+        bias_query=bias_query, bias_value=bias_value,
+        bias_out=bias_out, bias_up=bias_up, bias_down=bias_down,
+        gain_one=gain_one, bias_one=bias_one, gain_two=gain_two, bias_two=bias_two,
+    )
+    outs = dict(
+        output_hbm=((rows, width), LOW), grad_inputs_hbm=((rows, width), LOW),
+        grad_w_out_hbm=((part, near), WIDE), grad_w_up_hbm=((part, feed), WIDE), grad_w_down_hbm=((part, feed), WIDE),
+        grad_near_hbm=((3, part, near), WIDE), vectors=((8, width), WIDE), smalls=((8, PAD), WIDE),
+    )
+    scratch = dict(
+        inputs=low(rows, width), cotangent=low(rows, width), output=low(rows, width), grad_inputs=low(rows, width),
+        grad_w_out=wide(part, near), grad_w_up=wide(part, feed), grad_w_down=wide(part, feed),
+        grad_near=wide(3, part, near), io=sem(8),
+        packed=low(part, 4 * near), w_near=low(count, part, 4 * near), out_rows=low(width, near),
+        full_up=low(count, part, feed), full_down=low(count, part, feed),
+        member=low(rows, two), band=low(heads * BLOCK, 2 * SPAN), band_back=low(heads * BLOCK, 2 * SPAN),
+        queries=low(rows, near), keys=low(rows, near), value_ext=low(rows + 2 * REACH, PAD),
+        land_part=low(count, 3 * BORDER, 128), query_land=low(two, near), key_land=low(two, near),
+        query_heads=low(heads * two, near), key_heads=low(heads * two, near),
+        weights_b=wide(heads * two, rows), weights_b_low=low(heads * two, rows),
+        max_b=wide(heads * two, 1), total_b=wide(heads * two, 1),
+        numer_out=wide(count, LAND // count, PAD), numer_in=wide(count, LAND // count, PAD),
+        kernel_v=wide(count, LAND // count, PAD), kernel_edge=wide(LAND, PAD),
+        land_kernel=wide(2 * heads, LAND, LAND), inverse=wide(2 * heads, LAND, LAND),
+        history=wide(PINV_STEPS, 4, 2 * heads, LAND, LAND),
+        weights_f=wide(rows, heads * two), conv=wide(rows, near),
+        mixing=low(two, near), mixing_heads=low(heads * two, near), mixed=low(rows, near),
+        terms=low(CHUNKS, size, width), core_in=low(CHUNKS, half, width),
+        x_out=low(CHUNKS, half, width), x_in=low(2, CHUNKS, half, width),
+        hidden=low(rows, width), active=low(rows, feed), slope=low(rows, feed),
+        grad_two=low(rows, width), grad_lift=low(rows, feed), grad_one=low(rows, width),
+        norm_one=wide(rows // 2, width), inv_one=wide(rows // 2, 1), wide_grad=wide(rows // 2, width),
+        tmp=wide(size, feed), acc=wide(7, 8, width),
+        grad_ext=low(rows + 2 * REACH, near), grad_query=wide(rows, near), grad_key=wide(rows, near),
+        mix_grad=wide(heads * two, near), kland_grad=wide(heads * two, near),
+        mix_part=low(count, 3 * LAND // 2, 128), kland_part=low(count, 3 * LAND // 2, 128),
+        qland_part=low(count, 3 * LAND // 2, 128),
+        tap_grad=wide(heads * BLOCK, 128), numer_heads=low(heads * two, near), total_grad=wide(heads * two, 1),
+        scores_b=low(heads * two, rows), near_grads=low(rows, 3 * near),
+        slot_q=low(2 * two, near), slot_k=low(2 * two, near),
+        vector_part=wide(count, 8, width), vector_sum=wide(2, 8, width), small_part=wide(count, 8, PAD),
+    )
+    scatter = lambda lanes: (
+        low(count, part, lanes), low(lines, part, lanes), low(lines - 1, part, lanes), low(lines - 1, part, lanes)
+    )
+    for_out, for_up, for_down, for_qkv = (scatter(lanes) for lanes in (near, feed, feed, 3 * near))
+    scratch.update(
+        t_out=for_out[0], yb_out=for_out[1], pr_out=for_out[2], zb_out=for_out[3],
+        t_up=for_up[0], yb_up=for_up[1], pr_up=for_up[2], zb_up=for_up[3],
+        t_down=for_down[0], yb_down=for_down[1], pr_down=for_down[2], zb_down=for_down[3],
+        t_qkv=for_qkv[0], yb_qkv=for_qkv[1], pr_qkv=for_qkv[2], zb_qkv=for_qkv[3],
+        g_own=sem(6), g_zs=sem(6, lines - 1), g_zr=sem(6, lines - 1), g_ys=sem(6, lines), g_yr=sem(6, lines),
+        s_ys=sem(4, lines), s_yr=sem(4, lines), s_zs=sem(4, lines - 1), s_zr=sem(4, lines - 1),
+        e_s=sem(8, count - 1), e_r=sem(8, count - 1), h_sems=sem(4, 4, CHUNKS),
+        rim_s=sem(2, 2), rim_r=sem(2, 2), share_s=sem(5, CHUNKS), share_r=sem(5, CHUNKS),
+        core_s=sem(1), core_r=sem(1),
+    )
+    any_place = pl.BlockSpec(memory_space=pltpu.HBM)
+    results = pl.pallas_call(
+        functools.partial(layer_kernel, count, list(operands) + list(outs) + list(scratch)),
+        out_shape=tuple(jax.ShapeDtypeStruct(*out) for out in outs.values()),
+        in_specs=[smem, smem, any_place, any_place] + [vmem] * (len(operands) - 4),
+        out_specs=(any_place,) * 6 + (vmem, vmem),
+        scratch_shapes=list(scratch.values()),
+        compiler_params=pltpu.CompilerParams(
+            collective_id=1, has_side_effects=True, vmem_limit_bytes=63 * 2**20
+        ),
+    )(*operands.values())
+    vector = lambda length: jax.ShapeDtypeStruct((length,), WIDE)
+    block = lambda lanes: jax.ShapeDtypeStruct((part, lanes), WIDE)
+    whole = jax.ShapeDtypeStruct((rows, width), LOW)
+    return pl.pallas_call(
+        hand_out,
+        out_shape=(
+            whole, whole, block(near), block(near), block(near), block(near), block(feed), block(feed),
+            vector(near), vector(near), vector(width), vector(feed), vector(width),
+            vector(width), vector(width), vector(width), vector(width),
+            jax.ShapeDtypeStruct((heads, KERNEL), WIDE),
+        ),
+        in_specs=[vmem] * 8,
+        out_specs=(any_place,) * 8 + (vmem,) * 10,
+        scratch_shapes=[sem(8, 4)],
+    )(*results)
+
+
+def plain_body(
     inputs,
     cotangent,
     item_lengths,
@@ -422,8 +1537,9 @@
 
 
 def solution(mesh):
+    aligned = (768 // mesh.shape["seq"]) % 16 == 0
     return jax.shard_map(
-        body,
+        fused_body if aligned else plain_body,
         mesh=mesh,
         in_specs=(
             P("seq", None),

time: 909 us -> 190 us (0.21)
  waiting for transfers between devices: 358 us -> 0 us
  blocking collectives: 241 us -> 0 us
  Pallas kernels: 0 us -> 188 us
  matrix products: 131 us -> 0 us
  other arithmetic: 80.5 us -> 0 us
  local copies, waits for them, and re-layouts: 55.6 us -> 0 us
  starting transfers between devices: 17.7 us -> 0 us
  between operations: 18.5 us -> 0.83 us
    psum x8 -> x0, waiting for transfers between devices: 280 us -> none  [the longest x1 60.1 us: body(): lax.psum((grad_mix_part, grad_kland_part), 'seq')]
    pallas_call x0 -> x2, Pallas kernels: none -> 188 us  [the longest x1 183 us: fused_body(): pl.pallas_call(functools.partial(layer_kernel, count, list(operands) + li...]
    dot_general x111 -> x0, matrix products: 128 us -> none  [the longest x6 15.2 us: matmul_low(): return jnp.dot(left, right, preferred_element_type=jnp.float32)]
    all_gather x4 -> x0, blocking collectives: 127 us -> none  [the longest x1 33 us: body(): lax.all_gather(w_query, 'seq', axis=0, tiled=True)]
    psum x2 -> x0, blocking collectives: 92.3 us -> none  [the longest x1 75 us: body(): lax.psum((grad_qland_part, grad_gain_one, grad_bias_one, grad_gain_two, g...]
    all_gather x2 -> x0, waiting for transfers between devices: 76.5 us -> none  [the longest x1 39.5 us: body(): lax.all_gather(w_up, 'seq', axis=0, tiled=True)]
    reduce_sum x54 -> x0, other arithmetic: 37.7 us -> none  [the longest x38 14 us: body(): jnp.sum((grad_mixed_wide * neighbour).reshape(tok_rows, heads_here, HEAD_...]
    pmax x1 -> x0, blocking collectives: 22.4 us -> none  [body(): maxima_b = lax.pmax(jnp.max(scores_b, axis=2), 'seq')]
  transfers between devices with their start and end apart: 15 -> 0, of which waited for: 8 -> 0; matrix products, arithmetic and copies ran while one was open for 19% -> 0% of each run, Pallas kernels for 0% -> 0%
where the time goes in v2:
time: 190 us; the launch traced here: 189 us
  Pallas kernels  188 us (99%)
    pallas_call x1, Pallas kernels, fused_body(): pl.pallas_call(functools.partial(layer_kernel, count, list(operands) + li...  183 us
    pallas_call x1, Pallas kernels, fused_body(): pl.pallas_call(hand_out, out_shape=(whole, whole, block(near), block(near...  5.05 us

profile of v2, /device:TPU:0, one launch (start us, length us, event | category | flops | bytes accessed | tf_op | source)
XLA Modules:
  0.0 188.8 jit_solution(1124209636333312346)
XLA Ops:
  0.7 182.9 %shard_map.322 = (bf16[1024,768]{1,0:T(8,128)(2,1)}, bf16[1024,768]{1,0:T(8,128)(2,1)}, f32[96,192]{1,0:T(8,128)}, f32[96,768]{1,0:T(8,128)}, f32[96,768]{1,0:T(...) custom-call(s32[3]{0:T(128)} %refs_0_.1, f32[3,33]{1,0:T(4,128)} %refs_1_.1, ...), custom_call_target="tpu_custom_call" | custom-call | tf_op jit(solution)/shard_map/pallas_call | solution.py:1207
  183.6 5.0 %shard_map.323 = (bf16[1024,768]{1,0:T(8,128)(2,1)}, bf16[1024,768]{1,0:T(8,128)(2,1)}, f32[96,192]{1,0:T(8,128)}, f32[96,192]{1,0:T(8,128)}, f32[96,192]{1,0:T(...) custom-call(bf16[1024,768]{1,0:T(8,128)(2,1)} %get-tuple-element.26., ...), custom_call_target="tpu_custom_call" | custom-call | tf_op jit(solution)/shard_map/pallas_call | solution.py:1220

commit v3 on v2

--- a/solution.py
+++ b/solution.py
@@ -238,6 +238,15 @@
     def fill(self, left, right):
         self.terms[...] = across(left, right).astype(LOW).reshape(self.terms.shape)
 
+    def fill_dense(self, left, right):
+        terms = across(left, right).astype(LOW)
+        part = terms.shape[0] // self.terms.shape[0]
+        terms = terms.reshape(self.terms.shape[0], part, terms.shape[1])
+        self.terms[:, 0:part] = terms[:, :, 0:128]
+        self.terms[:, part:] = jnp.concatenate(
+            [terms[:, 0 : part // 2, 128:], terms[:, part // 2 :, 128:]], axis=2
+        )
+
     def start(self, first=0, last=None):
         order = list(range(1, self.lines)) + [0]
         for j in order[first:last]:
@@ -424,16 +433,17 @@
 
     gather_qk = gather(0, r.packed, r.w_near, 0, 2 * near)
     gather_vo = gather(1, r.packed, r.w_near, 2 * near, 4 * near)
-    gather_up1 = gather(2, r.w_up, r.full_up, 0, feed // 2)
-    gather_up2 = gather(3, r.w_up, r.full_up, feed // 2, feed)
-    gather_down1 = gather(4, r.w_down, r.full_down, 0, feed // 2)
-    gather_down2 = gather(5, r.w_down, r.full_down, feed // 2, feed)
-    gathers = [gather_qk, gather_vo, gather_up1, gather_up2, gather_down1, gather_down2]
+    third = feed // 3
+    ups = [gather(2 + k, r.w_up, r.full_up, k * third, (k + 1) * third) for k in range(3)]
+    downs = [gather(5 + k, r.w_down, r.full_down, k * third, (k + 1) * third) for k in range(3)]
+    gathers = [gather_qk, gather_vo] + ups + downs
     scatter_out = scatter(0, r.t_out, r.yb_out, r.pr_out, r.zb_out)
     scatter_up = scatter(1, r.t_up, r.yb_up, r.pr_up, r.zb_up)
     scatter_down = scatter(2, r.t_down, r.yb_down, r.pr_down, r.zb_down)
-    scatter_qkv = scatter(3, r.t_qkv, r.yb_qkv, r.pr_qkv, r.zb_qkv)
-    scatters = [scatter_out, scatter_up, scatter_down, scatter_qkv]
+    scatter_qk = scatter(3, r.t_qk, r.yb_qk, r.pr_qk, r.zb_qk)
+    scatter_v = scatter(4, r.t_v, r.yb_v, r.pr_v, r.zb_v)
+    scatters = [scatter_out, scatter_up, scatter_down, scatter_qk, scatter_v]
+    correction = HeadSum(0, r.corr_terms, r.corr_core, r.corr_out, r.corr_in, r.corr_sems)
     sums = [HeadSum(k, r.terms, r.core_in, r.x_out, r.x_in, r.h_sems) for k in range(4)]
     landmarks = Spread(count, r.land_part, r.e_s.at[0], r.e_r.at[0])
     numer_swap = Swap(count, r.numer_out, r.numer_in, r.e_s.at[1], r.e_r.at[1])
@@ -470,7 +480,7 @@
         for k, (ref, out) in enumerate(
             (
                 (r.output, r.output_hbm),
-                (r.grad_inputs, r.grad_inputs_hbm),
+                (r.cotangent, r.grad_inputs_hbm),
                 (r.grad_w_out, r.grad_w_out_hbm),
                 (r.grad_w_up, r.grad_w_up_hbm),
                 (r.grad_w_down, r.grad_w_down_hbm),
@@ -560,6 +570,7 @@
         return own_heads(matmul_low(band[...], jnp.concatenate([taken, taken], axis=0)), BLOCK, taken.shape[1])
 
     gather_qk.forward()
+    gather_vo.forward()
     load_inputs.wait()
     gather_qk.finish()
 
@@ -577,8 +588,8 @@
     border = jnp.concatenate([query_sums[0:BORDER], key_sums[0:BORDER]], axis=0) * mid_scale
     r.land_part[s] = dense(border).astype(LOW)
     landmarks.start()
-    gather_vo.forward()
-    gather_up1.start()
+    ups[0].start()
+    ups[1].start()
     r.query_land[LAND:two] = (query_sums[LAND:two] * edge_scale).astype(LOW)
     r.key_land[LAND:two] = (key_sums[LAND:two] * edge_scale).astype(LOW)
 
@@ -595,6 +606,14 @@
     for copy in rims[0]:
         copy.start()
     r.out_rows[...] = r.w_near[:, :, 3 * near :].reshape(width, near)
+
+    def convolve_values(b):
+        r.conv[pl.ds(pl.multiple_of(b * BLOCK, BLOCK), BLOCK), :] = convolve(
+            r.band, window(r.value_ext, b)
+        )[:, :near]
+
+    blocks = rows // BLOCK
+    loop(blocks - 2, lambda b: convolve_values(b + 1))
 
     landmarks.finish()
     lane = iota((LAND, count * BORDER), 1)
@@ -611,13 +630,16 @@
 
     own_values = lambda: r.value_ext[pl.ds(REACH, rows), :]
 
+    def score_b(c):
+        at = chunk_rows(c)
+        r.weights_b[:, at] = against(r.query_heads[...], r.keys[at]) * scale
+
     def attend_b(g):
         at = pl.ds(pl.multiple_of(g * LAND, LAND), LAND)
-        scores = against(r.query_heads[at], r.keys[...]) * scale
         token = iota((LAND, rows), 1)
         at_edge = jnp.where((token >= edge_start) & (token < edge_end), 1.0, 0.0)
         member = jnp.where(lax.rem(g, 2) == 1, at_edge, 1.0 - at_edge)
-        scores = jnp.where(member > 0.5, scores, MASKED)
+        scores = jnp.where(member > 0.5, r.weights_b[at], MASKED)
         largest = jnp.max(scores, axis=1, keepdims=True)
         weights = jnp.exp(scores - largest) * member
         r.weights_b[at] = weights
@@ -625,6 +647,7 @@
         r.max_b[at] = largest
         r.total_b[at] = jnp.sum(weights, axis=1, keepdims=True)
 
+    loop(CHUNKS, score_b)
     loop(2 * heads, attend_b)
     numer = own_heads(matmul_low(r.weights_b_low[...], own_values()), two, PAD)
     lane = iota((two, PAD), 1)
@@ -633,6 +656,10 @@
         numer = jnp.where(lane == near + heads + k, r.max_b[k * two : (k + 1) * two], numer)
     r.numer_out[...] = numer[0:LAND].reshape(count, LAND // count, PAD)
     numer_swap.start()
+    ups[2].start()
+    for copy in rims[0]:
+        copy.wait_recv()
+    loop(2, lambda b: convolve_values(b * (blocks - 1)))
 
     def wide_heads(stats, base):
         lane = iota(stats.shape, 1)
@@ -661,20 +688,18 @@
     def invert(it, inverses):
         kernels = [r.land_kernel[i] for i in range(len(pairs))]
         products = [exact(a, b) for a, b in zip(kernels, inverses)]
+        for i, (a, p) in enumerate(zip(inverses, products)):
+            r.befores[it, i] = a
+            r.products[it, i] = p
         nested = [15.0 * identity - exact(p, 7.0 * identity - p) for p in products]
-        for i, p in enumerate(products):
-            r.history[it, 0, i] = inverses[i]
-            r.history[it, 1, i] = p
-            r.history[it, 2, i] = nested[i]
         nested = [13.0 * identity - exact(p, n) for p, n in zip(products, nested)]
-        for i, n in enumerate(nested):
-            r.history[it, 3, i] = n
         return tuple(0.25 * exact(a, n) for a, n in zip(inverses, nested))
 
     inverses = tuple(first_inverse(k, g, i) for i, (k, g) in enumerate(pairs))
     inverses = lax.fori_loop(0, PINV_STEPS // 2, invert, inverses)
 
-    gather_up1.forward()
+    ups[0].forward()
+    ups[1].forward()
 
     numer_swap.finish()
     parts = [r.numer_in[d] for d in range(count)]
@@ -694,11 +719,11 @@
         )
     r.kernel_v[s] = joined
     kernel_spread.start()
-    gather_up2.start()
+    for piece in downs:
+        piece.start()
     inverses = lax.fori_loop(PINV_STEPS // 2, PINV_STEPS, invert, inverses)
     for i, inverse in enumerate(inverses):
         r.inverse[i] = inverse
-    gather_down1.start()
 
     def attend_f(c):
         at = pl.ds(pl.multiple_of(c * half, half), half)
@@ -712,17 +737,6 @@
             r.weights_f[at, k * two : (k + 1) * two] = weights / jnp.sum(weights, axis=1, keepdims=True)
 
     loop(rows // half, attend_f)
-    for copy in rims[0]:
-        copy.wait_recv()
-
-    def convolve_values(b):
-        r.conv[pl.ds(pl.multiple_of(b * BLOCK, BLOCK), BLOCK), :] = convolve(
-            r.band, window(r.value_ext, b)
-        )[:, :near]
-
-    loop(rows // BLOCK, convolve_values)
-    gather_up2.forward()
-    gather_down2.start()
     kernel_spread.finish()
     kernel_mid = r.kernel_v[...].reshape(LAND, PAD)
     kernel_of = lambda g: kernel_mid if g == 0 else r.kernel_edge[...]
@@ -733,6 +747,7 @@
                 mixed = mixed + exact(r.inverse[i], kernel_of(g)) * masks[k]
         r.mixing[group(g), :] = mixed[:, :near].astype(LOW)
     spread_heads(r.mixing_heads, r.mixing[...])
+    ups[2].forward()
 
     def project_out(c):
         at = chunk_rows(c)
@@ -742,10 +757,31 @@
 
     loop(CHUNKS, project_out)
     loop(CHUNKS, sums[0].pair_up)
-    gather_down1.forward()
+    downs[0].forward()
+
+    def prepare(it):
+        many = range(len(pairs))
+        befores = [r.befores[it, i] for i in many]
+        products = [r.products[it, i] for i in many]
+        squares = [exact(p, p) for p in products]
+        firsts = [exact(a, p) for a, p in zip(befores, products)]
+        cubes = [exact(p, q) for p, q in zip(products, squares)]
+        seconds = [exact(t, p) for t, p in zip(firsts, products)]
+        for i in many:
+            p, q, c = products[i].T, squares[i].T, cubes[i].T
+            r.uppers[it, i, :, 0:LAND] = 3.25 * identity - 3.75 * p + 1.75 * q - 0.25 * c
+            r.uppers[it, i, :, LAND:two] = 1.75 * p - 3.75 * identity - 0.25 * q
+            r.uppers[it, i, :, two:] = 1.75 * identity - 0.25 * p
+            r.lowers[it, i, :, 0:LAND] = befores[i].T
+            r.lowers[it, i, :, LAND:two] = firsts[i].T
+            r.lowers[it, i, :, two:] = -0.25 * seconds[i].T
+
+    loop(PINV_STEPS, prepare)
+    for i in range(len(pairs)):
+        r.turned_kernel[i] = r.land_kernel[i].T
     r.acc[...] = jnp.zeros_like(r.acc)
-    gather_up1.finish()
-    gather_up2.finish()
+    for piece in ups:
+        piece.finish()
     load_cotangent.wait()
     pieces = lambda body: loop(half // step, lambda i: body(pl.multiple_of(i * step, step)))
 
@@ -792,9 +828,10 @@
 
         @pl.when(c == 0)
         def _():
-            gather_down2.forward()
-            gather_down1.finish()
-            gather_down2.finish()
+            for piece in downs[1:]:
+                piece.forward()
+            for piece in downs:
+                piece.finish()
 
         lower(c)
 
@@ -839,7 +876,6 @@
 
     scatter_down.fill(r.grad_two[...], r.active[...])
     scatter_down.start()
-    scatter_up.fill(r.hidden[...], r.grad_lift[...])
     r.mix_grad[...] = jnp.zeros_like(r.mix_grad)
     r.kland_grad[...] = jnp.zeros_like(r.kland_grad)
 
@@ -874,6 +910,10 @@
         r.mix_grad[...] += across(weights.astype(LOW), grad)
         r.kland_grad[...] += across(scores, r.queries[at])
 
+        @pl.when(c == 1)
+        def _():
+            scatter_up.fill(r.hidden[...], r.grad_lift[...])
+
         @pl.when(c == 2)
         def _():
             scatter_down.forward(1, 2)
@@ -886,39 +926,19 @@
     mixing_spread.start()
     for copy in rims[1]:
         copy.start()
-    scatter_up.start(0, 2)
-    scatter_down.forward(2)
-
-    def settle_output(c):
-        share(2, r.output, c).wait_recv()
-
-    loop(CHUNKS, settle_output)
-    store_output.start()
-    for k in range(7):
-        r.vector_part[s, k : k + 1] = jnp.sum(r.acc[k], axis=0, keepdims=True)
-    r.vector_part[s, 7:8] = jnp.zeros((1, width), WIDE)
-    for copy in rims[1]:
-        copy.wait_recv()
-
-    r.tap_grad[...] = jnp.zeros_like(r.tap_grad)
 
     def convolve_back(b):
         at = pl.ds(pl.multiple_of(b * BLOCK, BLOCK), BLOCK)
         r.conv[at] = convolve(r.band_back, window(r.grad_ext, b))
-        own = r.grad_ext[pl.ds(pl.multiple_of(b * BLOCK + REACH, REACH), BLOCK), :]
-        own = jnp.concatenate([own * m for m in masks_low], axis=0)
-        r.tap_grad[:, 0:SPAN] += against(own, window(r.value_ext, b)[:, :near])
-
-    loop(rows // BLOCK, convolve_back)
-    token = lax.rem(iota((heads * BLOCK, 128), 0), BLOCK)
-    slanted = r.tap_grad[...]
-    for bit in range(6):
-        moved = pltpu.roll(slanted, 128 - (1 << bit), 1)
-        slanted = jnp.where(lax.rem(token // (1 << bit), 2) == 1, moved, slanted)
-    for k in range(heads):
-        r.small_part[s, 2 + k : 3 + k, 0:128] = jnp.sum(
-            slanted[k * BLOCK : (k + 1) * BLOCK], axis=0, keepdims=True
-        )
+
+    scatter_out.fill_dense(r.grad_one[...], r.mixed[...])
+    scatter_out.start()
+    scatter_up.start(0, 1)
+    loop(blocks - 2, lambda b: convolve_back(b + 1))
+    for copy in rims[1]:
+        copy.wait_recv()
+    loop(2, lambda b: convolve_back(b * (blocks - 1)))
+    scatter_down.forward(2)
 
     mixing_spread.finish()
     over_seq = lambda ref: undense(functools.reduce(jnp.add, [ref[d].astype(WIDE) for d in range(count)]))
@@ -948,54 +968,56 @@
             r.numer_heads[at] = (grad * factor * masks[k][:, :near]).astype(LOW)
             r.total_grad[at] = -jnp.sum(lost * masks[k][:, :near], axis=1, keepdims=True) * factor
 
-    def back_b(g):
-        at = pl.ds(pl.multiple_of(g * LAND, LAND), LAND)
-        grad = against(r.numer_heads[at], own_values()[:, :near]) + r.total_grad[at]
-        r.scores_b[at] = (r.weights_b[at] * grad).astype(LOW)
-
-    loop(2 * heads, back_b)
+    def back_b(c):
+        at = chunk_rows(c)
+        values = r.value_ext[pl.ds(pl.multiple_of(REACH + c * size, REACH), size), 0:near]
+        grad = against(r.numer_heads[...], values) + r.total_grad[...]
+        r.scores_b[:, at] = (r.weights_b[:, at] * grad).astype(LOW)
+
+    loop(CHUNKS, back_b)
     qland_grad = own_heads(matmul_low(r.scores_b[...], r.keys[...]), two, near) * scale
     r.qland_part[s] = dense(qland_grad[0:LAND]).astype(LOW)
     qland_spread.start()
     kland_spread.start()
-    scatter_up.start(2)
-    vector_spread.start()
-    scatter_out.fill(r.grad_one[...], r.mixed[...])
-    scatter_out.start()
+    scatter_up.start(1)
 
     def keys_values(c):
         at = chunk_rows(c)
         r.grad_key[at] = across(r.scores_b[:, at], r.query_heads[...]) * scale
         values = across(r.weights_b_low[:, at], r.numer_heads[...]) + r.conv[at]
+        r.near_grads[at, 0:near] = r.grad_query[at].astype(LOW)
+        r.near_grads[at, near : 2 * near] = r.grad_key[at].astype(LOW)
         r.near_grads[at, 2 * near : 3 * near] = values.astype(LOW)
+        terms = against(r.near_grads[at], r.w_near[:, :, 0 : 3 * near].reshape(width, 3 * near))
+        behind(c, sums[3])
+        sums[3].offer(c, terms.astype(LOW))
         return jnp.sum(values, axis=0, keepdims=True)
 
     value_bias = lax.fori_loop(
         0, CHUNKS, lambda c, total: total + keys_values(c), jnp.zeros((1, near), WIDE)
     )
+    sums[3].pair_up(CHUNKS - 1)
+    scatter_v.fill_dense(r.inputs[...], r.near_grads[:, 2 * near : 3 * near])
+    scatter_v.start()
 
     def invert_back(i, carry):
         it = PINV_STEPS - 1 - i
         grads, kernel_grads = carry
         many = range(len(pairs))
-        held = [[r.history[it, part, p] for p in many] for part in range(4)]
-        befores, products, nested_two, nested_three = held
-        kernels = [r.land_kernel[p] for p in many]
-        grad_three = [0.25 * exact(a, b, (0, 0)) for a, b in zip(befores, grads)]
-        grad_two = [-exact(a, b, (0, 0)) for a, b in zip(products, grad_three)]
-        grad_one = [-exact(a, b, (0, 0)) for a, b in zip(products, grad_two)]
-        grad_product = [
-            -exact(a, b, (1, 1)) - exact(c, 7.0 * identity - d, (1, 1)) - e
-            for a, b, c, d, e in zip(grad_three, nested_two, grad_two, products, grad_one)
+        wides = [exact(grads[p], r.uppers[it, p]) for p in many]
+        product_grads = [
+            exact(r.lowers[it, p], jnp.concatenate([w[:, LAND:two], w[:, two:], grads[p]], axis=0))
+            for p, w in enumerate(wides)
         ]
-        kernel_grads = [k + exact(a, b, (1, 1)) for k, a, b in zip(kernel_grads, grad_product, befores)]
-        grads = [
-            0.25 * exact(a, b, (1, 1)) + exact(k, p, (0, 0))
-            for a, b, k, p in zip(grads, nested_three, kernels, grad_product)
+        kernel_grads = [
+            old + exact(grad, r.lowers[it, p, :, 0:LAND])
+            for p, (old, grad) in enumerate(zip(kernel_grads, product_grads))
         ]
+        grads = [wides[p][:, 0:LAND] + exact(r.turned_kernel[p], product_grads[p]) for p in many]
         return tuple(grads), tuple(kernel_grads)
 
-    scatter_up.forward(1, 3)
+    scatter_up.forward(1, 2)
+    scatter_out.forward()
     zeros = tuple(jnp.zeros((LAND, LAND), WIDE) for _ in pairs)
     grads, kernel_grads = lax.fori_loop(0, PINV_STEPS, invert_back, (tuple(inverse_grads), zeros))
     qland_a = [jnp.zeros((LAND, near), WIDE)] * 2
@@ -1010,66 +1032,113 @@
         qland_a[g] = qland_a[g] + exact(grad, r.key_land[group(g)].astype(WIDE)) * mask
         kland_a[g] = kland_a[g] + exact(grad, r.query_land[group(g)].astype(WIDE), (0, 0)) * mask
 
-    scatter_up.forward(3)
+    scatter_up.forward(2)
 
     kland_spread.finish()
     qland_spread.finish()
     pick = (iota((LAND, LAND), 1) == iota((LAND, LAND), 0) + first_slot).astype(WIDE)
 
     def slot_grads(mid, edge):
-        mid = exact(pick, mid * mid_scale)
-        both = jnp.concatenate([mid, edge * edge_scale], axis=0)
+        return jnp.concatenate([exact(pick, mid * mid_scale), edge * edge_scale], axis=0)
+
+    def parted(both):
         high = both.astype(LOW)
         return jnp.concatenate([high, (both - high.astype(WIDE)).astype(LOW)], axis=0)
 
-    r.slot_q[...] = slot_grads(qland_a[0] + over_seq(r.qland_part), qland_a[1] + qland_grad[LAND:two])
-    r.slot_k[...] = slot_grads(kland_a[0] + over_seq(r.kland_part), kland_a[1] + kland_grad[LAND:two])
-
-    def input_back(c):
+    slot_q = slot_grads(qland_a[0] + over_seq(r.qland_part), qland_a[1] + qland_grad[LAND:two])
+    slot_k = slot_grads(kland_a[0] + over_seq(r.kland_part), kland_a[1] + kland_grad[LAND:two])
+    r.slot_q[...] = parted(slot_q)
+    r.slot_k[...] = parted(slot_k)
+    r.slot_both[:, 0:near] = r.slot_q[0:two]
+    r.slot_both[:, near:] = r.slot_k[0:two]
+    slot_terms = against(r.slot_both[...], r.w_near[:, :, 0 : 2 * near].reshape(width, 2 * near))
+    correction.offer(0, slot_terms.astype(LOW))
+
+    def add_slots(c):
         at = chunk_rows(c)
         member = jnp.concatenate([r.member[at]] * 2, axis=1)
         queries = r.grad_query[at] + matmul_low(member, r.slot_q[...])
         keys = r.grad_key[at] + matmul_low(member, r.slot_k[...])
         r.near_grads[at, 0:near] = queries.astype(LOW)
         r.near_grads[at, near : 2 * near] = keys.astype(LOW)
-        terms = against(r.near_grads[at], r.w_near[:, :, 0 : 3 * near].reshape(width, 3 * near))
-        sums[3].offer(c, terms.astype(LOW))
-        sums[3].pair_up(c)
         return jnp.sum(queries, axis=0, keepdims=True)
 
     query_bias = lax.fori_loop(
-        0, CHUNKS, lambda c, total: total + input_back(c), jnp.zeros((1, near), WIDE)
-    )
+        0, CHUNKS, lambda c, total: total + add_slots(c), jnp.zeros((1, near), WIDE)
+    )
+    correction.pair_up(0)
+    scatter_qk.fill(r.inputs[...], r.near_grads[:, 0 : 2 * near])
+    scatter_qk.start()
+    scatter_v.forward()
+
+    r.tap_grad[...] = jnp.zeros_like(r.tap_grad)
+
+    def tap_products(b):
+        own = r.grad_ext[pl.ds(pl.multiple_of(b * BLOCK + REACH, REACH), BLOCK), :]
+        own = jnp.concatenate([own * m for m in masks_low], axis=0)
+        r.tap_grad[:, 0:SPAN] += against(own, window(r.value_ext, b)[:, :near])
+
+    loop(blocks, tap_products)
+    token = lax.rem(iota((heads * BLOCK, 128), 0), BLOCK)
+    slanted = r.tap_grad[...]
+    for bit in range(6):
+        moved = pltpu.roll(slanted, 128 - (1 << bit), 1)
+        slanted = jnp.where(lax.rem(token // (1 << bit), 2) == 1, moved, slanted)
+    for k in range(heads):
+        r.small_part[s, 2 + k : 3 + k, 0:128] = jnp.sum(
+            slanted[k * BLOCK : (k + 1) * BLOCK], axis=0, keepdims=True
+        )
     r.small_part[s, 0:1, 0:near] = query_bias
     r.small_part[s, 1:2, 0:near] = value_bias
+    for k in range(7):
+        r.vector_part[s, k : k + 1] = jnp.sum(r.acc[k], axis=0, keepdims=True)
+    r.vector_part[s, 7:8] = jnp.zeros((1, width), WIDE)
     small_spread.start()
-    scatter_qkv.fill(r.inputs[...], r.near_grads[...])
-    scatter_qkv.start()
-    scatter_out.forward()
-    vector_spread.finish()
-    r.vector_sum[0] = functools.reduce(jnp.add, [r.vector_part[d] for d in range(count)])
-    vector_core.start()
+    vector_spread.start()
+
+    def settle_output(c):
+        share(2, r.output, c).wait_recv()
+
+    loop(CHUNKS, settle_output)
+    store_output.start()
     r.grad_w_down[...] = scatter_down.finish()
     store_down.start()
     r.grad_w_up[...] = scatter_up.finish()
     store_up.start()
-    r.grad_w_out[...] = scatter_out.finish()
+    r.grad_w_out[...] = undense(scatter_out.finish())
     store_out.start()
-    scatter_qkv.forward()
-
-    def inputs_done(c):
+    r.grad_near[2] = undense(scatter_v.finish())
+    scatter_qk.forward()
+    vector_spread.finish()
+    r.vector_sum[0] = functools.reduce(jnp.add, [r.vector_part[d] for d in range(count)])
+    vector_core.start()
+
+    def total_inputs(c):
         def piece(i):
-            at = pl.ds(pl.multiple_of(c * size + core * half + i, step), step)
             kept = pl.ds(pl.multiple_of(c * half + i, step), step)
-            r.grad_inputs[at] = (r.wide_grad[kept] + sums[3].total(c, pl.ds(i, step))).astype(LOW)
+            r.wide_grad[kept] = r.wide_grad[kept] + sums[3].total(c, pl.ds(i, step))
 
         sums[3].arrived(c)
         pieces(piece)
-        share(4, r.grad_inputs, c).start()
+
+    loop(CHUNKS, total_inputs)
+    here = pl.ds(pl.multiple_of(core * LAND, LAND), LAND)
+    share_slots = remote(
+        r.corr_all.at[here], r.corr_all.at[here], r.corr_s.at[0], r.corr_r.at[0], core_of_chip()
+    )
+    correction.arrived(0)
+    r.corr_all[here] = correction.total(0, pl.ds(0, LAND)).astype(LOW)
+    share_slots.start()
+    share_slots.wait_recv()
+
+    def inputs_done(c):
+        slots = matmul_low(r.member[my_rows(c)], r.corr_all[...])
+        r.cotangent[my_rows(c)] = (r.wide_grad[pl.ds(pl.multiple_of(c * half, half), half)] + slots).astype(LOW)
+        share(4, r.cotangent, c).start()
 
     loop(CHUNKS, inputs_done)
-    near_total = scatter_qkv.finish()
-    for k in range(3):
+    near_total = scatter_qk.finish()
+    for k in range(2):
         r.grad_near[k] = near_total[:, k * near : (k + 1) * near]
     store_near.start()
     vector_core.wait_recv()
@@ -1079,7 +1148,7 @@
     r.smalls[...] = functools.reduce(jnp.add, [r.small_part[d] for d in range(count)])
 
     def settle_inputs(c):
-        share(4, r.grad_inputs, c).wait_recv()
+        share(4, r.cotangent, c).wait_recv()
 
     loop(CHUNKS, settle_inputs)
     store_grad_inputs.start()
@@ -1087,11 +1156,14 @@
     def settle(c):
         sums[3].core_copy(c).wait_send()
         sums[3].x_copy(c).wait_send()
-        for k, ref in enumerate((r.hidden, r.grad_two, r.output, r.grad_one, r.grad_inputs)):
+        for k, ref in enumerate((r.hidden, r.grad_two, r.output, r.grad_one, r.cotangent)):
             share(k, ref, c).wait_send()
 
     loop(CHUNKS, settle)
     vector_core.wait_send()
+    correction.core_copy(0).wait_send()
+    correction.x_copy(0).wait_send()
+    share_slots.wait_send()
     for copy in stores:
         copy.wait()
     for copy in rims[0] + rims[1]:
@@ -1156,7 +1228,7 @@
         grad_near_hbm=((3, part, near), WIDE), vectors=((8, width), WIDE), smalls=((8, PAD), WIDE),
     )
     scratch = dict(
-        inputs=low(rows, width), cotangent=low(rows, width), output=low(rows, width), grad_inputs=low(rows, width),
+        inputs=low(rows, width), cotangent=low(rows, width), output=low(rows, width),
         grad_w_out=wide(part, near), grad_w_up=wide(part, feed), grad_w_down=wide(part, feed),
         grad_near=wide(3, part, near), io=sem(8),
         packed=low(part, 4 * near), w_near=low(count, part, 4 * near), out_rows=low(width, near),
@@ -1170,7 +1242,9 @@
         numer_out=wide(count, LAND // count, PAD), numer_in=wide(count, LAND // count, PAD),
         kernel_v=wide(count, LAND // count, PAD), kernel_edge=wide(LAND, PAD),
         land_kernel=wide(2 * heads, LAND, LAND), inverse=wide(2 * heads, LAND, LAND),
-        history=wide(PINV_STEPS, 4, 2 * heads, LAND, LAND),
+        befores=wide(PINV_STEPS, 2 * heads, LAND, LAND), products=wide(PINV_STEPS, 2 * heads, LAND, LAND),
+        uppers=wide(PINV_STEPS, 2 * heads, LAND, 3 * LAND), lowers=wide(PINV_STEPS, 2 * heads, LAND, 3 * LAND),
+        turned_kernel=wide(2 * heads, LAND, LAND),
         weights_f=wide(rows, heads * two), conv=wide(rows, near),
         mixing=low(two, near), mixing_heads=low(heads * two, near), mixed=low(rows, near),
         terms=low(CHUNKS, size, width), core_in=low(CHUNKS, half, width),
@@ -1185,20 +1259,25 @@
         qland_part=low(count, 3 * LAND // 2, 128),
         tap_grad=wide(heads * BLOCK, 128), numer_heads=low(heads * two, near), total_grad=wide(heads * two, 1),
         scores_b=low(heads * two, rows), near_grads=low(rows, 3 * near),
-        slot_q=low(2 * two, near), slot_k=low(2 * two, near),
+        slot_q=low(2 * two, near), slot_k=low(2 * two, near), slot_both=low(two, 2 * near),
         vector_part=wide(count, 8, width), vector_sum=wide(2, 8, width), small_part=wide(count, 8, PAD),
     )
-    scatter = lambda lanes: (
-        low(count, part, lanes), low(lines, part, lanes), low(lines - 1, part, lanes), low(lines - 1, part, lanes)
-    )
-    for_out, for_up, for_down, for_qkv = (scatter(lanes) for lanes in (near, feed, feed, 3 * near))
+    tall = 3 * part // 2
+    for_out, for_up, for_down, for_qk, for_v = (
+        (low(count, *of), low(lines, *of), low(lines - 1, *of), low(lines - 1, *of))
+        for of in ((tall, 128), (part, feed), (part, feed), (part, 2 * near), (tall, 128))
+    )
     scratch.update(
         t_out=for_out[0], yb_out=for_out[1], pr_out=for_out[2], zb_out=for_out[3],
         t_up=for_up[0], yb_up=for_up[1], pr_up=for_up[2], zb_up=for_up[3],
         t_down=for_down[0], yb_down=for_down[1], pr_down=for_down[2], zb_down=for_down[3],
-        t_qkv=for_qkv[0], yb_qkv=for_qkv[1], pr_qkv=for_qkv[2], zb_qkv=for_qkv[3],
-        g_own=sem(6), g_zs=sem(6, lines - 1), g_zr=sem(6, lines - 1), g_ys=sem(6, lines), g_yr=sem(6, lines),
-        s_ys=sem(4, lines), s_yr=sem(4, lines), s_zs=sem(4, lines - 1), s_zr=sem(4, lines - 1),
+        t_qk=for_qk[0], yb_qk=for_qk[1], pr_qk=for_qk[2], zb_qk=for_qk[3],
+        t_v=for_v[0], yb_v=for_v[1], pr_v=for_v[2], zb_v=for_v[3],
+        corr_terms=low(1, two, width), corr_core=low(1, LAND, width), corr_out=low(1, LAND, width),
+        corr_in=low(2, 1, LAND, width), corr_sems=sem(1, 4, 1), corr_all=low(two, width),
+        corr_s=sem(1), corr_r=sem(1),
+        g_own=sem(8), g_zs=sem(8, lines - 1), g_zr=sem(8, lines - 1), g_ys=sem(8, lines), g_yr=sem(8, lines),
+        s_ys=sem(5, lines), s_yr=sem(5, lines), s_zs=sem(5, lines - 1), s_zr=sem(5, lines - 1),
         e_s=sem(8, count - 1), e_r=sem(8, count - 1), h_sems=sem(4, 4, CHUNKS),
         rim_s=sem(2, 2), rim_r=sem(2, 2), share_s=sem(5, CHUNKS), share_r=sem(5, CHUNKS),
         core_s=sem(1), core_r=sem(1),

time: 190 us -> 181 us (0.953)
  Pallas kernels: 188 us -> 179 us
    pallas_call x1, Pallas kernels: 183 us -> 174 us  [fused_body(): pl.pallas_call(functools.partial(layer_kernel, count, list(operands) + li...]
where the time goes in v3:
time: 181 us; the launch traced here: 180 us
  Pallas kernels  179 us (99%)
    pallas_call x1, Pallas kernels, fused_body(): pl.pallas_call(functools.partial(layer_kernel, count, list(operands) + li...  174 us
    pallas_call x1, Pallas kernels, fused_body(): pl.pallas_call(hand_out, out_shape=(whole, whole, block(near), block(near...  5.05 us

profile of v3, /device:TPU:0, one launch (start us, length us, event | category | flops | bytes accessed | tf_op | source)
XLA Modules:
  0.0 179.6 jit_solution(3494240198255547304)
XLA Ops:
  0.7 173.7 %shard_map.322 = (bf16[1024,768]{1,0:T(8,128)(2,1)}, bf16[1024,768]{1,0:T(8,128)(2,1)}, f32[96,192]{1,0:T(8,128)}, f32[96,768]{1,0:T(8,128)}, f32[96,768]{1,0:T(...) custom-call(s32[3]{0:T(128)} %refs_0_.1, f32[3,33]{1,0:T(4,128)} %refs_1_.1, ...), custom_call_target="tpu_custom_call" | custom-call | tf_op jit(solution)/shard_map/pallas_call | solution.py:1286
  174.4 5.0 %shard_map.323 = (bf16[1024,768]{1,0:T(8,128)(2,1)}, bf16[1024,768]{1,0:T(8,128)(2,1)}, f32[96,192]{1,0:T(8,128)}, f32[96,192]{1,0:T(8,128)}, f32[96,192]{1,0:T(...) custom-call(bf16[1024,768]{1,0:T(8,128)(2,1)} %get-tuple-element.26., ...), custom_call_target="tpu_custom_call" | custom-call | tf_op jit(solution)/shard_map/pallas_call | solution.py:1299

commit v4 on v3

--- a/solution.py
+++ b/solution.py
@@ -247,13 +247,12 @@
             [terms[:, 0 : part // 2, 128:], terms[:, part // 2 :, 128:]], axis=2
         )
 
-    def start(self, first=0, last=None):
-        order = list(range(1, self.lines)) + [0]
-        for j in order[first:last]:
+    def start(self, *away):
+        for j in away or list(range(1, self.lines)) + [0]:
             self.y_copies[j].start()
 
-    def forward(self, first=1, last=None):
-        for j in range(self.lines)[first:last]:
+    def forward(self, *away):
+        for j in away or range(1, self.lines):
             line = lax.rem(self.z + j, self.lines)
             self.y_copies[j].wait_recv()
             self.pair[j - 1] = (
@@ -308,6 +307,28 @@
         s = place()[0]
         super().start()
         self.into[s] = self.out[s]
+
+
+class SeqSum:
+    def __init__(self, count, out, into, sums, send, recv):
+        self.count, self.into, self.sums = count, into, sums
+        self.swap = Swap(count, out, into, send.at[0], recv.at[0])
+        self.spread = Spread(count, sums, send.at[1], recv.at[1])
+
+    def start(self):
+        self.swap.start()
+
+    def add(self):
+        self.swap.finish()
+        self.sums[place()[0]] = functools.reduce(jnp.add, [self.into[d] for d in range(self.count)])
+        self.spread.start()
+
+    def finish(self):
+        self.spread.finish()
+
+    def close(self):
+        self.swap.close()
+        self.spread.close()
 
 
 class HeadSum:
@@ -448,14 +469,18 @@
     landmarks = Spread(count, r.land_part, r.e_s.at[0], r.e_r.at[0])
     numer_swap = Swap(count, r.numer_out, r.numer_in, r.e_s.at[1], r.e_r.at[1])
     kernel_spread = Spread(count, r.kernel_v, r.e_s.at[2], r.e_r.at[2])
-    mixing_spread = Spread(count, r.mix_part, r.e_s.at[3], r.e_r.at[3])
-    kland_spread = Spread(count, r.kland_part, r.e_s.at[4], r.e_r.at[4])
-    qland_spread = Spread(count, r.qland_part, r.e_s.at[5], r.e_r.at[5])
-    vector_spread = Spread(count, r.vector_part, r.e_s.at[6], r.e_r.at[6])
-    small_spread = Spread(count, r.small_part, r.e_s.at[7], r.e_r.at[7])
-    spreads = [
-        landmarks, numer_swap, kernel_spread, mixing_spread, kland_spread, qland_spread, vector_spread, small_spread,
-    ]
+    small_spread = Spread(count, r.small_part, r.e_s.at[3], r.e_r.at[3])
+    mix_sum, land_sum, vector_total = (
+        SeqSum(count, out, into, total, r.e_s.at[pl.ds(4 + 2 * k, 2)], r.e_r.at[pl.ds(4 + 2 * k, 2)])
+        for k, (out, into, total) in enumerate(
+            (
+                (r.mix_out, r.mix_in, r.mix_sums),
+                (r.land_out, r.land_in, r.land_sums),
+                (r.vector_out, r.vector_in, r.vector_sums),
+            )
+        )
+    )
+    spreads = [landmarks, numer_swap, kernel_spread, small_spread, mix_sum, land_sum, vector_total]
 
     def rim(k, ext):
         first = remote(
@@ -525,6 +550,7 @@
     gather_vo.start()
     load_cotangent.start()
     r.small_part[s] = jnp.zeros((8, PAD), WIDE)
+    r.vectors[...] = jnp.zeros_like(r.vectors)
     head_lane = iota((8, PAD), 1) // HEAD_DIM
     masks = [(head_lane == k).astype(WIDE)[0:1] for k in range(heads)]
     masks_low = [m[:, :near].astype(LOW) for m in masks]
@@ -698,8 +724,6 @@
     inverses = tuple(first_inverse(k, g, i) for i, (k, g) in enumerate(pairs))
     inverses = lax.fori_loop(0, PINV_STEPS // 2, invert, inverses)
 
-    ups[0].forward()
-    ups[1].forward()
 
     numer_swap.finish()
     parts = [r.numer_in[d] for d in range(count)]
@@ -719,8 +743,9 @@
         )
     r.kernel_v[s] = joined
     kernel_spread.start()
-    for piece in downs:
-        piece.start()
+    ups[0].forward()
+    ups[1].forward()
+    downs[0].start()
     inverses = lax.fori_loop(PINV_STEPS // 2, PINV_STEPS, invert, inverses)
     for i, inverse in enumerate(inverses):
         r.inverse[i] = inverse
@@ -748,6 +773,8 @@
         r.mixing[group(g), :] = mixed[:, :near].astype(LOW)
     spread_heads(r.mixing_heads, r.mixing[...])
     ups[2].forward()
+    downs[1].start()
+    downs[2].start()
 
     def project_out(c):
         at = chunk_rows(c)
@@ -838,6 +865,8 @@
     loop(CHUNKS, feed_forward)
     sums[1].pair_up(CHUNKS - 1)
 
+    order = [2, 1] + list(range(3, lines)) + [0] if lines > 2 else [1, 0]
+
     def feed_back(c):
         def piece(i):
             at = pl.ds(pl.multiple_of(c * size + core * half + i, step), step)
@@ -859,6 +888,12 @@
         share(2, r.output, c).start()
         behind(c, sums[2])
         share(1, r.grad_two, c).wait_recv()
+
+        @pl.when(c == CHUNKS - 1)
+        def _():
+            scatter_down.fill(r.grad_two[...], r.active[...])
+            scatter_down.start(*order)
+
         at = chunk_rows(c)
         r.tmp[...] = matmul_low(r.grad_two[at], r.full_down[...].reshape(width, feed))
 
@@ -874,8 +909,7 @@
     loop(CHUNKS, feed_back)
     sums[2].pair_up(CHUNKS - 1)
 
-    scatter_down.fill(r.grad_two[...], r.active[...])
-    scatter_down.start()
+    ups_next = list(range(2, lines)) + [0]
     r.mix_grad[...] = jnp.zeros_like(r.mix_grad)
     r.kland_grad[...] = jnp.zeros_like(r.kland_grad)
 
@@ -891,6 +925,21 @@
             r.acc[3] += fold(grad * normed)
             r.acc[4] += fold(grad)
             r.acc[5] += fold(back)
+
+        @pl.when(c == 1)
+        def _():
+            scatter_down.forward(order[0])
+            scatter_up.fill(r.hidden[...], r.grad_lift[...])
+
+        if lines > 2:
+
+            @pl.when(c == 2)
+            def _():
+                scatter_down.forward(order[1])
+
+        @pl.when(c == CHUNKS - 1)
+        def _():
+            scatter_up.start(1)
 
         sums[2].arrived(c)
         pieces(piece)
@@ -910,20 +959,12 @@
         r.mix_grad[...] += across(weights.astype(LOW), grad)
         r.kland_grad[...] += across(scores, r.queries[at])
 
-        @pl.when(c == 1)
-        def _():
-            scatter_up.fill(r.hidden[...], r.grad_lift[...])
-
-        @pl.when(c == 2)
-        def _():
-            scatter_down.forward(1, 2)
-
     loop(CHUNKS, mix_back)
     mix_grad = own_heads(r.mix_grad[...], two, near)
     kland_grad = own_heads(r.kland_grad[...], two, near) * scale
-    r.mix_part[s] = dense(mix_grad[0:LAND]).astype(LOW)
-    r.kland_part[s] = dense(kland_grad[0:LAND]).astype(LOW)
-    mixing_spread.start()
+    each = LAND // count
+    r.mix_out[...] = mix_grad[0:LAND].reshape(count, each, near)
+    mix_sum.start()
     for copy in rims[1]:
         copy.start()
 
@@ -933,16 +974,18 @@
 
     scatter_out.fill_dense(r.grad_one[...], r.mixed[...])
     scatter_out.start()
-    scatter_up.start(0, 1)
-    loop(blocks - 2, lambda b: convolve_back(b + 1))
+    loop(blocks // 2 - 1, lambda b: convolve_back(b + 1))
+    mix_sum.add()
+    if order[2:-1]:
+        scatter_down.forward(*order[2:-1])
+    scatter_up.start(*ups_next[:1])
+    loop(blocks // 2 - 1, lambda b: convolve_back(b + blocks // 2))
     for copy in rims[1]:
         copy.wait_recv()
     loop(2, lambda b: convolve_back(b * (blocks - 1)))
-    scatter_down.forward(2)
-
-    mixing_spread.finish()
-    over_seq = lambda ref: undense(functools.reduce(jnp.add, [ref[d].astype(WIDE) for d in range(count)]))
-    mix_grads = [over_seq(r.mix_part), mix_grad[LAND:two]]
+
+    mix_sum.finish()
+    mix_grads = [r.mix_sums[...].reshape(LAND, near), mix_grad[LAND:two]]
     stats = r.kernel_v[...].reshape(LAND, PAD)
     mid_totals = wide_heads(stats, near)[:, :near]
     divisors = [mid_totals, edge_totals[:, :near]]
@@ -976,29 +1019,38 @@
 
     loop(CHUNKS, back_b)
     qland_grad = own_heads(matmul_low(r.scores_b[...], r.keys[...]), two, near) * scale
-    r.qland_part[s] = dense(qland_grad[0:LAND]).astype(LOW)
-    qland_spread.start()
-    kland_spread.start()
-    scatter_up.start(1)
-
-    def keys_values(c):
+    r.land_out[:, :, 0:near] = qland_grad[0:LAND].reshape(count, each, near)
+    r.land_out[:, :, near:] = kland_grad[0:LAND].reshape(count, each, near)
+    land_sum.start()
+    if ups_next[1:]:
+        scatter_up.start(*ups_next[1:])
+    scatter_up.forward(1)
+
+    def values_back(c):
+        at = chunk_rows(c)
+        values = across(r.weights_b_low[:, at], r.numer_heads[...]) + r.conv[at]
+        r.near_grads[at, 2 * near : 3 * near] = values.astype(LOW)
+        return jnp.sum(values, axis=0, keepdims=True)
+
+    value_bias = lax.fori_loop(
+        0, CHUNKS, lambda c, total: total + values_back(c), jnp.zeros((1, near), WIDE)
+    )
+    scatter_v.fill_dense(r.inputs[...], r.near_grads[:, 2 * near : 3 * near])
+    scatter_v.start()
+
+    def input_terms(c):
         at = chunk_rows(c)
         r.grad_key[at] = across(r.scores_b[:, at], r.query_heads[...]) * scale
-        values = across(r.weights_b_low[:, at], r.numer_heads[...]) + r.conv[at]
         r.near_grads[at, 0:near] = r.grad_query[at].astype(LOW)
         r.near_grads[at, near : 2 * near] = r.grad_key[at].astype(LOW)
-        r.near_grads[at, 2 * near : 3 * near] = values.astype(LOW)
         terms = against(r.near_grads[at], r.w_near[:, :, 0 : 3 * near].reshape(width, 3 * near))
         behind(c, sums[3])
         sums[3].offer(c, terms.astype(LOW))
-        return jnp.sum(values, axis=0, keepdims=True)
-
-    value_bias = lax.fori_loop(
-        0, CHUNKS, lambda c, total: total + keys_values(c), jnp.zeros((1, near), WIDE)
-    )
-    sums[3].pair_up(CHUNKS - 1)
-    scatter_v.fill_dense(r.inputs[...], r.near_grads[:, 2 * near : 3 * near])
-    scatter_v.start()
+
+    loop(CHUNKS // 2, input_terms)
+    land_sum.add()
+    if lines > 2:
+        scatter_up.forward(2)
 
     def invert_back(i, carry):
         it = PINV_STEPS - 1 - i
@@ -1016,10 +1068,19 @@
         grads = [wides[p][:, 0:LAND] + exact(r.turned_kernel[p], product_grads[p]) for p in many]
         return tuple(grads), tuple(kernel_grads)
 
-    scatter_up.forward(1, 2)
-    scatter_out.forward()
     zeros = tuple(jnp.zeros((LAND, LAND), WIDE) for _ in pairs)
     grads, kernel_grads = lax.fori_loop(0, PINV_STEPS, invert_back, (tuple(inverse_grads), zeros))
+    scatter_out.forward()
+    loop(CHUNKS // 2, lambda c: input_terms(c + CHUNKS // 2))
+    sums[3].pair_up(CHUNKS - 1)
+    for k in range(7):
+        r.vectors[k : k + 1] = jnp.sum(r.acc[k], axis=0, keepdims=True)
+    lanes = r.vector_out.shape[2]
+    for d in range(count):
+        r.vector_out[d] = r.vectors[:, d * lanes : (d + 1) * lanes] if d * lanes < width else jnp.zeros((8, lanes), WIDE)
+    vector_total.start()
+    if lines > 3:
+        scatter_up.forward(*range(3, lines))
     qland_a = [jnp.zeros((LAND, near), WIDE)] * 2
     kland_a = [jnp.zeros((LAND, near), WIDE)] * 2
     for i, (k, g) in enumerate(pairs):
@@ -1032,10 +1093,9 @@
         qland_a[g] = qland_a[g] + exact(grad, r.key_land[group(g)].astype(WIDE)) * mask
         kland_a[g] = kland_a[g] + exact(grad, r.query_land[group(g)].astype(WIDE), (0, 0)) * mask
 
-    scatter_up.forward(2)
-
-    kland_spread.finish()
-    qland_spread.finish()
+
+    land_sum.finish()
+    land_total = r.land_sums[...].reshape(LAND, 2 * near)
     pick = (iota((LAND, LAND), 1) == iota((LAND, LAND), 0) + first_slot).astype(WIDE)
 
     def slot_grads(mid, edge):
@@ -1045,8 +1105,8 @@
         high = both.astype(LOW)
         return jnp.concatenate([high, (both - high.astype(WIDE)).astype(LOW)], axis=0)
 
-    slot_q = slot_grads(qland_a[0] + over_seq(r.qland_part), qland_a[1] + qland_grad[LAND:two])
-    slot_k = slot_grads(kland_a[0] + over_seq(r.kland_part), kland_a[1] + kland_grad[LAND:two])
+    slot_q = slot_grads(qland_a[0] + land_total[:, 0:near], qland_a[1] + qland_grad[LAND:two])
+    slot_k = slot_grads(kland_a[0] + land_total[:, near:], kland_a[1] + kland_grad[LAND:two])
     r.slot_q[...] = parted(slot_q)
     r.slot_k[...] = parted(slot_k)
     r.slot_both[:, 0:near] = r.slot_q[0:two]
@@ -1069,6 +1129,7 @@
     correction.pair_up(0)
     scatter_qk.fill(r.inputs[...], r.near_grads[:, 0 : 2 * near])
     scatter_qk.start()
+    vector_total.add()
     scatter_v.forward()
 
     r.tap_grad[...] = jnp.zeros_like(r.tap_grad)
@@ -1090,11 +1151,7 @@
         )
     r.small_part[s, 0:1, 0:near] = query_bias
     r.small_part[s, 1:2, 0:near] = value_bias
-    for k in range(7):
-        r.vector_part[s, k : k + 1] = jnp.sum(r.acc[k], axis=0, keepdims=True)
-    r.vector_part[s, 7:8] = jnp.zeros((1, width), WIDE)
     small_spread.start()
-    vector_spread.start()
 
     def settle_output(c):
         share(2, r.output, c).wait_recv()
@@ -1109,8 +1166,9 @@
     store_out.start()
     r.grad_near[2] = undense(scatter_v.finish())
     scatter_qk.forward()
-    vector_spread.finish()
-    r.vector_sum[0] = functools.reduce(jnp.add, [r.vector_part[d] for d in range(count)])
+    vector_total.finish()
+    for d in range(width // lanes):
+        r.vector_sum[0, :, d * lanes : (d + 1) * lanes] = r.vector_sums[d]
     vector_core.start()
 
     def total_inputs(c):
@@ -1210,6 +1268,7 @@
     near, feed, heads = w_query.shape[1], w_up.shape[1], conv_taps.shape[0]
     size, part, lines = rows // CHUNKS, width // count, count // 2
     half, two = size // 2, 2 * LAND
+    share = 128 * -(-width // 128 // count)
     low = lambda *shape: pltpu.VMEM(shape, LOW)
     wide = lambda *shape: pltpu.VMEM(shape, WIDE)
     sem = lambda *shape: pltpu.SemaphoreType.DMA(shape)
@@ -1255,12 +1314,14 @@
         tmp=wide(size, feed), acc=wide(7, 8, width),
         grad_ext=low(rows + 2 * REACH, near), grad_query=wide(rows, near), grad_key=wide(rows, near),
         mix_grad=wide(heads * two, near), kland_grad=wide(heads * two, near),
-        mix_part=low(count, 3 * LAND // 2, 128), kland_part=low(count, 3 * LAND // 2, 128),
-        qland_part=low(count, 3 * LAND // 2, 128),
+        mix_out=wide(count, LAND // count, near), mix_in=wide(count, LAND // count, near),
+        mix_sums=wide(count, LAND // count, near), land_out=wide(count, LAND // count, 2 * near),
+        land_in=wide(count, LAND // count, 2 * near), land_sums=wide(count, LAND // count, 2 * near),
+        vector_out=wide(count, 8, share), vector_in=wide(count, 8, share), vector_sums=wide(count, 8, share),
         tap_grad=wide(heads * BLOCK, 128), numer_heads=low(heads * two, near), total_grad=wide(heads * two, 1),
         scores_b=low(heads * two, rows), near_grads=low(rows, 3 * near),
         slot_q=low(2 * two, near), slot_k=low(2 * two, near), slot_both=low(two, 2 * near),
-        vector_part=wide(count, 8, width), vector_sum=wide(2, 8, width), small_part=wide(count, 8, PAD),
+        vector_sum=wide(2, 8, width), small_part=wide(count, 8, PAD),
     )
     tall = 3 * part // 2
     for_out, for_up, for_down, for_qk, for_v = (
@@ -1278,7 +1339,7 @@
         corr_s=sem(1), corr_r=sem(1),
         g_own=sem(8), g_zs=sem(8, lines - 1), g_zr=sem(8, lines - 1), g_ys=sem(8, lines), g_yr=sem(8, lines),
         s_ys=sem(5, lines), s_yr=sem(5, lines), s_zs=sem(5, lines - 1), s_zr=sem(5, lines - 1),
-        e_s=sem(8, count - 1), e_r=sem(8, count - 1), h_sems=sem(4, 4, CHUNKS),
+        e_s=sem(10, count - 1), e_r=sem(10, count - 1), h_sems=sem(4, 4, CHUNKS),
         rim_s=sem(2, 2), rim_r=sem(2, 2), share_s=sem(5, CHUNKS), share_r=sem(5, CHUNKS),
         core_s=sem(1), core_r=sem(1),
     )
@@ -1616,9 +1677,10 @@
 
 
 def solution(mesh):
-    aligned = (768 // mesh.shape["seq"]) % 16 == 0
+    seq, head = mesh.shape["seq"], mesh.shape["head"]
+    fits = head == 4 and seq >= 4 and LAND % (8 * seq) == 0
     return jax.shard_map(
-        fused_body if aligned else plain_body,
+        fused_body if fits else plain_body,
         mesh=mesh,
         in_specs=(
             P("seq", None),

time: 181 us -> 170 us (0.939)
  Pallas kernels: 179 us -> 169 us
    pallas_call x1, Pallas kernels: 174 us -> 164 us  [fused_body(): pl.pallas_call(functools.partial(layer_kernel, count, list(operands) + li...]
where the time goes in v4:
time: 170 us
  Pallas kernels  169 us (99%)
    pallas_call x1, Pallas kernels, fused_body(): pl.pallas_call(functools.partial(layer_kernel, count, list(operands) + li...  164 us
    pallas_call x1, Pallas kernels, fused_body(): pl.pallas_call(hand_out, out_shape=(whole, whole, block(near), block(near...  5.05 us

profile of v4, /device:TPU:0, one launch (start us, length us, event | category | flops | bytes accessed | tf_op | source)
XLA Modules:
  0.0 170.2 jit_solution(11464471758509451791)
XLA Ops:
  0.7 164.3 %shard_map.322 = (bf16[1024,768]{1,0:T(8,128)(2,1)}, bf16[1024,768]{1,0:T(8,128)(2,1)}, f32[96,192]{1,0:T(8,128)}, f32[96,768]{1,0:T(8,128)}, f32[96,768]{1,0:T(...) custom-call(s32[3]{0:T(128)} %refs_0_.1, f32[3,33]{1,0:T(4,128)} %refs_1_.1, ...), custom_call_target="tpu_custom_call" | custom-call | tf_op jit(solution)/shard_map/pallas_call | solution.py:1347
  165.0 5.0 %shard_map.323 = (bf16[1024,768]{1,0:T(8,128)(2,1)}, bf16[1024,768]{1,0:T(8,128)(2,1)}, f32[96,192]{1,0:T(8,128)}, f32[96,192]{1,0:T(8,128)}, f32[96,192]{1,0:T(...) custom-call(bf16[1024,768]{1,0:T(8,128)(2,1)} %get-tuple-element.26., ...), custom_call_target="tpu_custom_call" | custom-call | tf_op jit(solution)/shard_map/pallas_call | solution.py:1360

commit v5 on v4

--- a/solution.py
+++ b/solution.py
@@ -145,6 +145,11 @@
 def x_neighbour():
     s, _, _, _, x, core = place()
     return (s, 2 * (1 - x) + core)
+
+
+def across_x():
+    s, _, _, _, x, core = place()
+    return (s, 2 * (1 - x) + 1 - core)
 
 
 def y_neighbour():
@@ -413,6 +418,15 @@
     return jnp.concatenate([block[0:n], rest], axis=1)
 
 
+def halves(wide_block):
+    high = wide_block.astype(LOW)
+    return high, (wide_block - high.astype(WIDE)).astype(LOW)
+
+
+def thrice(left, right):
+    return matmul_low(left[0], right[0]) + (matmul_low(left[0], right[1]) + matmul_low(left[1], right[0]))
+
+
 def loop(count, body):
     lax.fori_loop(0, count, lambda i, carry: (body(i), carry)[1], 0)
 
@@ -435,11 +449,25 @@
     everyone = along_seq(count)
     before, after = (lax.rem(s + count - 1, count), h), (lax.rem(s + 1, count), h)
 
-    flat = lambda ref: ref[...].reshape(1, ref.shape[0])
-    bias_query, bias_value, bias_out = flat(r.bias_query), flat(r.bias_value), flat(r.bias_out)
-    bias_up, bias_down = flat(r.bias_up), flat(r.bias_down)
-    gain_one, bias_one, gain_two, bias_two = (
-        flat(r.gain_one), flat(r.bias_one), flat(r.gain_two), flat(r.bias_two)
+    load_shards, load_vectors = (
+        [pltpu.make_async_copy(ref, held, sems.at[k]) for k, (ref, held) in enumerate(pairs_of)]
+        for pairs_of, sems in (
+            (
+                (
+                    (r.w_query_hbm, r.w_query), (r.w_key_hbm, r.w_key),
+                    (r.w_value_hbm, r.w_value), (r.w_out_hbm, r.w_out),
+                ),
+                r.shard_sems,
+            ),
+            (
+                (
+                    (r.bias_query_hbm, r.bias_query), (r.bias_value_hbm, r.bias_value), (r.bias_out_hbm, r.bias_out),
+                    (r.bias_up_hbm, r.bias_up), (r.bias_down_hbm, r.bias_down), (r.gain_one_hbm, r.gain_one),
+                    (r.bias_one_hbm, r.bias_one), (r.gain_two_hbm, r.gain_two), (r.bias_two_hbm, r.bias_two),
+                ),
+                r.vector_sems,
+            ),
+        )
     )
 
     def gather(k, shard, full, lo, hi):
@@ -465,7 +493,22 @@
     scatter_v = scatter(4, r.t_v, r.yb_v, r.pr_v, r.zb_v)
     scatters = [scatter_out, scatter_up, scatter_down, scatter_qk, scatter_v]
     correction = HeadSum(0, r.corr_terms, r.corr_core, r.corr_out, r.corr_in, r.corr_sems)
-    sums = [HeadSum(k, r.terms, r.core_in, r.x_out, r.x_in, r.h_sems) for k in range(4)]
+    sums = [HeadSum(k, r.terms, r.core_in, r.x_out, r.x_in, r.h_sems) for k in range(3)]
+
+    out_copies = [
+        remote(r.out_turned.at[0], r.out_turned.at[1], r.w_s.at[0], r.w_r.at[0], core_of_chip()),
+        remote(r.out_turned.at[0], r.out_turned.at[2], r.w_s.at[1], r.w_r.at[1], x_neighbour()),
+        remote(r.out_turned.at[2], r.out_turned.at[3], r.w_s.at[2], r.w_r.at[2], core_of_chip()),
+    ]
+
+    def mixed_copies(c):
+        return [
+            remote(r.mixed_out.at[c, part], r.mixed_in.at[k, c], r.m_s.at[k, c], r.m_r.at[k, c], device)
+            for k, (part, device) in enumerate(
+                ((1 - core, core_of_chip()), (core, x_neighbour()), (1 - core, across_x()))
+            )
+        ]
+
     landmarks = Spread(count, r.land_part, r.e_s.at[0], r.e_r.at[0])
     numer_swap = Swap(count, r.numer_out, r.numer_in, r.e_s.at[1], r.e_r.at[1])
     kernel_spread = Spread(count, r.kernel_v, r.e_s.at[2], r.e_r.at[2])
@@ -505,7 +548,6 @@
         for k, (ref, out) in enumerate(
             (
                 (r.output, r.output_hbm),
-                (r.cotangent, r.grad_inputs_hbm),
                 (r.grad_w_out, r.grad_w_out_hbm),
                 (r.grad_w_up, r.grad_w_up_hbm),
                 (r.grad_w_down, r.grad_w_down_hbm),
@@ -513,14 +555,17 @@
             )
         )
     ]
-    store_output, store_grad_inputs, store_out, store_up, store_down, store_near = stores
+    store_output, store_out, store_up, store_down, store_near = stores
     vector_core = remote(
         r.vector_sum.at[0], r.vector_sum.at[1], r.core_s.at[0], r.core_r.at[0], core_of_chip()
     )
 
-    met = [core_of_chip(), x_neighbour()] + everyone
+    met = [core_of_chip(), x_neighbour(), across_x()] + everyone
     greet(met)
-    load_inputs.start()
+    for copy in load_shards + [load_inputs] + load_vectors:
+        copy.start()
+    for copy in load_shards:
+        copy.wait()
     r.packed[:, 0:near] = r.w_query[...]
     r.packed[:, near : 2 * near] = r.w_key[...]
     r.packed[:, 2 * near : 3 * near] = r.w_value[...]
@@ -598,6 +643,14 @@
     gather_qk.forward()
     gather_vo.forward()
     load_inputs.wait()
+    for copy in load_vectors:
+        copy.wait()
+    flat = lambda ref: ref[...].reshape(1, ref.shape[0])
+    bias_query, bias_value, bias_out = flat(r.bias_query), flat(r.bias_value), flat(r.bias_out)
+    bias_up, bias_down = flat(r.bias_up), flat(r.bias_down)
+    gain_one, bias_one, gain_two, bias_two = (
+        flat(r.gain_one), flat(r.bias_one), flat(r.gain_two), flat(r.bias_two)
+    )
     gather_qk.finish()
 
     def project_qk(c):
@@ -631,7 +684,9 @@
     loop(CHUNKS, project_v)
     for copy in rims[0]:
         copy.start()
-    r.out_rows[...] = r.w_near[:, :, 3 * near :].reshape(width, near)
+    r.out_turned[0] = r.w_near[:, :, 3 * near :].reshape(width, near).T
+    for copy in out_copies[0:2]:
+        copy.start()
 
     def convolve_values(b):
         r.conv[pl.ds(pl.multiple_of(b * BLOCK, BLOCK), BLOCK), :] = convolve(
@@ -669,13 +724,12 @@
         largest = jnp.max(scores, axis=1, keepdims=True)
         weights = jnp.exp(scores - largest) * member
         r.weights_b[at] = weights
-        r.weights_b_low[at] = weights.astype(LOW)
         r.max_b[at] = largest
         r.total_b[at] = jnp.sum(weights, axis=1, keepdims=True)
 
     loop(CHUNKS, score_b)
     loop(2 * heads, attend_b)
-    numer = own_heads(matmul_low(r.weights_b_low[...], own_values()), two, PAD)
+    numer = own_heads(matmul_low(r.weights_b[...].astype(LOW), own_values()), two, PAD)
     lane = iota((two, PAD), 1)
     for k in range(heads):
         numer = jnp.where(lane == near + k, r.total_b[k * two : (k + 1) * two], numer)
@@ -780,10 +834,17 @@
         at = chunk_rows(c)
         attended = matmul_low(r.weights_f[at].astype(LOW), r.mixing_heads[...])
         r.mixed[at] = (attended + r.conv[at]).astype(LOW)
-        sums[0].offer(c, against(r.mixed[at], r.out_rows[...]).astype(LOW))
-
+        for part in range(2):
+            at = pl.ds(pl.multiple_of(c * size + part * half, half), half)
+            r.mixed_out[c, part] = dense(r.mixed[at])
+        for copy in mixed_copies(c):
+            copy.start()
+
+    out_copies[1].wait_recv()
+    out_copies[2].start()
     loop(CHUNKS, project_out)
-    loop(CHUNKS, sums[0].pair_up)
+    out_copies[0].wait_recv()
+    out_copies[2].wait_recv()
     downs[0].forward()
 
     def prepare(it):
@@ -796,16 +857,19 @@
         seconds = [exact(t, p) for t, p in zip(firsts, products)]
         for i in many:
             p, q, c = products[i].T, squares[i].T, cubes[i].T
-            r.uppers[it, i, :, 0:LAND] = 3.25 * identity - 3.75 * p + 1.75 * q - 0.25 * c
-            r.uppers[it, i, :, LAND:two] = 1.75 * p - 3.75 * identity - 0.25 * q
-            r.uppers[it, i, :, two:] = 1.75 * identity - 0.25 * p
-            r.lowers[it, i, :, 0:LAND] = befores[i].T
-            r.lowers[it, i, :, LAND:two] = firsts[i].T
-            r.lowers[it, i, :, two:] = -0.25 * seconds[i].T
+            uppers = (
+                3.25 * identity - 3.75 * p + 1.75 * q - 0.25 * c,
+                1.75 * p - 3.75 * identity - 0.25 * q,
+                1.75 * identity - 0.25 * p,
+            )
+            for k, (upper, lower) in enumerate(zip(uppers, (befores[i].T, firsts[i].T, -0.25 * seconds[i].T))):
+                for half_of, (a, b) in enumerate(zip(halves(upper), halves(lower))):
+                    r.uppers[it, i, half_of, :, group(k)] = a
+                    r.lowers[it, i, half_of, :, group(k)] = b
 
     loop(PINV_STEPS, prepare)
     for i in range(len(pairs)):
-        r.turned_kernel[i] = r.land_kernel[i].T
+        r.turned_kernel[i, 0], r.turned_kernel[i, 1] = halves(r.land_kernel[i].T)
     r.acc[...] = jnp.zeros_like(r.acc)
     for piece in ups:
         piece.finish()
@@ -813,16 +877,22 @@
     pieces = lambda body: loop(half // step, lambda i: body(pl.multiple_of(i * step, step)))
 
     def norm_first(c):
+        for copy in mixed_copies(c):
+            copy.wait_recv()
+        theirs = [undense(r.mixed_in[k, c]) for k in range(3)]
+        r.tmp[0:half] = matmul_low(r.mixed[my_rows(c)], r.out_turned[0]) + matmul_low(theirs[0], r.out_turned[1])
+        r.tmp[half:size] = matmul_low(theirs[1], r.out_turned[2]) + matmul_low(theirs[2], r.out_turned[3])
+
         def piece(i):
             at = pl.ds(pl.multiple_of(c * size + core * half + i, step), step)
             kept = pl.ds(pl.multiple_of(c * half + i, step), step)
-            pre = r.inputs[at].astype(WIDE) + sums[0].total(c, pl.ds(i, step)) + bias_out
+            attended = r.tmp[pl.ds(i, step)] + r.tmp[pl.ds(pl.multiple_of(half + i, step), step)]
+            pre = r.inputs[at].astype(WIDE) + attended + bias_out
             normed, inv = normalize(pre)
             r.norm_one[kept] = normed
             r.inv_one[kept] = inv
             r.hidden[at] = (normed * gain_one + bias_one).astype(LOW)
 
-        sums[0].arrived(c)
         pieces(piece)
         share(0, r.hidden, c).start()
 
@@ -841,7 +911,7 @@
 
     def lower(c):
         at = chunk_rows(c)
-        sums[1].offer(c, against(r.active[at], r.full_down[...].reshape(width, feed)).astype(LOW))
+        sums[0].offer(c, against(r.active[at], r.full_down[...].reshape(width, feed)).astype(LOW))
 
     def behind(c, total):
         @pl.when(c > 0)
@@ -850,7 +920,7 @@
 
     def feed_forward(c):
         norm_first(c)
-        behind(c, sums[1])
+        behind(c, sums[0])
         lift(c)
 
         @pl.when(c == 0)
@@ -863,7 +933,7 @@
         lower(c)
 
     loop(CHUNKS, feed_forward)
-    sums[1].pair_up(CHUNKS - 1)
+    sums[0].pair_up(CHUNKS - 1)
 
     order = [2, 1] + list(range(3, lines)) + [0] if lines > 2 else [1, 0]
 
@@ -871,7 +941,7 @@
         def piece(i):
             at = pl.ds(pl.multiple_of(c * size + core * half + i, step), step)
             kept = pl.ds(pl.multiple_of(c * half + i, step), step)
-            pre = r.norm_one[kept] * gain_one + bias_one + sums[1].total(c, pl.ds(i, step)) + bias_down
+            pre = r.norm_one[kept] * gain_one + bias_one + sums[0].total(c, pl.ds(i, step)) + bias_down
             normed, inv = normalize(pre)
             r.output[at] = (normed * gain_two + bias_two).astype(LOW)
             grad = r.cotangent[at].astype(WIDE)
@@ -882,11 +952,11 @@
             r.acc[1] += fold(grad)
             r.acc[2] += fold(back)
 
-        sums[1].arrived(c)
+        sums[0].arrived(c)
         pieces(piece)
         share(1, r.grad_two, c).start()
         share(2, r.output, c).start()
-        behind(c, sums[2])
+        behind(c, sums[1])
         share(1, r.grad_two, c).wait_recv()
 
         @pl.when(c == CHUNKS - 1)
@@ -904,10 +974,10 @@
             r.acc[6] += fold(value)
 
         loop(size // step, curve)
-        sums[2].offer(c, against(r.grad_lift[at], r.full_up[...].reshape(width, feed)).astype(LOW))
+        sums[1].offer(c, against(r.grad_lift[at], r.full_up[...].reshape(width, feed)).astype(LOW))
 
     loop(CHUNKS, feed_back)
-    sums[2].pair_up(CHUNKS - 1)
+    sums[1].pair_up(CHUNKS - 1)
 
     ups_next = list(range(2, lines)) + [0]
     r.mix_grad[...] = jnp.zeros_like(r.mix_grad)
@@ -918,7 +988,7 @@
             at = pl.ds(pl.multiple_of(c * size + core * half + i, step), step)
             kept = pl.ds(pl.multiple_of(c * half + i, step), step)
             normed = r.norm_one[kept]
-            grad = r.wide_grad[kept] + sums[2].total(c, pl.ds(i, step))
+            grad = r.wide_grad[kept] + sums[1].total(c, pl.ds(i, step))
             back = norm_back(grad * gain_one, normed, r.inv_one[kept])
             r.wide_grad[kept] = back
             r.grad_one[at] = back.astype(LOW)
@@ -941,12 +1011,12 @@
         def _():
             scatter_up.start(1)
 
-        sums[2].arrived(c)
+        sums[1].arrived(c)
         pieces(piece)
         share(3, r.grad_one, c).start()
         share(3, r.grad_one, c).wait_recv()
         at = chunk_rows(c)
-        grad = matmul_low(r.grad_one[at], r.out_rows[...]).astype(LOW)
+        grad = against(r.grad_one[at], r.out_turned[0]).astype(LOW)
         r.grad_ext[pl.ds(pl.multiple_of(REACH + c * size, REACH), size)] = grad
         weights = r.weights_f[at]
         weighted = weights * against(grad, r.mixing_heads[...])
@@ -1022,13 +1092,19 @@
     r.land_out[:, :, 0:near] = qland_grad[0:LAND].reshape(count, each, near)
     r.land_out[:, :, near:] = kland_grad[0:LAND].reshape(count, each, near)
     land_sum.start()
+    for k in range(7):
+        r.vectors[k : k + 1] = jnp.sum(r.acc[k], axis=0, keepdims=True)
+    lanes = r.vector_out.shape[2]
+    for d in range(count):
+        r.vector_out[d] = r.vectors[:, d * lanes : (d + 1) * lanes] if d * lanes < width else jnp.zeros((8, lanes), WIDE)
+    vector_total.start()
     if ups_next[1:]:
         scatter_up.start(*ups_next[1:])
     scatter_up.forward(1)
 
     def values_back(c):
         at = chunk_rows(c)
-        values = across(r.weights_b_low[:, at], r.numer_heads[...]) + r.conv[at]
+        values = across(r.weights_b[:, at].astype(LOW), r.numer_heads[...]) + r.conv[at]
         r.near_grads[at, 2 * near : 3 * near] = values.astype(LOW)
         return jnp.sum(values, axis=0, keepdims=True)
 
@@ -1044,11 +1120,14 @@
         r.near_grads[at, 0:near] = r.grad_query[at].astype(LOW)
         r.near_grads[at, near : 2 * near] = r.grad_key[at].astype(LOW)
         terms = against(r.near_grads[at], r.w_near[:, :, 0 : 3 * near].reshape(width, 3 * near))
-        behind(c, sums[3])
-        sums[3].offer(c, terms.astype(LOW))
-
-    loop(CHUNKS // 2, input_terms)
+        sums[2].offer(c, terms.astype(LOW))
+
+    input_terms(0)
+    input_terms(1)
+    sums[2].pair_up(0)
     land_sum.add()
+    vector_total.add()
+    sums[2].pair_up(1)
     if lines > 2:
         scatter_up.forward(2)
 
@@ -1056,31 +1135,32 @@
         it = PINV_STEPS - 1 - i
         grads, kernel_grads = carry
         many = range(len(pairs))
-        wides = [exact(grads[p], r.uppers[it, p]) for p in many]
+        both = lambda ref: (ref[0], ref[1])
+        wides = [thrice(halves(grads[p]), both(r.uppers[it, p])) for p in many]
         product_grads = [
-            exact(r.lowers[it, p], jnp.concatenate([w[:, LAND:two], w[:, two:], grads[p]], axis=0))
+            thrice(
+                both(r.lowers[it, p]),
+                halves(jnp.concatenate([w[:, LAND:two], w[:, two:], grads[p]], axis=0)),
+            )
             for p, w in enumerate(wides)
         ]
+        parts = [halves(grad) for grad in product_grads]
         kernel_grads = [
-            old + exact(grad, r.lowers[it, p, :, 0:LAND])
-            for p, (old, grad) in enumerate(zip(kernel_grads, product_grads))
+            old + thrice(part, both(r.lowers[it, p, :, :, 0:LAND]))
+            for p, (old, part) in enumerate(zip(kernel_grads, parts))
         ]
-        grads = [wides[p][:, 0:LAND] + exact(r.turned_kernel[p], product_grads[p]) for p in many]
+        grads = [wides[p][:, 0:LAND] + thrice(both(r.turned_kernel[p]), parts[p]) for p in many]
         return tuple(grads), tuple(kernel_grads)
 
     zeros = tuple(jnp.zeros((LAND, LAND), WIDE) for _ in pairs)
     grads, kernel_grads = lax.fori_loop(0, PINV_STEPS, invert_back, (tuple(inverse_grads), zeros))
     scatter_out.forward()
-    loop(CHUNKS // 2, lambda c: input_terms(c + CHUNKS // 2))
-    sums[3].pair_up(CHUNKS - 1)
-    for k in range(7):
-        r.vectors[k : k + 1] = jnp.sum(r.acc[k], axis=0, keepdims=True)
-    lanes = r.vector_out.shape[2]
-    for d in range(count):
-        r.vector_out[d] = r.vectors[:, d * lanes : (d + 1) * lanes] if d * lanes < width else jnp.zeros((8, lanes), WIDE)
-    vector_total.start()
-    if lines > 3:
-        scatter_up.forward(*range(3, lines))
+    input_terms(2)
+    vector_total.finish()
+    for d in range(width // lanes):
+        r.vector_sum[0, :, d * lanes : (d + 1) * lanes] = r.vector_sums[d]
+    vector_core.start()
+
     qland_a = [jnp.zeros((LAND, near), WIDE)] * 2
     kland_a = [jnp.zeros((LAND, near), WIDE)] * 2
     for i, (k, g) in enumerate(pairs):
@@ -1094,6 +1174,9 @@
         kland_a[g] = kland_a[g] + exact(grad, r.query_land[group(g)].astype(WIDE), (0, 0)) * mask
 
 
+    sums[2].pair_up(2)
+    if lines > 3:
+        scatter_up.forward(*range(3, lines))
     land_sum.finish()
     land_total = r.land_sums[...].reshape(LAND, 2 * near)
     pick = (iota((LAND, LAND), 1) == iota((LAND, LAND), 0) + first_slot).astype(WIDE)
@@ -1113,6 +1196,8 @@
     r.slot_both[:, near:] = r.slot_k[0:two]
     slot_terms = against(r.slot_both[...], r.w_near[:, :, 0 : 2 * near].reshape(width, 2 * near))
     correction.offer(0, slot_terms.astype(LOW))
+    input_terms(3)
+    correction.pair_up(0)
 
     def add_slots(c):
         at = chunk_rows(c)
@@ -1126,10 +1211,9 @@
     query_bias = lax.fori_loop(
         0, CHUNKS, lambda c, total: total + add_slots(c), jnp.zeros((1, near), WIDE)
     )
-    correction.pair_up(0)
+    sums[2].pair_up(3)
     scatter_qk.fill(r.inputs[...], r.near_grads[:, 0 : 2 * near])
     scatter_qk.start()
-    vector_total.add()
     scatter_v.forward()
 
     r.tap_grad[...] = jnp.zeros_like(r.tap_grad)
@@ -1166,20 +1250,6 @@
     store_out.start()
     r.grad_near[2] = undense(scatter_v.finish())
     scatter_qk.forward()
-    vector_total.finish()
-    for d in range(width // lanes):
-        r.vector_sum[0, :, d * lanes : (d + 1) * lanes] = r.vector_sums[d]
-    vector_core.start()
-
-    def total_inputs(c):
-        def piece(i):
-            kept = pl.ds(pl.multiple_of(c * half + i, step), step)
-            r.wide_grad[kept] = r.wide_grad[kept] + sums[3].total(c, pl.ds(i, step))
-
-        sums[3].arrived(c)
-        pieces(piece)
-
-    loop(CHUNKS, total_inputs)
     here = pl.ds(pl.multiple_of(core * LAND, LAND), LAND)
     share_slots = remote(
         r.corr_all.at[here], r.corr_all.at[here], r.corr_s.at[0], r.corr_r.at[0], core_of_chip()
@@ -1189,10 +1259,21 @@
     share_slots.start()
     share_slots.wait_recv()
 
+    def store_inputs(c):
+        at = chunk_rows(c)
+        return pltpu.make_async_copy(r.cotangent.at[at], r.grad_inputs_hbm.at[at], r.chunk_sems.at[c])
+
     def inputs_done(c):
+        sums[2].arrived(c)
         slots = matmul_low(r.member[my_rows(c)], r.corr_all[...])
-        r.cotangent[my_rows(c)] = (r.wide_grad[pl.ds(pl.multiple_of(c * half, half), half)] + slots).astype(LOW)
+        kept = r.wide_grad[pl.ds(pl.multiple_of(c * half, half), half)]
+        r.cotangent[my_rows(c)] = (kept + sums[2].total(c, pl.ds(0, half)) + slots).astype(LOW)
         share(4, r.cotangent, c).start()
+
+        @pl.when(c > 0)
+        def _():
+            share(4, r.cotangent, c - 1).wait_recv()
+            store_inputs(c - 1).start()
 
     loop(CHUNKS, inputs_done)
     near_total = scatter_qk.finish()
@@ -1205,15 +1286,15 @@
     small_spread.finish()
     r.smalls[...] = functools.reduce(jnp.add, [r.small_part[d] for d in range(count)])
 
-    def settle_inputs(c):
-        share(4, r.cotangent, c).wait_recv()
-
-    loop(CHUNKS, settle_inputs)
-    store_grad_inputs.start()
+    share(4, r.cotangent, CHUNKS - 1).wait_recv()
+    store_inputs(CHUNKS - 1).start()
 
     def settle(c):
-        sums[3].core_copy(c).wait_send()
-        sums[3].x_copy(c).wait_send()
+        sums[2].core_copy(c).wait_send()
+        sums[2].x_copy(c).wait_send()
+        store_inputs(c).wait()
+        for copy in mixed_copies(c):
+            copy.wait_send()
         for k, ref in enumerate((r.hidden, r.grad_two, r.output, r.grad_one, r.cotangent)):
             share(k, ref, c).wait_send()
 
@@ -1224,7 +1305,7 @@
     share_slots.wait_send()
     for copy in stores:
         copy.wait()
-    for copy in rims[0] + rims[1]:
+    for copy in rims[0] + rims[1] + out_copies:
         copy.wait_send()
     for group_of in gathers + scatters + spreads:
         group_of.close()
@@ -1233,30 +1314,45 @@
 def hand_out(
     output, grad_inputs, grad_out, grad_up, grad_down, grad_near, vectors, smalls,
     to_output, to_inputs, to_query, to_key, to_value, to_out, to_up, to_down,
-    bias_query, bias_value, bias_out, bias_up, bias_down, gain_one, bias_one, gain_two, bias_two, taps, sems,
+    bias_query, bias_value, bias_out, bias_up, bias_down, gain_one, bias_one, gain_two, bias_two, taps,
+    hold, hold_near, hold_feed, hold_vectors, hold_smalls, sems, more, few_sems,
 ):
-    rows = output.shape[0] // 4
-    copies = []
-    for k, (ref, to) in enumerate(((output, to_output), (grad_inputs, to_inputs))):
-        for j in range(4):
+    parts = hold.shape[1]
+    rows = output.shape[0] // parts
+    copy = pltpu.make_async_copy
+    first, second = [], []
+    for j in range(parts):
+        for k, (ref, to) in enumerate(((output, to_output), (grad_inputs, to_inputs))):
             at = pl.ds(j * rows, rows)
-            copies.append(pltpu.make_async_copy(ref.at[at], to.at[at], sems.at[k, j]))
-    for k, (ref, to) in enumerate(
+            first.append(copy(ref.at[at], hold.at[k, j], sems.at[k, j, 0]))
+            second.append(copy(hold.at[k, j], to.at[at], sems.at[k, j, 1]))
+    for k, (ref, held, to) in enumerate(
         (
-            (grad_near.at[0], to_query), (grad_near.at[1], to_key), (grad_near.at[2], to_value),
-            (grad_out, to_out), (grad_up, to_up), (grad_down, to_down),
+            (grad_near.at[0], hold_near.at[0], to_query),
+            (grad_near.at[1], hold_near.at[1], to_key),
+            (grad_near.at[2], hold_near.at[2], to_value),
+            (grad_out, hold_near.at[3], to_out),
+            (grad_up, hold_feed.at[0], to_up),
+            (grad_down, hold_feed.at[1], to_down),
         )
     ):
-        copies.append(pltpu.make_async_copy(ref, to, sems.at[2 + k, 0]))
-    for copy in copies:
-        copy.start()
+        first.append(copy(ref, held, more.at[k, 0]))
+        second.append(copy(held, to, more.at[k, 1]))
+    few = [copy(vectors, hold_vectors, few_sems.at[0]), copy(smalls, hold_smalls, few_sems.at[1])]
+    for one in few + first:
+        one.start()
+    for one in few:
+        one.wait()
     for k, ref in enumerate((gain_two, bias_two, bias_down, gain_one, bias_one, bias_out, bias_up)):
-        ref[...] = vectors[k : k + 1].reshape(ref.shape)
+        ref[...] = hold_vectors[k : k + 1].reshape(ref.shape)
     for k, ref in enumerate((bias_query, bias_value)):
-        ref[...] = smalls[k : k + 1, 0 : ref.shape[0]].reshape(ref.shape)
-    taps[...] = smalls[2 : 2 + taps.shape[0], 0:KERNEL]
-    for copy in copies:
-        copy.wait()
+        ref[...] = hold_smalls[k : k + 1, 0 : ref.shape[0]].reshape(ref.shape)
+    taps[...] = hold_smalls[2 : 2 + taps.shape[0], 0:KERNEL]
+    for arriving, leaving in zip(first, second):
+        arriving.wait()
+        leaving.start()
+    for one in second:
+        one.wait()
 
 
 def fused_body(
@@ -1276,34 +1372,41 @@
     operands = dict(
         lengths=item_lengths, conv_taps=conv_taps,
         inputs_hbm=inputs, cotangent_hbm=cotangent,
-        w_query=w_query, w_key=w_key, w_value=w_value, w_out=w_out, w_up=w_up, w_down=w_down,
-        bias_query=bias_query, bias_value=bias_value,
-        bias_out=bias_out, bias_up=bias_up, bias_down=bias_down,
-        gain_one=gain_one, bias_one=bias_one, gain_two=gain_two, bias_two=bias_two,
+        w_up=w_up, w_down=w_down,
+        w_query_hbm=w_query, w_key_hbm=w_key, w_value_hbm=w_value, w_out_hbm=w_out,
+        bias_query_hbm=bias_query, bias_value_hbm=bias_value,
+        bias_out_hbm=bias_out, bias_up_hbm=bias_up, bias_down_hbm=bias_down,
+        gain_one_hbm=gain_one, bias_one_hbm=bias_one, gain_two_hbm=gain_two, bias_two_hbm=bias_two,
     )
     outs = dict(
         output_hbm=((rows, width), LOW), grad_inputs_hbm=((rows, width), LOW),
         grad_w_out_hbm=((part, near), WIDE), grad_w_up_hbm=((part, feed), WIDE), grad_w_down_hbm=((part, feed), WIDE),
         grad_near_hbm=((3, part, near), WIDE), vectors=((8, width), WIDE), smalls=((8, PAD), WIDE),
     )
+    line = lambda length: pltpu.VMEM((length,), WIDE)
     scratch = dict(
+        w_query=low(part, near), w_key=low(part, near), w_value=low(part, near), w_out=low(part, near),
+        bias_query=line(near), bias_value=line(near), bias_out=line(width), bias_up=line(feed), bias_down=line(width),
+        gain_one=line(width), bias_one=line(width), gain_two=line(width), bias_two=line(width),
+        shard_sems=sem(4), vector_sems=sem(9),
         inputs=low(rows, width), cotangent=low(rows, width), output=low(rows, width),
         grad_w_out=wide(part, near), grad_w_up=wide(part, feed), grad_w_down=wide(part, feed),
         grad_near=wide(3, part, near), io=sem(8),
-        packed=low(part, 4 * near), w_near=low(count, part, 4 * near), out_rows=low(width, near),
+        packed=low(part, 4 * near), w_near=low(count, part, 4 * near), out_turned=low(4, near, width),
+        mixed_out=low(CHUNKS, 2, 3 * half // 2, 128), mixed_in=low(3, CHUNKS, 3 * half // 2, 128),
         full_up=low(count, part, feed), full_down=low(count, part, feed),
         member=low(rows, two), band=low(heads * BLOCK, 2 * SPAN), band_back=low(heads * BLOCK, 2 * SPAN),
         queries=low(rows, near), keys=low(rows, near), value_ext=low(rows + 2 * REACH, PAD),
         land_part=low(count, 3 * BORDER, 128), query_land=low(two, near), key_land=low(two, near),
         query_heads=low(heads * two, near), key_heads=low(heads * two, near),
-        weights_b=wide(heads * two, rows), weights_b_low=low(heads * two, rows),
+        weights_b=wide(heads * two, rows),
         max_b=wide(heads * two, 1), total_b=wide(heads * two, 1),
         numer_out=wide(count, LAND // count, PAD), numer_in=wide(count, LAND // count, PAD),
         kernel_v=wide(count, LAND // count, PAD), kernel_edge=wide(LAND, PAD),
         land_kernel=wide(2 * heads, LAND, LAND), inverse=wide(2 * heads, LAND, LAND),
         befores=wide(PINV_STEPS, 2 * heads, LAND, LAND), products=wide(PINV_STEPS, 2 * heads, LAND, LAND),
-        uppers=wide(PINV_STEPS, 2 * heads, LAND, 3 * LAND), lowers=wide(PINV_STEPS, 2 * heads, LAND, 3 * LAND),
-        turned_kernel=wide(2 * heads, LAND, LAND),
+        uppers=low(PINV_STEPS, 2 * heads, 2, LAND, 3 * LAND), lowers=low(PINV_STEPS, 2 * heads, 2, LAND, 3 * LAND),
+        turned_kernel=low(2 * heads, 2, LAND, LAND),
         weights_f=wide(rows, heads * two), conv=wide(rows, near),
         mixing=low(two, near), mixing_heads=low(heads * two, near), mixed=low(rows, near),
         terms=low(CHUNKS, size, width), core_in=low(CHUNKS, half, width),
@@ -1339,15 +1442,15 @@
         corr_s=sem(1), corr_r=sem(1),
         g_own=sem(8), g_zs=sem(8, lines - 1), g_zr=sem(8, lines - 1), g_ys=sem(8, lines), g_yr=sem(8, lines),
         s_ys=sem(5, lines), s_yr=sem(5, lines), s_zs=sem(5, lines - 1), s_zr=sem(5, lines - 1),
-        e_s=sem(10, count - 1), e_r=sem(10, count - 1), h_sems=sem(4, 4, CHUNKS),
+        e_s=sem(10, count - 1), e_r=sem(10, count - 1), h_sems=sem(3, 4, CHUNKS), w_s=sem(3), w_r=sem(3), m_s=sem(3, CHUNKS), m_r=sem(3, CHUNKS),
         rim_s=sem(2, 2), rim_r=sem(2, 2), share_s=sem(5, CHUNKS), share_r=sem(5, CHUNKS),
-        core_s=sem(1), core_r=sem(1),
+        core_s=sem(1), core_r=sem(1), chunk_sems=sem(CHUNKS),
     )
     any_place = pl.BlockSpec(memory_space=pltpu.HBM)
     results = pl.pallas_call(
         functools.partial(layer_kernel, count, list(operands) + list(outs) + list(scratch)),
         out_shape=tuple(jax.ShapeDtypeStruct(*out) for out in outs.values()),
-        in_specs=[smem, smem, any_place, any_place] + [vmem] * (len(operands) - 4),
+        in_specs=[smem, smem] + [any_place] * (len(operands) - 2),
         out_specs=(any_place,) * 6 + (vmem, vmem),
         scratch_shapes=list(scratch.values()),
         compiler_params=pltpu.CompilerParams(
@@ -1365,9 +1468,12 @@
             vector(width), vector(width), vector(width), vector(width),
             jax.ShapeDtypeStruct((heads, KERNEL), WIDE),
         ),
-        in_specs=[vmem] * 8,
+        in_specs=[any_place] * 8,
         out_specs=(any_place,) * 8 + (vmem,) * 10,
-        scratch_shapes=[sem(8, 4)],
+        scratch_shapes=[
+            low(2, CHUNKS, size, width), wide(4, part, near), wide(2, part, feed), wide(8, width), wide(8, PAD),
+            sem(2, CHUNKS, 2), sem(6, 2), sem(2),
+        ],
     )(*results)
 
 
@@ -1678,7 +1784,7 @@
 
 def solution(mesh):
     seq, head = mesh.shape["seq"], mesh.shape["head"]
-    fits = head == 4 and seq >= 4 and LAND % (8 * seq) == 0
+    fits = head == 4 and seq == 8
     return jax.shard_map(
         fused_body if fits else plain_body,
         mesh=mesh,

time: 170 us -> 169 us (level)
  no operation moved by 1% of the time
where the time goes in v5:
time: 169 us; the launch traced here: 168 us
  Pallas kernels  168 us (99%)
    pallas_call x1, Pallas kernels, fused_body(): pl.pallas_call(functools.partial(layer_kernel, count, list(operands) + li...  163 us
    pallas_call x1, Pallas kernels, fused_body(): pl.pallas_call(hand_out, out_shape=(whole, whole, block(near), block(near...  4.64 us

profile of v5, /device:TPU:0, one launch (start us, length us, event | category | flops | bytes accessed | tf_op | source)
XLA Modules:
  0.0 168.4 jit_solution(4554515609837850508)
XLA Ops:
  0.7 162.9 %shard_map.322 = (bf16[1024,768]{1,0:T(8,128)(2,1)}, bf16[1024,768]{1,0:T(8,128)(2,1)}, f32[96,192]{1,0:T(8,128)}, f32[96,768]{1,0:T(8,128)}, f32[96,768]{1,0:T(...) custom-call(s32[3]{0:T(128)} %refs_0_.1, f32[3,33]{1,0:T(4,128)} %refs_1_.1, ...), custom_call_target="tpu_custom_call" | custom-call | tf_op jit(solution)/shard_map/pallas_call | solution.py:1450
  163.6 4.6 %shard_map.323 = (bf16[1024,768]{1,0:T(8,128)(2,1)}, bf16[1024,768]{1,0:T(8,128)(2,1)}, f32[96,192]{1,0:T(8,128)}, f32[96,192]{1,0:T(8,128)}, f32[96,192]{1,0:T(...) custom-call(bf16[1024,768]{1,0:T(8,128)(2,1)} %get-tuple-element.26., ...), custom_call_target="tpu_custom_call" | custom-call | tf_op jit(solution)/shard_map/pallas_call | solution.py:1463

commit v6 on v5

--- a/solution.py
+++ b/solution.py
@@ -440,7 +440,7 @@
     feed = r.w_up.shape[1]
     size = rows // CHUNKS
     half = size // 2
-    step = 32
+    step = 128
     lines = count // 2
     two = 2 * LAND
     scale = HEAD_DIM**-0.5
@@ -805,9 +805,9 @@
         r.inverse[i] = inverse
 
     def attend_f(c):
-        at = pl.ds(pl.multiple_of(c * half, half), half)
+        at = pl.ds(pl.multiple_of(c * size, size), size)
         scores = against(r.queries[at], r.key_heads[...]) * scale
-        token, lane = iota((half, two), 0) + c * half, iota((half, two), 1)
+        token, lane = iota((size, two), 0) + c * size, iota((size, two), 1)
         at_edge = (token >= edge_start) & (token < edge_end)
         member = jnp.where(lane < LAND, jnp.where(at_edge, 0.0, 1.0), jnp.where(at_edge, 1.0, 0.0))
         for k in range(heads):
@@ -815,7 +815,7 @@
             weights = jnp.exp(own - jnp.max(own, axis=1, keepdims=True))
             r.weights_f[at, k * two : (k + 1) * two] = weights / jnp.sum(weights, axis=1, keepdims=True)
 
-    loop(rows // half, attend_f)
+    loop(rows // size, attend_f)
     kernel_spread.finish()
     kernel_mid = r.kernel_v[...].reshape(LAND, PAD)
     kernel_of = lambda g: kernel_mid if g == 0 else r.kernel_edge[...]
@@ -1116,9 +1116,9 @@
 
     def input_terms(c):
         at = chunk_rows(c)
-        r.grad_key[at] = across(r.scores_b[:, at], r.query_heads[...]) * scale
+        r.weights_f[at, 0:near] = across(r.scores_b[:, at], r.query_heads[...]) * scale
         r.near_grads[at, 0:near] = r.grad_query[at].astype(LOW)
-        r.near_grads[at, near : 2 * near] = r.grad_key[at].astype(LOW)
+        r.near_grads[at, near : 2 * near] = r.weights_f[at, 0:near].astype(LOW)
         terms = against(r.near_grads[at], r.w_near[:, :, 0 : 3 * near].reshape(width, 3 * near))
         sums[2].offer(c, terms.astype(LOW))
 
@@ -1203,7 +1203,7 @@
         at = chunk_rows(c)
         member = jnp.concatenate([r.member[at]] * 2, axis=1)
         queries = r.grad_query[at] + matmul_low(member, r.slot_q[...])
-        keys = r.grad_key[at] + matmul_low(member, r.slot_k[...])
+        keys = r.weights_f[at, 0:near] + matmul_low(member, r.slot_k[...])
         r.near_grads[at, 0:near] = queries.astype(LOW)
         r.near_grads[at, near : 2 * near] = keys.astype(LOW)
         return jnp.sum(queries, axis=0, keepdims=True)
@@ -1415,7 +1415,7 @@
         grad_two=low(rows, width), grad_lift=low(rows, feed), grad_one=low(rows, width),
         norm_one=wide(rows // 2, width), inv_one=wide(rows // 2, 1), wide_grad=wide(rows // 2, width),
         tmp=wide(size, feed), acc=wide(7, 8, width),
-        grad_ext=low(rows + 2 * REACH, near), grad_query=wide(rows, near), grad_key=wide(rows, near),
+        grad_ext=low(rows + 2 * REACH, near), grad_query=wide(rows, near),
         mix_grad=wide(heads * two, near), kland_grad=wide(heads * two, near),
         mix_out=wide(count, LAND // count, near), mix_in=wide(count, LAND // count, near),
         mix_sums=wide(count, LAND // count, near), land_out=wide(count, LAND // count, 2 * near),
@@ -1438,7 +1438,7 @@
         t_qk=for_qk[0], yb_qk=for_qk[1], pr_qk=for_qk[2], zb_qk=for_qk[3],
         t_v=for_v[0], yb_v=for_v[1], pr_v=for_v[2], zb_v=for_v[3],
         corr_terms=low(1, two, width), corr_core=low(1, LAND, width), corr_out=low(1, LAND, width),
-        corr_in=low(2, 1, LAND, width), corr_sems=sem(1, 4, 1), corr_all=low(two, width),
+        corr_in=low(1, 1, LAND, width), corr_sems=sem(1, 4, 1), corr_all=low(two, width),
         corr_s=sem(1), corr_r=sem(1),
         g_own=sem(8), g_zs=sem(8, lines - 1), g_zr=sem(8, lines - 1), g_ys=sem(8, lines), g_yr=sem(8, lines),
         s_ys=sem(5, lines), s_yr=sem(5, lines), s_zs=sem(5, lines - 1), s_zr=sem(5, lines - 1),

time: 169 us -> 164 us (0.970)
  Pallas kernels: 168 us -> 162 us
    pallas_call x1, Pallas kernels: 163 us -> 157 us  [fused_body(): pl.pallas_call(functools.partial(layer_kernel, count, list(operands) + li...]
where the time goes in v6:
time: 164 us; the launch traced here: 163 us
  Pallas kernels  162 us (99%)
    pallas_call x1, Pallas kernels, fused_body(): pl.pallas_call(functools.partial(layer_kernel, count, list(operands) + li...  157 us
    pallas_call x1, Pallas kernels, fused_body(): pl.pallas_call(hand_out, out_shape=(whole, whole, block(near), block(near...  4.64 us

profile of v6, /device:TPU:0, one launch (start us, length us, event | category | flops | bytes accessed | tf_op | source)
XLA Modules:
  0.0 162.8 jit_solution(15151012551311109005)
XLA Ops:
  0.7 157.3 %shard_map.322 = (bf16[1024,768]{1,0:T(8,128)(2,1)}, bf16[1024,768]{1,0:T(8,128)(2,1)}, f32[96,192]{1,0:T(8,128)}, f32[96,768]{1,0:T(8,128)}, f32[96,768]{1,0:T(...) custom-call(s32[3]{0:T(128)} %refs_0_.1, f32[3,33]{1,0:T(4,128)} %refs_1_.1, ...), custom_call_target="tpu_custom_call" | custom-call | tf_op jit(solution)/shard_map/pallas_call | solution.py:1450
  158.0 4.6 %shard_map.323 = (bf16[1024,768]{1,0:T(8,128)(2,1)}, bf16[1024,768]{1,0:T(8,128)(2,1)}, f32[96,192]{1,0:T(8,128)}, f32[96,192]{1,0:T(8,128)}, f32[96,192]{1,0:T(...) custom-call(bf16[1024,768]{1,0:T(8,128)(2,1)} %get-tuple-element.26., ...), custom_call_target="tpu_custom_call" | custom-call | tf_op jit(solution)/shard_map/pallas_call | solution.py:1463
